TPU v7x, 32 devices: a whole 2x2x4 slice. The times are simulated.
32 devices in a mesh: ka: 2 (over core), fft: 16 (over z, y, x).
Axes of the slice: x: 2, y: 2, z: 4, core: 2. Of those that a mesh axis runs over, the one named last changes fastest.
Arguments:
- orbitals: float32 [2, 1, 2, 128, 128, 128], P('ka', None, None, 'fft'), may hold values from -3 to 3
- costate: float32 [2, 1, 2, 128, 128, 128], P('ka', None, None, 'fft'), may hold values from -6 to 6
- potential: float32 [128, 128, 128], P('fft'), may hold values from -4 to 4
- xc_kernel: float32 [128, 128, 128], P('fft'), may hold values from -1 to -0.1
- vector_potential: float32 [8], replicated, may hold values from -0.6 to 0.6
- kpoint_weight: int32 [2], replicated, may hold values from 1 to 8
- occupation: int32 [1], replicated, may hold values from 100 to 200
Outputs:
- adjoint_out: float32 [2, 1, 2, 128, 128, 128], P('ka', None, None, 'fft')
- cross_potential: float32 [128, 128, 128], P('fft')
Inputs may be any that keep to these rules, and one draw needn't show every extreme that they name: `kpoint_weight`: symmetry multiplicities of the k-points.
All inputs are finite; a program needn't handle non-finite values.
Results may differ from a plain program's by a relative error of at most 0.0003.
Values sent between devices are 32-bit elements; how exact they have to be, the bound alone decides.
No kernel may reach another device: no remote copies, remote signals or barrier semaphores. Data moves between devices by JAX's collectives and lax.ppermute only.
A program may use at most 192 MiB of HBM per device.

v0:
```python
import math

import jax
import jax.numpy as jnp
from jax import lax
from jax.sharding import PartitionSpec as P

STEPS = 2
SUB = 4


spacing = 0.25
step_time = 0.6
highest = lax.Precision.HIGHEST
form_x = "cx,kbxyz->kbcyz"
form_y = "cy,kbxyz->kbxcz"
form_z = "cz,kbxyz->kbxyc"


def wave_numbers(grid_line, grid_size):
    signed_line = jnp.where(grid_line < grid_size // 2, grid_line, grid_line - grid_size)
    return 2.0 * math.pi / (grid_size * spacing) * signed_line.astype(jnp.float32)


def dft_tables(grid_size):
    row_index = lax.broadcasted_iota(jnp.int32, (grid_size, grid_size), 0)
    col_index = lax.broadcasted_iota(jnp.int32, (grid_size, grid_size), 1)
    table_angle = (
        2.0 * math.pi / grid_size * (row_index * col_index % grid_size).astype(jnp.float32)
    )
    return (jnp.cos(table_angle), -jnp.sin(table_angle))


def contract(einsum_form, matrix, vector):
    return jnp.einsum(
        einsum_form, matrix, vector, precision=highest, preferred_element_type=jnp.float32
    )


def apply_line(real_part, imag_part, matrix_real, matrix_imag, einsum_form):
    new_real = contract(einsum_form, matrix_real, real_part) - contract(
        einsum_form, matrix_imag, imag_part
    )
    new_imag = contract(einsum_form, matrix_real, imag_part) + contract(
        einsum_form, matrix_imag, real_part
    )
    return (new_real, new_imag)


def rotate(real_part, imag_part, phase_angle, time_sign):
    cosine = jnp.cos(phase_angle)
    sine_part = time_sign * jnp.sin(phase_angle)
    return (real_part * cosine + imag_part * sine_part, imag_part * cosine - real_part * sine_part)


def to_columns(real_part, imag_part, local_work):
    return local_work(
        (
            lax.all_to_all(real_part, "fft", split_axis=3, concat_axis=2, tiled=True),
            lax.all_to_all(imag_part, "fft", split_axis=3, concat_axis=2, tiled=True),
        )
    )


def to_planes(real_part, imag_part, local_work):
    return local_work(
        (
            lax.all_to_all(real_part, "fft", split_axis=2, concat_axis=3, tiled=True),
            lax.all_to_all(imag_part, "fft", split_axis=2, concat_axis=3, tiled=True),
        )
    )


def local(orbitals, costate, potential, xc_kernel, vector_potential, kpoint_weight, occupation):
    planes = potential.shape[0]
    grid_size = potential.shape[1]
    fft_index = lax.axis_index("fft")
    k_index = lax.axis_index("ka")
    sub_time = step_time / SUB
    lattice_unit = 2.0 * math.pi / (grid_size * spacing)
    k_fraction = (k_index.astype(jnp.float32) + 0.5) / lax.axis_size("ka") - 0.5
    shift_x = lattice_unit * k_fraction
    shift_y = lattice_unit * 0.25
    shift_z = -lattice_unit * 0.25
    numbers = wave_numbers(lax.iota(jnp.int32, grid_size), grid_size)
    numbers_local = wave_numbers(fft_index * planes + lax.iota(jnp.int32, planes), grid_size)
    fwd_real, fwd_imag = dft_tables(grid_size)
    inv_real = fwd_real / grid_size
    inv_imag = -fwd_imag / grid_size
    half_planes = 0.5 * sub_time * potential
    plus_z = shift_z + numbers

    def kinetic_columns(push_value):
        plus_x = shift_x + numbers + push_value
        plus_local = shift_y + numbers_local
        return (
            0.5
            * sub_time
            * (
                (plus_x * plus_x)[:, None, None]
                + (plus_local * plus_local)[None, :, None]
                + (plus_z * plus_z)[None, None, :]
            )
        )

    def substep(real_part, imag_part, push_value, time_sign):
        real_part, imag_part = rotate(real_part, imag_part, half_planes, time_sign)
        real_part, imag_part = apply_line(real_part, imag_part, fwd_real, fwd_imag, form_y)
        real_part, imag_part = apply_line(real_part, imag_part, fwd_real, fwd_imag, form_z)

        def spectral(halves):
            col_real, col_imag = apply_line(halves[0], halves[1], fwd_real, fwd_imag, form_x)
            col_real, col_imag = rotate(col_real, col_imag, kinetic_columns(push_value), time_sign)
            return apply_line(col_real, col_imag, inv_real, inv_imag, form_x)

        def finish(halves):
            row_real, row_imag = apply_line(halves[0], halves[1], inv_real, inv_imag, form_y)
            row_real, row_imag = apply_line(row_real, row_imag, inv_real, inv_imag, form_z)
            return rotate(row_real, row_imag, half_planes, time_sign)

        real_part, imag_part = to_columns(real_part, imag_part, spectral)
        return to_planes(real_part, imag_part, finish)

    def propagate(real_part, imag_part, step_index, time_sign):
        if time_sign > 0:
            sub_order = list(range(SUB))
        else:
            sub_order = list(range(SUB - 1, -1, -1))
        for sub_count, sub_index in enumerate(sub_order):
            push_value = vector_potential[step_index * SUB + sub_index]
            real_part, imag_part = substep(real_part, imag_part, push_value, time_sign)
        return (real_part, imag_part)

    g_squared = (
        (numbers * numbers)[:, None, None]
        + (numbers_local * numbers_local)[None, :, None]
        + (numbers * numbers)[None, None, :]
    )
    coulomb = jnp.where(
        g_squared > 0, 4.0 * math.pi / jnp.where(g_squared > 0, g_squared, 1.0), 0.0
    )
    orbital_real = orbitals[:, :, 0]
    orbital_imag = orbitals[:, :, 1]
    history = [(orbital_real, orbital_imag)]
    for step_index in range(STEPS):
        orbital_real, orbital_imag = propagate(orbital_real, orbital_imag, step_index, 1.0)
        history.append((orbital_real, orbital_imag))
    occupied = occupation.astype(jnp.float32) / 100.0
    own_weight = lax.dynamic_slice_in_dim(kpoint_weight, k_index, 1)[0].astype(jnp.float32)
    weight = own_weight / jnp.sum(kpoint_weight).astype(jnp.float32)
    band_factor = 2.0 * weight * occupied
    adjoint_real = costate[:, :, 0]
    adjoint_imag = costate[:, :, 1]
    cross_pot = jnp.zeros_like(potential)
    for step_index in range(STEPS - 1, -1, -1):
        forward_real, forward_imag = history[step_index + 1]
        intersection = adjoint_real * forward_real + adjoint_imag * forward_imag
        partial_density = jnp.einsum(
            "b,kbxyz->xyz",
            band_factor,
            intersection,
            precision=highest,
            preferred_element_type=jnp.float32,
        )
        density = lax.psum(partial_density, "ka")
        hartree_col_real = contract("cy,xyz->xcz", fwd_real, density)
        hartree_col_imag = contract("cy,xyz->xcz", fwd_imag, density)
        hartree_col_real, hartree_col_imag = apply_line(
            hartree_col_real, hartree_col_imag, fwd_real, fwd_imag, "cz,xyz->xyc"
        )
        hartree_col_real, hartree_col_imag = (
            lax.all_to_all(hartree_col_real, "fft", split_axis=1, concat_axis=0, tiled=True),
            lax.all_to_all(hartree_col_imag, "fft", split_axis=1, concat_axis=0, tiled=True),
        )
        hartree_col_real, hartree_col_imag = apply_line(
            hartree_col_real, hartree_col_imag, fwd_real, fwd_imag, "cx,xyz->cyz"
        )
        hartree_col_real = hartree_col_real * coulomb
        hartree_col_imag = hartree_col_imag * coulomb
        hartree_col_real, hartree_col_imag = apply_line(
            hartree_col_real, hartree_col_imag, inv_real, inv_imag, "cx,xyz->cyz"
        )
        hartree_row_real = lax.all_to_all(
            hartree_col_real, "fft", split_axis=0, concat_axis=1, tiled=True
        )
        hartree_row_imag = lax.all_to_all(
            hartree_col_imag, "fft", split_axis=0, concat_axis=1, tiled=True
        )
        hartree_row_real, hartree_row_imag = apply_line(
            hartree_row_real, hartree_row_imag, inv_real, inv_imag, "cy,xyz->xcz"
        )
        cross_pot = (
            contract("cz,xyz->xyc", inv_real, hartree_row_real)
            - contract("cz,xyz->xyc", inv_imag, hartree_row_imag)
            + xc_kernel * density
        )
        adjoint_real = adjoint_real + step_time * cross_pot * forward_imag
        adjoint_imag = adjoint_imag - step_time * cross_pot * forward_real
        adjoint_real, adjoint_imag = propagate(adjoint_real, adjoint_imag, step_index, -1.0)
    return (jnp.stack([adjoint_real, adjoint_imag], axis=2), cross_pot)


def solution(mesh):
    placed = (
        P("ka", None, None, "fft", None, None),
        P("ka", None, None, "fft", None, None),
        P("fft", None, None),
        P("fft", None, None),
        P(),
        P(),
        P(),
    )
    return jax.shard_map(
        local,
        mesh=mesh,
        in_specs=placed,
        out_specs=(P("ka", None, None, "fft", None, None), P("fft", None, None)),
        check_vma=False,
    )
```

profile of v0, /device:TPU:1, one launch (start us, length us, event | category | flops | bytes accessed | tf_op | source)
XLA Modules:
  0.0 1981.3 jit_solution(10247985731113316442)
XLA Ops:
  35.3 8.9 all-to-all-done.1
  72.2 18.9 all-to-all-start.3
  110.2 10.4 all-to-all-done.2
  156.9 7.9 all-to-all-done.5
  171.9 10.8 all-to-all-done.4
  218.8 9.5 all-to-all-done.6
  264.7 7.6 all-to-all-done.9
  279.3 10.5 all-to-all-done.8
  325.6 9.6 all-to-all-done.10
  371.6 7.6 all-to-all-done.13
  386.2 10.5 all-to-all-done.12
  432.8 9.4 all-to-all-done.14
  488.0 7.7 all-to-all-done.17
  533.5 9.6 all-to-all-done.18
  597.2 7.8 all-to-all-done.20
  643.0 9.4 all-to-all-done.22
  706.5 7.8 all-to-all-done.24
  752.0 9.6 all-to-all-done.26
  815.8 7.8 all-to-all-done.28
  881.7 22.0 %all-reduce.3.cloned.1.call-done = f32[8,128,128]{2,1,0:T(8,128)} async-done(((f32[8,128,128]{2,1,0:T(8,128)}), f32[8,128,128]{2,1,0:T(8,128)}) %all-reduce.3.cloned.1.call-update) | async-done | bytes 524304 | tf_op jit(solution)/shard_map/psum | solution.py:165
  921.6 8.4 all-to-all-done.33
  938.4 8.9 all-to-all-done.32
  966.6 7.7 all-to-all-done.35
  982.9 9.1 all-to-all-done.34
  1037.9 7.7 all-to-all-done.37
  1083.9 9.4 all-to-all-done.38
  1147.6 7.8 all-to-all-done.40
  1193.1 9.6 all-to-all-done.42
  1257.0 7.8 all-to-all-done.44
  1302.8 9.4 all-to-all-done.46
  1366.5 7.8 all-to-all-done.48
  1412.2 9.6 all-to-all-done.50
  1432.5 22.1 %all-reduce.5.cloned.1.call-done = f32[8,128,128]{2,1,0:T(8,128)} async-done(((f32[8,128,128]{2,1,0:T(8,128)}), f32[8,128,128]{2,1,0:T(8,128)}) %all-reduce.5.cloned.1.call-update) | async-done | bytes 524304 | tf_op jit(solution)/shard_map/psum | solution.py:165
  1472.7 8.4 all-to-all-done.53
  1489.3 9.0 all-to-all-done.52
  1517.6 7.7 all-to-all-done.55
  1533.9 9.1 all-to-all-done.54
  1571.9 7.7 all-to-all-done.56
  1586.9 10.6 all-to-all-done.57
  1633.7 9.6 all-to-all-done.58
  1679.9 7.6 all-to-all-done.61
  1694.5 10.5 all-to-all-done.60
  1741.1 9.4 all-to-all-done.62
  1787.1 7.6 all-to-all-done.65
  1801.8 10.5 all-to-all-done.64
  1848.1 9.6 all-to-all-done.66
  1906.9 10.5 all-to-all-done.68
  1953.6 9.8 all-to-all-done.70
  (808 shorter events, 1493.9 us)
Async XLA Ops:
  24.5 19.7 all-to-all-start.1
  44.2 17.7 all-to-all-start
  72.2 30.4 %all-to-all-start.3 = ((f32[1,1,128,8,128]{4,3,1,0,2:T(8,128)}), f32[1,1,128,8,128]{4,3,1,0,2:T(8,128)S(1)}, u32[]{:S(2)}, u32[]{:S(2)}) async-start(f32[1,1,128,8,128]{4,3,1,0,2:T(8,128)} %copy.1190), calls=%async_computation.3 | async-start | bytes 1048576 | tf_op jit(solution)/shard_map/all_to_all | solution.py:69
  102.6 18.0 all-to-all-start.2
  147.1 17.8 all-to-all-start.5
  164.9 17.8 all-to-all-start.4
  192.9 17.7 all-to-all-start.7
  210.7 17.6 all-to-all-start.6
  254.7 17.6 all-to-all-start.9
  300.0 17.6 all-to-all-start.11
  317.6 17.6 all-to-all-start.10
  361.6 17.6 all-to-all-start.13
  379.2 17.6 all-to-all-start.12
  407.0 17.6 all-to-all-start.15
  424.6 17.6 all-to-all-start.14
  477.2 18.5 all-to-all-start.17
  586.9 18.1 all-to-all-start.20
  696.2 18.1 all-to-all-start.24
  744.1 17.6 all-to-all-start.26
  805.5 18.1 all-to-all-start.28
  853.4 17.6 all-to-all-start.30
  860.1 43.7 %all-reduce.3.cloned.1.call-start = ((), (), s32[]{:S(2)}) async-start(), calls=%async_computation.72 | async-start | bytes 1048576 | tf_op jit(solution)/shard_map/psum | solution.py:165
  910.6 19.4 all-to-all-start.33
  956.2 18.1 all-to-all-start.35
  974.3 17.7 all-to-all-start.34
  1010.1 17.6 all-to-all-start.36
  1027.7 17.9 all-to-all-start.37
  1058.0 17.6 all-to-all-start.39
  1075.6 17.6 all-to-all-start.38
  1137.2 18.1 all-to-all-start.40
  1246.7 18.1 all-to-all-start.44
  1294.7 17.6 all-to-all-start.46
  1356.2 18.1 all-to-all-start.48
  1410.8 43.7 %all-reduce.5.cloned.1.call-start = ((), (), s32[]{:S(2)}) async-start(), calls=%async_computation.73 | async-start | bytes 1048576 | tf_op jit(solution)/shard_map/psum | solution.py:165
  1461.6 19.4 all-to-all-start.53
  1507.2 18.1 all-to-all-start.55
  1525.3 17.7 all-to-all-start.54
  1561.9 17.7 all-to-all-start.56
  1579.6 17.8 all-to-all-start.57
  1607.7 18.0 all-to-all-start.59
  1669.9 17.6 all-to-all-start.61
  1687.5 17.6 all-to-all-start.60
  1732.9 17.6 all-to-all-start.62
  1794.7 17.6 all-to-all-start.64
  1840.1 17.6 all-to-all-start.66
  1899.9 17.6 all-to-all-start.68
  1927.8 17.7 all-to-all-start.71
  1945.5 17.8 all-to-all-start.70
  (76 other events, 1308.2 us)
Sparse Core Ops, SparseCore 0:
  881.8 21.8 all-reduce.2
  1432.6 21.9 all-reduce.4
where the time goes:
time: 2010 us; the launch traced here: 1980 us
  matrix products  738 us (37%)
  waiting for transfers between devices  578 us (29%)
  starting transfers between devices  496 us (25%)
  local copies, waits for them, and re-layouts  141 us (7%)
  between operations  21.4 us (1%)
    dot_general x424, matrix products, contract(): jnp.einsum(einsum_form, matrix, vector, precision=highest, preferred_elem...  738 us
    all_to_all x16, waiting for transfers between devices, to_planes(): lax.all_to_all(real_part, 'fft', split_axis=2, concat_axis=3, tiled=True)  149 us
    all_to_all x16, waiting for transfers between devices, to_columns(): lax.all_to_all(real_part, 'fft', split_axis=3, concat_axis=2, tiled=True)  137 us
    all_to_all x16, waiting for transfers between devices, to_columns(): lax.all_to_all(imag_part, 'fft', split_axis=3, concat_axis=2, tiled=True)  124 us
    all_to_all x16, starting transfers between devices, to_planes(): lax.all_to_all(imag_part, 'fft', split_axis=2, concat_axis=3, tiled=True)  119 us
    all_to_all x16, starting transfers between devices, to_planes(): lax.all_to_all(real_part, 'fft', split_axis=2, concat_axis=3, tiled=True)  110 us
    all_to_all x16, starting transfers between devices, to_columns(): lax.all_to_all(imag_part, 'fft', split_axis=3, concat_axis=2, tiled=True)  108 us
    all_to_all x16, starting transfers between devices, to_columns(): lax.all_to_all(real_part, 'fft', split_axis=3, concat_axis=2, tiled=True)  108 us
  transfers between devices with their start and end apart: 74, of which 74 were waited for; matrix products, arithmetic and copies ran while one was open for 13% of the time, Pallas kernels for 0%

commit v1 on v0

v1 whole, which is shorter than its diff:
```python
import math

import jax
import jax.numpy as jnp
from jax import lax
from jax.sharding import PartitionSpec as P

STEPS = 2
SUB = 4


spacing = 0.25
step_time = 0.6
sub_time = step_time / SUB
highest = lax.Precision.HIGHEST


def wave_numbers(grid_line, grid_size):
    signed_line = jnp.where(grid_line < grid_size // 2, grid_line, grid_line - grid_size)
    return 2.0 * math.pi / (grid_size * spacing) * signed_line.astype(jnp.float32)


def table_angles(grid_size):
    row_index = lax.broadcasted_iota(jnp.int32, (grid_size, grid_size), 0)
    col_index = lax.broadcasted_iota(jnp.int32, (grid_size, grid_size), 1)
    return 2.0 * math.pi / grid_size * (row_index * col_index % grid_size).astype(jnp.float32)


def line_matrices(shifts, grid_size):
    numbers = wave_numbers(lax.iota(jnp.int32, grid_size), grid_size)
    along = shifts[:, None] + numbers[None, :]
    phase = 0.5 * sub_time * (along * along)
    angles = table_angles(grid_size)
    cosine, sine = jnp.cos(angles), jnp.sin(angles)
    q_real, q_imag = jnp.cos(phase)[:, None, :], -jnp.sin(phase)[:, None, :]
    left_real = (cosine * q_real - sine * q_imag) / grid_size
    left_imag = (cosine * q_imag + sine * q_real) / grid_size
    both = jnp.stack([left_real, left_imag])
    by_cos = jnp.einsum("csam,mb->csab", both, cosine, precision=highest)
    by_sin = jnp.einsum("csam,mb->csab", both, sine, precision=highest)
    return by_cos[0] + by_sin[1], by_cos[1] - by_sin[0]


def real_form(real_part, imag_part):
    upper = jnp.stack([real_part, -imag_part], axis=-2)
    lower = jnp.stack([imag_part, real_part], axis=-2)
    return jnp.stack([upper, lower], axis=-4)


def spin(field, angle):
    cosine, sine = jnp.cos(angle), jnp.sin(angle)
    return jnp.stack(
        [field[0] * cosine + field[1] * sine, field[1] * cosine - field[0] * sine]
    )


def apply(form, matrix, field):
    return jnp.einsum(
        form, matrix, field, precision=lax.Precision.HIGHEST, preferred_element_type=jnp.float32
    )


def plain(orbitals, costate, potential, xc_kernel, vector_potential, kpoint_weight, occupation):
    grid_size = potential.shape[1]
    k_index = lax.axis_index("ka")
    fft_index = lax.axis_index("fft")
    planes = potential.shape[0]
    lattice_unit = 2.0 * math.pi / (grid_size * spacing)
    k_fraction = (k_index.astype(jnp.float32) + 0.5) / lax.axis_size("ka") - 0.5
    shifts = jnp.concatenate(
        [
            lattice_unit * k_fraction + vector_potential,
            jnp.array([lattice_unit * 0.25, -lattice_unit * 0.25], jnp.float32),
        ]
    )
    lines = real_form(*line_matrices(shifts, grid_size))
    back = jnp.transpose(lines, (0, 3, 4, 1, 2))

    def to_columns(field, split, concat):
        return lax.all_to_all(field, "fft", split_axis=split, concat_axis=concat, tiled=True)

    pot_rows = 0.5 * sub_time * potential
    pot_cols = to_columns(pot_rows, 1, 0)

    def propagate(field, step_index, sign):
        table = lines if sign > 0 else back
        order = range(SUB) if sign > 0 else range(SUB - 1, -1, -1)
        mat_y, mat_z = table[STEPS * SUB], table[STEPS * SUB + 1]
        in_rows = True
        field = spin(field, sign * pot_rows)
        for count, sub_index in enumerate(order):
            mat_x = table[step_index * SUB + sub_index]
            last = count == SUB - 1
            turn = sign * (1.0 if last else 2.0)
            field = apply("cadb,dkxyb->ckxya", mat_z, field)
            if in_rows:
                field = apply("cadb,dkxbz->ckxaz", mat_y, field)
                field = to_columns(field, 3, 2)
                field = apply("cadb,dkbyz->ckayz", mat_x, field)
                field = spin(field, turn * pot_cols)
            else:
                field = apply("cadb,dkbyz->ckayz", mat_x, field)
                field = to_columns(field, 2, 3)
                field = apply("cadb,dkxbz->ckxaz", mat_y, field)
                field = spin(field, turn * pot_rows)
            in_rows = not in_rows
        return field

    def parts_first(field):
        bands = field.shape[0] * field.shape[1]
        return jnp.moveaxis(field, 2, 0).reshape((2, bands) + field.shape[3:])

    angles = table_angles(grid_size)
    cas = (jnp.cos(angles) + jnp.sin(angles)) / math.sqrt(grid_size)
    numbers = wave_numbers(lax.iota(jnp.int32, grid_size), grid_size)
    numbers_local = wave_numbers(fft_index * planes + lax.iota(jnp.int32, planes), grid_size)
    g_squared = (
        (numbers * numbers)[:, None, None]
        + (numbers_local * numbers_local)[None, :, None]
        + (numbers * numbers)[None, None, :]
    )
    coulomb = jnp.where(
        g_squared > 0, 4.0 * math.pi / jnp.where(g_squared > 0, g_squared, 1.0), 0.0
    )
    orbital = parts_first(orbitals)
    history = [orbital]
    for step_index in range(STEPS):
        orbital = propagate(orbital, step_index, 1.0)
        history.append(orbital)
    occupied = occupation.astype(jnp.float32) / 100.0
    own_weight = lax.dynamic_slice_in_dim(kpoint_weight, k_index, 1)[0].astype(jnp.float32)
    weight = own_weight / jnp.sum(kpoint_weight).astype(jnp.float32)
    band_factor = 2.0 * weight * occupied
    adjoint = parts_first(costate)
    cross_pot = jnp.zeros_like(potential)
    for step_index in range(STEPS - 1, -1, -1):
        forward = history[step_index + 1]
        density = lax.psum(
            jnp.sum(band_factor[:, None, None, None] * jnp.sum(adjoint * forward, axis=0), axis=0),
            "ka",
        )
        hartree = apply("ab,xyb->xya", cas, density)
        hartree = apply("ab,xbz->xaz", cas, hartree)
        hartree = to_columns(hartree, 1, 0)
        hartree = apply("ab,byz->ayz", cas, hartree)
        hartree = apply("ab,byz->ayz", cas, hartree * coulomb)
        hartree = to_columns(hartree, 0, 1)
        hartree = apply("ab,xbz->xaz", cas, hartree)
        hartree = apply("ab,xyb->xya", cas, hartree)
        cross_pot = hartree + xc_kernel * density
        turned = jnp.stack([forward[1], -forward[0]])
        adjoint = propagate(adjoint + step_time * cross_pot * turned, step_index, -1.0)
    result = jnp.moveaxis(adjoint.reshape((2,) + orbitals.shape[:2] + adjoint.shape[2:]), 0, 2)
    return (result, cross_pot)


def solution(mesh):
    placed = (
        P("ka", None, None, "fft", None, None),
        P("ka", None, None, "fft", None, None),
        P("fft", None, None),
        P("fft", None, None),
        P(),
        P(),
        P(),
    )
    return jax.shard_map(
        plain,
        mesh=mesh,
        in_specs=placed,
        out_specs=(P("ka", None, None, "fft", None, None), P("fft", None, None)),
        check_vma=False,
    )
```

time: 2010 us -> 833 us (0.41)
  matrix products: 738 us -> 116 us
  starting transfers between devices: 496 us -> 45.1 us
  waiting for transfers between devices: 578 us -> 129 us
  blocking collectives: 0 us -> 390 us
  local copies, waits for them, and re-layouts: 141 us -> 81 us
  other arithmetic: 7 us -> 40.1 us
    dot_general x424 -> x62, matrix products: 738 us -> 116 us  [the longest x60 114 us: apply(): jnp.einsum(form, matrix, field, precision=lax.Precision.HIGHEST, preferre...]
    all_to_all x72 -> x7, starting transfers between devices: 496 us -> 44.9 us  [to_columns(): lax.all_to_all(field, 'fft', split_axis=split, concat_axis=concat, tiled=...]
    all_to_all x72 -> x7, waiting for transfers between devices: 534 us -> 86.3 us  [to_columns(): lax.all_to_all(field, 'fft', split_axis=split, concat_axis=concat, tiled=...]
    all_to_all x0 -> x14, blocking collectives: none -> 390 us  [to_columns(): lax.all_to_all(field, 'fft', split_axis=split, concat_axis=concat, tiled=...]
    sub x36 -> x0, local copies, waits for them, and re-layouts: 46.5 us -> none  [apply_line(): contract(einsum_form, matrix_real, real_part)]
    transpose x0 -> x18, local copies, waits for them, and re-layouts: none -> 40.3 us  [apply(): jnp.einsum(form, matrix, field, precision=lax.Precision.HIGHEST, preferre...]
    add x36 -> x0, local copies, waits for them, and re-layouts: 38.2 us -> none  [apply_line(): contract(einsum_form, matrix_real, imag_part)]
    another operation x1 -> x15, other arithmetic: 1.07 us -> 29.3 us  [the longest x12 27.9 us: spin(): jnp.stack([field[0] * cosine + field[1] * sine, field[1] * cosine - field...]
  transfers between devices with their start and end apart: 74 -> 9, of which waited for: 74 -> 9; matrix products, arithmetic and copies ran while one was open for 13% -> 4% of each run, Pallas kernels for 0% -> 0%
where the time goes in v1:
time: 833 us; the launch traced here: 820 us
  blocking collectives  390 us (47%)
  waiting for transfers between devices  129 us (15%)
  matrix products  116 us (14%)
  local copies, waits for them, and re-layouts  81 us (10%)
  starting transfers between devices  45.1 us (5%)
  other arithmetic  40.1 us (5%)
  between operations  17.9 us (2%)
    all_to_all x14, blocking collectives, to_columns(): lax.all_to_all(field, 'fft', split_axis=split, concat_axis=concat, tiled=...  390 us
    dot_general x60, matrix products, apply(): jnp.einsum(form, matrix, field, precision=lax.Precision.HIGHEST, preferre...  114 us
    all_to_all x7, waiting for transfers between devices, to_columns(): lax.all_to_all(field, 'fft', split_axis=split, concat_axis=concat, tiled=...  86.3 us
    all_to_all x7, starting transfers between devices, to_columns(): lax.all_to_all(field, 'fft', split_axis=split, concat_axis=concat, tiled=...  44.9 us
    psum x2, waiting for transfers between devices, plain(): lax.psum(jnp.sum(band_factor[:, None, None, None] * jnp.sum(adjoint * for...  42.7 us
    transpose x18, local copies, waits for them, and re-layouts, apply(): jnp.einsum(form, matrix, field, precision=lax.Precision.HIGHEST, preferre...  40.3 us
    another operation x12, other arithmetic, spin(): jnp.stack([field[0] * cosine + field[1] * sine, field[1] * cosine - field...  27.9 us
  transfers between devices with their start and end apart: 9, of which 9 were waited for; matrix products, arithmetic and copies ran while one was open for 4% of the time, Pallas kernels for 0%

profile of v1, /device:TPU:1, one launch (start us, length us, event | category | flops | bytes accessed | tf_op | source)
XLA Modules:
  0.0 819.8 jit_solution(13787783062163788892)
XLA Ops:
  7.2 3.9 fusion.70
  12.2 7.5 all-to-all-start.1
  26.1 2.8 convolution_bitcast_fusion.46
  32.0 6.2 all-to-all-start
  38.2 5.5 cosine_bitcast_fusion.1
  50.6 9.9 %all-to-all-done = f32[2,1,8,128,128]{4,0,2,1,3:T(2,128)} async-done(((f32[2,1,8,128,128]{4,0,2,1,3:T(2,128)}), f32[2,1,8,128,128]{4,0,2,1,3:T(2,128)}, u32[]{:S(2)}, u32[]{:S(2)}) %all-to-all-start) | async-done | bytes 1048608 | tf_op jit(solution)/shard_map/all_to_all | solution.py:80
  66.0 2.8 convolution_bitcast_fusion.43
  71.1 6.8 all-to-all-start.2
  78.9 21.2 %all-to-all-done.2 = f32[2,1,128,8,128]{4,0,3,1,2:T(2,128)} async-done(((f32[2,1,128,8,128]{4,0,3,1,2:T(2,128)}), f32[2,1,128,8,128]{4,0,3,1,2:T(2,128)}, u32[]{:S(2)}, u32[]{:S(2)}) %all-to-all-start.2) | async-done | bytes 1048608 | tf_op jit(solution)/shard_map/all_to_all | solution.py:80
  107.1 2.8 convolution_bitcast_fusion.40
  112.2 30.9 %all_to_all.321 = f32[2,1,8,128,128]{4,0,2,1,3:T(2,128)S(1)} all-to-all(f32[2,1,8,128,128]{4,0,2,1,3:T(2,128)} %copy.455), channel_id=1, replica_groups=mesh['ka'=2,'fft'=16] {'fft'}, dimensions={3} | all-to-all | bytes 2097152 | tf_op jit(solution)/shard_map/all_to_all | solution.py:80
  153.3 28.8 %all_to_all.322 = f32[2,1,128,8,128]{4,0,3,1,2:T(2,128)S(1)} all-to-all(f32[2,1,128,8,128]{4,0,3,1,2:T(2,128)} %copy.465), channel_id=1, replica_groups=mesh['ka'=2,'fft'=16] {'fft'}, dimensions={2} | all-to-all | bytes 2097152 | tf_op jit(solution)/shard_map/all_to_all | solution.py:80
  185.3 2.9 subtract_bitcast_fusion.8
  189.2 2.8 convolution_bitcast_fusion.35
  194.3 29.0 %all_to_all.323 = f32[2,1,8,128,128]{4,0,2,1,3:T(2,128)S(1)} all-to-all(f32[2,1,8,128,128]{4,0,2,1,3:T(2,128)} %copy.472), channel_id=1, replica_groups=mesh['ka'=2,'fft'=16] {'fft'}, dimensions={3} | all-to-all | bytes 2097152 | tf_op jit(solution)/shard_map/all_to_all | solution.py:80
  228.3 2.8 convolution_bitcast_fusion.32
  233.4 28.7 %all_to_all.324 = f32[2,1,128,8,128]{4,0,3,1,2:T(2,128)S(1)} all-to-all(f32[2,1,128,8,128]{4,0,3,1,2:T(2,128)} %copy.482), channel_id=1, replica_groups=mesh['ka'=2,'fft'=16] {'fft'}, dimensions={2} | all-to-all | bytes 2097152 | tf_op jit(solution)/shard_map/all_to_all | solution.py:80
  268.0 2.8 convolution_bitcast_fusion.30
  273.0 29.0 %all_to_all.325 = f32[2,1,8,128,128]{4,0,2,1,3:T(2,128)S(1)} all-to-all(f32[2,1,8,128,128]{4,0,2,1,3:T(2,128)} %copy.489), channel_id=1, replica_groups=mesh['ka'=2,'fft'=16] {'fft'}, dimensions={3} | all-to-all | bytes 2097152 | tf_op jit(solution)/shard_map/all_to_all | solution.py:80
  307.1 2.8 convolution_bitcast_fusion.27
  312.2 5.1 all-to-all-start.8
  320.7 18.8 %all-to-all-done.8 = f32[2,1,128,8,128]{4,0,3,1,2:T(2,128)} async-done(((f32[2,1,128,8,128]{4,0,3,1,2:T(2,128)}), f32[2,1,128,8,128]{4,0,3,1,2:T(2,128)}, u32[]{:S(2)}, u32[]{:S(2)}) %all-to-all-start.8) | async-done | bytes 1048608 | tf_op jit(solution)/shard_map/all_to_all | solution.py:80
  341.9 2.8 fusion.251
  346.4 22.3 %all-reduce.3.cloned.1.call-done = f32[8,128,128]{2,1,0:T(8,128)} async-done(((f32[8,128,128]{2,1,0:T(8,128)}), f32[8,128,128]{2,1,0:T(8,128)}) %all-reduce.3.cloned.1.call-update) | async-done | bytes 524304 | tf_op jit(solution)/shard_map/psum | solution.py:138
  374.3 7.1 all-to-all-start.9
  381.5 12.7 %all-to-all-done.9 = f32[8,128,128]{2,0,1:T(8,128)} async-done(((f32[8,128,128]{2,0,1:T(8,128)}), f32[8,128,128]{2,0,1:T(8,128)}, u32[]{:S(2)}, u32[]{:S(2)}) %all-to-all-start.9) | async-done | bytes 524320 | tf_op jit(solution)/shard_map/all_to_all | solution.py:80
  398.2 5.6 all-to-all-start.10
  406.6 8.9 %all-to-all-done.10 = f32[128,8,128]{2,1,0:T(8,128)} async-done(((f32[128,8,128]{2,1,0:T(8,128)}), f32[128,8,128]{2,1,0:T(8,128)}, u32[]{:S(2)}, u32[]{:S(2)}) %all-to-all-start.10) | async-done | bytes 524320 | tf_op jit(solution)/shard_map/all_to_all | solution.py:80
  422.5 2.8 convolution_bitcast_fusion.14
  427.5 6.6 all-to-all-start.11
  442.2 14.1 %all-to-all-done.11 = f32[2,1,8,128,128]{4,0,2,1,3:T(2,128)} async-done(((f32[2,1,8,128,128]{4,0,2,1,3:T(2,128)}), f32[2,1,8,128,128]{4,0,2,1,3:T(2,128)}, u32[]{:S(2)}, u32[]{:S(2)}) %all-to-all-start.11) | async-done | bytes 1048608 | tf_op jit(solution)/shard_map/all_to_all | solution.py:80
  462.7 2.8 convolution_bitcast_fusion.12
  467.8 30.4 %all_to_all.326 = f32[2,1,128,8,128]{4,0,3,1,2:T(2,128)S(1)} all-to-all(f32[2,1,128,8,128]{4,0,3,1,2:T(2,128)} %copy.533), channel_id=1, replica_groups=mesh['ka'=2,'fft'=16] {'fft'}, dimensions={2} | all-to-all | bytes 2097152 | tf_op jit(solution)/shard_map/all_to_all | solution.py:80
  504.0 2.8 convolution_bitcast_fusion.11
  509.1 29.0 %all_to_all.327 = f32[2,1,8,128,128]{4,0,2,1,3:T(2,128)S(1)} all-to-all(f32[2,1,8,128,128]{4,0,2,1,3:T(2,128)} %copy.544), channel_id=1, replica_groups=mesh['ka'=2,'fft'=16] {'fft'}, dimensions={3} | all-to-all | bytes 2097152 | tf_op jit(solution)/shard_map/all_to_all | solution.py:80
  543.2 2.8 convolution_bitcast_fusion.9
  548.3 28.7 %all_to_all.328 = f32[2,1,128,8,128]{4,0,3,1,2:T(2,128)S(1)} all-to-all(f32[2,1,128,8,128]{4,0,3,1,2:T(2,128)} %copy.557), channel_id=1, replica_groups=mesh['ka'=2,'fft'=16] {'fft'}, dimensions={2} | all-to-all | bytes 2097152 | tf_op jit(solution)/shard_map/all_to_all | solution.py:80
  582.1 20.4 %all-reduce.5.cloned.1.call-done = f32[8,128,128]{2,1,0:T(8,128)} async-done(((f32[8,128,128]{2,1,0:T(8,128)}), f32[8,128,128]{2,1,0:T(8,128)}) %all-reduce.5.cloned.1.call-update) | async-done | bytes 524304 | tf_op jit(solution)/shard_map/psum | solution.py:138
  608.2 19.7 %all_to_all.329 = f32[8,128,128]{2,0,1:T(8,128)S(1)} all-to-all(f32[8,128,128]{2,0,1:T(8,128)} %copy.564), channel_id=1, replica_groups=mesh['ka'=2,'fft'=16] {'fft'}, dimensions={1} | all-to-all | bytes 1048576 | tf_op jit(solution)/shard_map/all_to_all | solution.py:80
  630.2 17.2 %all_to_all.330 = f32[128,8,128]{2,1,0:T(8,128)S(1)} all-to-all(f32[128,8,128]{2,1,0:T(8,128)S(1)} %copy.568), channel_id=1, replica_groups=mesh['ka'=2,'fft'=16] {'fft'}, dimensions={0} | all-to-all | bytes 1048576 | tf_op jit(solution)/shard_map/all_to_all | solution.py:80
  653.8 2.8 convolution_bitcast_fusion.7
  658.8 31.0 %all_to_all.331 = f32[2,1,8,128,128]{4,0,2,1,3:T(2,128)S(1)} all-to-all(f32[2,1,8,128,128]{4,0,2,1,3:T(2,128)} %copy.576), channel_id=1, replica_groups=mesh['ka'=2,'fft'=16] {'fft'}, dimensions={3} | all-to-all | bytes 2097152 | tf_op jit(solution)/shard_map/all_to_all | solution.py:80
  695.0 2.8 convolution_bitcast_fusion.5
  700.1 29.4 %all_to_all.332 = f32[2,1,128,8,128]{4,0,3,1,2:T(2,128)S(1)} all-to-all(f32[2,1,128,8,128]{4,0,3,1,2:T(2,128)} %copy.589), channel_id=1, replica_groups=mesh['ka'=2,'fft'=16] {'fft'}, dimensions={2} | all-to-all | bytes 2097152 | tf_op jit(solution)/shard_map/all_to_all | solution.py:80
  735.3 2.8 convolution_bitcast_fusion.3
  740.4 29.4 %all_to_all.333 = f32[2,1,8,128,128]{4,0,2,1,3:T(2,128)S(1)} all-to-all(f32[2,1,8,128,128]{4,0,2,1,3:T(2,128)} %copy.599), channel_id=1, replica_groups=mesh['ka'=2,'fft'=16] {'fft'}, dimensions={3} | all-to-all | bytes 2097152 | tf_op jit(solution)/shard_map/all_to_all | solution.py:80
  774.9 2.8 convolution_bitcast_fusion.1
  779.5 28.9 %all_to_all.334 = f32[2,1,128,8,128]{4,0,3,1,2:T(2,128)S(1)} all-to-all(f32[2,1,128,8,128]{4,0,3,1,2:T(2,128)S(1)} %copy.612), channel_id=1, replica_groups=mesh['ka'=2,'fft'=16] {'fft'}, dimensions={2} | all-to-all | bytes 2097152 | tf_op jit(solution)/shard_map/all_to_all | solution.py:80
  (271 shorter events, 181.7 us)
Async XLA Ops:
  11.0 8.9 %copy-start.58 = (f32[8]{0:T(128)S(1)}, f32[8]{0:T(128)}, u32[]{:S(2)}) copy-start(f32[8]{0:T(128)} %param.12) | copy-start | bytes 100
  11.0 8.9 %copy-start.60 = (f32[2]{0:T(128)S(1)}, f32[2]{0:T(128)}, u32[]{:S(2)}) copy-start(f32[2]{0:T(128)} %constant.91.clone) | copy-start | bytes 28
  12.2 19.8 %all-to-all-start.1 = ((f32[8,128,128]{2,0,1:T(8,128)}), f32[8,128,128]{2,0,1:T(8,128)}, u32[]{:S(2)}, u32[]{:S(2)}) async-start(f32[8,128,128]{2,0,1:T(8,128)} %copy.437), calls=%async_computation.1 | async-start | bytes 1048576 | tf_op jit(solution)/shard_map/all_to_all | solution.py:80
  23.8 40.3 %copy-start.1 = (f32[2,128,2,128,1]{3,1,2,0,4:T(8,128)}, f32[2,128,2,128,1]{3,1,2,0,4:T(8,128)S(1)}, u32[]{:S(2)}) copy-start(f32[2,128,2,128,1]{3,1,2,0,4:T(8,128)S(1)} %get-tuple-element.13) | copy-start | bytes 786436
  32.0 28.5 %all-to-all-start = ((f32[2,1,8,128,128]{4,0,2,1,3:T(2,128)}), f32[2,1,8,128,128]{4,0,2,1,3:T(2,128)}, u32[]{:S(2)}, u32[]{:S(2)}) async-start(f32[2,1,8,128,128]{4,0,2,1,3:T(2,128)} %copy.433), calls=%async_computation | async-start | bytes 2097152 | tf_op jit(solution)/shard_map/all_to_all | solution.py:80
  62.1 1.8 copy-start.22
  62.2 1.8 copy-start.26
  71.1 6.8 copy-start
  71.1 29.0 %all-to-all-start.2 = ((f32[2,1,128,8,128]{4,0,3,1,2:T(2,128)}), f32[2,1,128,8,128]{4,0,3,1,2:T(2,128)}, u32[]{:S(2)}, u32[]{:S(2)}) async-start(f32[2,1,128,8,128]{4,0,3,1,2:T(2,128)} %copy.447), calls=%async_computation.2 | async-start | bytes 2097152 | tf_op jit(solution)/shard_map/all_to_all | solution.py:80
  103.2 2.1 copy-start.2
  143.6 1.8 copy-start.23
  143.6 1.8 copy-start.27
  185.3 2.9 copy-start.36
  185.3 2.9 copy-start.4
  223.7 1.8 copy-start.24
  223.7 1.8 copy-start.28
  264.1 2.1 copy-start.6
  312.2 5.2 copy-start.59
  312.2 27.3 %all-to-all-start.8 = ((f32[2,1,128,8,128]{4,0,3,1,2:T(2,128)}), f32[2,1,128,8,128]{4,0,3,1,2:T(2,128)}, u32[]{:S(2)}, u32[]{:S(2)}) async-start(f32[2,1,128,8,128]{4,0,3,1,2:T(2,128)} %copy.499), calls=%async_computation.8 | async-start | bytes 2097152 | tf_op jit(solution)/shard_map/all_to_all | solution.py:80
  317.3 51.4 %all-reduce.3.cloned.1.call-start = ((), (), s32[]{:S(2)}) async-start(), calls=%async_computation.21 | async-start | bytes 1048576 | tf_op jit(solution)/shard_map/psum | solution.py:138
  341.9 2.9 copy-start.44
  374.3 19.8 %all-to-all-start.9 = ((f32[8,128,128]{2,0,1:T(8,128)}), f32[8,128,128]{2,0,1:T(8,128)}, u32[]{:S(2)}, u32[]{:S(2)}) async-start(f32[8,128,128]{2,0,1:T(8,128)} %copy.505), calls=%async_computation.9 | async-start | bytes 1048576 | tf_op jit(solution)/shard_map/all_to_all | solution.py:80
  398.2 17.2 %all-to-all-start.10 = ((f32[128,8,128]{2,1,0:T(8,128)}), f32[128,8,128]{2,1,0:T(8,128)}, u32[]{:S(2)}, u32[]{:S(2)}) async-start(f32[128,8,128]{2,1,0:T(8,128)} %copy.509), calls=%async_computation.10 | async-start | bytes 1048576 | tf_op jit(solution)/shard_map/all_to_all | solution.py:80
  406.6 11.0 %copy-start.48 = (f32[8,128,128]{2,1,0:T(8,128)S(1)}, f32[8,128,128]{2,1,0:T(8,128)}, u32[]{:S(2)}) copy-start(f32[8,128,128]{2,1,0:T(8,128)} %param.11) | copy-start | bytes 1572868
  406.6 11.1 %copy-start.51 = (f32[8,128,128]{2,1,0:T(8,128)S(1)}, f32[8,128,128]{2,1,0:T(8,128)}, u32[]{:S(2)}) copy-start(f32[8,128,128]{2,1,0:T(8,128)} %all-reduce.3.cloned.1.call-done) | copy-start | bytes 1572868
  419.2 2.2 copy-start.30
  419.4 3.1 copy-start.9
  427.5 28.8 %all-to-all-start.11 = ((f32[2,1,8,128,128]{4,0,2,1,3:T(2,128)}), f32[2,1,8,128,128]{4,0,2,1,3:T(2,128)}, u32[]{:S(2)}, u32[]{:S(2)}) async-start(f32[2,1,8,128,128]{4,0,2,1,3:T(2,128)} %copy.517), calls=%async_computation.11 | async-start | bytes 2097152 | tf_op jit(solution)/shard_map/all_to_all | solution.py:80
  434.1 168.4 %all-reduce.5.cloned.1.call-start = ((), (), s32[]{:S(2)}) async-start(), calls=%async_computation.22 | async-start | bytes 1048576 | tf_op jit(solution)/shard_map/psum | solution.py:138
  458.1 2.6 copy-start.14
  458.1 2.6 copy-start.18
  500.1 2.1 copy-start.31
  538.6 2.6 copy-start.15
  538.6 2.6 copy-start.19
  578.2 2.1 copy-start.34
  578.3 2.1 copy-start.37
  630.1 18.4 %copy-start.47 = (f32[8,128,128]{2,1,0:T(8,128)S(1)}, f32[8,128,128]{2,1,0:T(8,128)}, u32[]{:S(2)}) copy-start(f32[8,128,128]{2,1,0:T(8,128)} %all-reduce.5.cloned.1.call-done) | copy-start | bytes 1572868
  630.1 18.4 %copy-start.49 = (f32[8,128,128]{2,1,0:T(8,128)S(1)}, f32[8,128,128]{2,1,0:T(8,128)}, u32[]{:S(2)}) copy-start(f32[8,128,128]{2,1,0:T(8,128)} %param.11) | copy-start | bytes 1572868
  648.5 2.0 copy-start.35
  648.5 2.0 copy-start.39
  648.6 2.0 copy-start.41
  648.6 2.0 copy-start.46
  650.7 2.1 copy-start.32
  690.4 2.6 copy-start.16
  690.4 2.6 copy-start.20
  731.4 2.1 copy-start.33
  770.3 2.6 copy-start.17
  770.3 2.6 copy-start.21
  (22 other events, 28.2 us)
Sparse Core Ops, SparseCore 0:
  346.5 22.0 all-reduce.2
  582.3 20.2 all-reduce.4

commit v2 on v1

--- a/solution.py
+++ b/solution.py
@@ -1,8 +1,11 @@
+import functools
 import math
 
 import jax
 import jax.numpy as jnp
 from jax import lax
+from jax.experimental import pallas as pl
+from jax.experimental.pallas import tpu as pltpu
 from jax.sharding import PartitionSpec as P
 
 STEPS = 2
@@ -154,6 +157,432 @@
     return (result, cross_pot)
 
 
+ROWS = 128
+PLANES = 8
+AXES = ("ka", "fft")
+
+
+def halves_of(value):
+    high = value.astype(jnp.bfloat16)
+    return high, (value - high.astype(jnp.float32)).astype(jnp.bfloat16)
+
+
+def from_left(table, field):
+    high, low = halves_of(field)
+    return jnp.dot(
+        table, jnp.concatenate([high, low, high], axis=0), preferred_element_type=jnp.float32
+    )
+
+
+def from_right(field, table):
+    high, low = halves_of(field)
+    return jnp.dot(
+        jnp.concatenate([high, low, high], axis=1), table, preferred_element_type=jnp.float32
+    )
+
+
+def side_table(matrix, axis):
+    high = lax.reduce_precision(matrix, 8, 7)
+    low = (matrix - high).astype(jnp.bfloat16)
+    high = high.astype(jnp.bfloat16)
+    return jnp.concatenate([high, high, low], axis=axis)
+
+
+def cos_sin(angle):
+    square = angle * angle
+    cosine, sine = jnp.full_like(angle, 1.0), jnp.full_like(angle, 1.0)
+    for order in range(12, 0, -2):
+        cosine = 1.0 - cosine * square * (1.0 / (order * (order - 1)))
+        sine = 1.0 - sine * square * (1.0 / (order * (order + 1)))
+    return cosine, sine * angle
+
+
+def rotated(real_part, imag_part, cosine, sine):
+    return real_part * cosine + imag_part * sine, imag_part * cosine - real_part * sine
+
+
+def gather_planes(ref):
+    blocks = ref.shape[0]
+    return jnp.concatenate(
+        [
+            jnp.concatenate(
+                [ref[:, part, plane].reshape(blocks * PLANES, ROWS) for plane in range(PLANES)],
+                axis=1,
+            )
+            for part in range(2)
+        ],
+        axis=0,
+    )
+
+
+def natural(ref):
+    return jnp.concatenate([ref[plane] for plane in range(PLANES)], axis=1)
+
+
+def lane(value, plane):
+    return value[:, plane * ROWS : (plane + 1) * ROWS]
+
+
+def scatter_planes(real_part, imag_part, right_ref, out_ref):
+    rows = jnp.concatenate(
+        [
+            jnp.concatenate([lane(real_part, plane), lane(imag_part, plane)], axis=1)
+            for plane in range(PLANES)
+        ],
+        axis=0,
+    )
+    turned = from_right(rows, right_ref[...])
+    for plane in range(PLANES):
+        for part in range(2):
+            piece = turned[plane * ROWS : (plane + 1) * ROWS, part * ROWS : (part + 1) * ROWS]
+            for block in range(out_ref.shape[0]):
+                out_ref[block, part, pl.ds(plane, PLANES, stride=PLANES), :] = piece[
+                    block * PLANES : (block + 1) * PLANES
+                ]
+
+
+def mid_kernel(sign, field_ref, pot_ref, first_ref, second_ref, right_ref, out_ref):
+    field = from_left(first_ref[...], gather_planes(field_ref))
+    cosine, sine = cos_sin(sign * sub_time * natural(pot_ref))
+    real_part, imag_part = rotated(field[:ROWS], field[ROWS:], cosine, sine)
+    field = from_left(second_ref[...], jnp.concatenate([real_part, imag_part], axis=0))
+    scatter_planes(field[:ROWS], field[ROWS:], right_ref, out_ref)
+
+
+def store_natural(ref, part, value):
+    for plane in range(PLANES):
+        ref[part, plane] = lane(value, plane)
+
+
+def step_kernel(
+    sign, field_ref, pot_ref, first_ref, second_ref, right_ref, out_ref, keep_ref
+):
+    field = from_left(first_ref[...], gather_planes(field_ref))
+    cosine, sine = cos_sin(sign * 0.5 * sub_time * natural(pot_ref))
+    real_part, imag_part = rotated(field[:ROWS], field[ROWS:], cosine, sine)
+    store_natural(keep_ref, 0, real_part)
+    store_natural(keep_ref, 1, imag_part)
+    real_part, imag_part = rotated(real_part, imag_part, cosine, sine)
+    field = from_left(second_ref[...], jnp.concatenate([real_part, imag_part], axis=0))
+    scatter_planes(field[:ROWS], field[ROWS:], right_ref, out_ref)
+
+
+def start_kernel(sign, field_ref, pot_ref, second_ref, right_ref, out_ref):
+    cosine, sine = cos_sin(sign * 0.5 * sub_time * natural(pot_ref))
+    real_part, imag_part = rotated(
+        natural(field_ref.at[0]), natural(field_ref.at[1]), cosine, sine
+    )
+    field = from_left(second_ref[...], jnp.concatenate([real_part, imag_part], axis=0))
+    scatter_planes(field[:ROWS], field[ROWS:], right_ref, out_ref)
+
+
+def end_kernel(sign, field_ref, pot_ref, first_ref, other_ref, factor_ref, keep_ref, density_ref):
+    field = from_left(first_ref[...], gather_planes(field_ref))
+    cosine, sine = cos_sin(sign * 0.5 * sub_time * natural(pot_ref))
+    real_part, imag_part = rotated(field[:ROWS], field[ROWS:], cosine, sine)
+    store_natural(keep_ref, 0, real_part)
+    store_natural(keep_ref, 1, imag_part)
+    factor = factor_ref[0, 0]
+    for plane in range(PLANES):
+        density_ref[plane] = factor * (
+            lane(real_part, plane) * other_ref[0, plane]
+            + lane(imag_part, plane) * other_ref[1, plane]
+        )
+
+
+def final_kernel(sign, field_ref, pot_ref, first_ref, keep_ref):
+    field = from_left(first_ref[...], gather_planes(field_ref))
+    cosine, sine = cos_sin(sign * 0.5 * sub_time * natural(pot_ref))
+    real_part, imag_part = rotated(field[:ROWS], field[ROWS:], cosine, sine)
+    store_natural(keep_ref, 0, real_part)
+    store_natural(keep_ref, 1, imag_part)
+
+
+def stack_planes(value):
+    return jnp.concatenate([lane(value, plane) for plane in range(PLANES)], axis=0)
+
+
+def density_kernel(own_ref, other_ref, left_ref, right_ref, density_ref, out_ref):
+    density = natural(own_ref) + natural(other_ref)
+    for plane in range(PLANES):
+        density_ref[plane] = lane(density, plane)
+    spectrum = from_right(stack_planes(from_left(left_ref[...], density)), right_ref[...])
+    for plane in range(PLANES):
+        for block in range(out_ref.shape[0]):
+            start = plane * ROWS + block * PLANES
+            out_ref[block, pl.ds(plane, PLANES, stride=PLANES), :] = spectrum[
+                start : start + PLANES
+            ]
+
+
+def coulomb_kernel(unit, field_ref, square_ref, left_ref, out_ref):
+    blocks = field_ref.shape[0]
+    rows = jnp.concatenate(
+        [field_ref[:, line].reshape(ROWS, ROWS) for line in range(PLANES)], axis=1
+    )
+    rows = from_left(left_ref[...], rows)
+    index = lax.broadcasted_iota(jnp.int32, (ROWS, ROWS), 0)
+    number = unit * jnp.where(index < ROWS // 2, index, index - ROWS).astype(jnp.float32)
+    along = number * number
+    parts = []
+    for line in range(PLANES):
+        square = along + square_ref[pl.ds(line, 1), :]
+        nonzero = square > 0
+        parts.append(
+            lane(rows, line) * jnp.where(nonzero, 4.0 * math.pi / jnp.where(nonzero, square, 1.0), 0.0)
+        )
+    rows = from_left(left_ref[...], jnp.concatenate(parts, axis=1))
+    for line in range(PLANES):
+        out_ref[:, line] = lane(rows, line).reshape(blocks, PLANES, ROWS)
+
+
+def hartree_kernel(
+    sign,
+    field_ref,
+    density_ref,
+    xc_ref,
+    orbital_ref,
+    adjoint_ref,
+    pot_ref,
+    cas_left_ref,
+    cas_right_ref,
+    second_ref,
+    right_ref,
+    out_ref,
+    cross_ref,
+):
+    blocks = field_ref.shape[0]
+    spectrum = jnp.concatenate(
+        [
+            jnp.concatenate(
+                [
+                    field_ref[block, pl.ds(plane, PLANES, stride=PLANES), :]
+                    for block in range(blocks)
+                ],
+                axis=0,
+            )
+            for plane in range(PLANES)
+        ],
+        axis=1,
+    )
+    hartree = from_right(
+        stack_planes(from_left(cas_left_ref[...], spectrum)), cas_right_ref[...]
+    )
+    real_parts, imag_parts = [], []
+    for plane in range(PLANES):
+        cross = hartree[plane * ROWS : (plane + 1) * ROWS] + xc_ref[plane] * density_ref[plane]
+        cross_ref[plane] = cross
+        real_parts.append(adjoint_ref[0, plane] + step_time * cross * orbital_ref[1, plane])
+        imag_parts.append(adjoint_ref[1, plane] - step_time * cross * orbital_ref[0, plane])
+    cosine, sine = cos_sin(sign * 0.5 * sub_time * natural(pot_ref))
+    real_part, imag_part = rotated(
+        jnp.concatenate(real_parts, axis=1), jnp.concatenate(imag_parts, axis=1), cosine, sine
+    )
+    field = from_left(second_ref[...], jnp.concatenate([real_part, imag_part], axis=0))
+    scatter_planes(field[:ROWS], field[ROWS:], right_ref, out_ref)
+
+
+def run(kernel, outputs, *operands):
+    in_specs = [
+        pl.BlockSpec(memory_space=pltpu.SMEM if operand.size == 1 else pltpu.VMEM)
+        for operand in operands
+    ]
+    made = pl.pallas_call(
+        kernel,
+        out_shape=[jax.ShapeDtypeStruct(shape, jnp.float32) for shape in outputs],
+        in_specs=in_specs,
+        out_specs=[pl.BlockSpec(memory_space=pltpu.VMEM) for _ in outputs],
+        compiler_params=pltpu.CompilerParams(vmem_limit_bytes=40 * 2**20),
+    )(*operands)
+    return made[0] if len(outputs) == 1 else made
+
+
+def grouped(
+    orbitals, costate, potential, xc_kernel, vector_potential, kpoint_weight, occupation
+):
+    grid_size = potential.shape[1]
+    blocks = lax.axis_size("fft")
+    half = blocks // 2
+    core = lax.axis_index("ka")
+    fft_index = lax.axis_index("fft")
+    side = fft_index // half
+    place = core * half + fft_index % half
+    lattice_unit = 2.0 * math.pi / (grid_size * spacing)
+
+    groups = [
+        [c * blocks + h * half + j for c in range(2) for j in range(half)] for h in range(2)
+    ]
+    regroup = []
+    for c in range(2):
+        for f in range(blocks):
+            h, j = f // half, f % half
+            regroup.append((c * blocks + f, h * blocks + c * half + j))
+    across = [
+        (c * blocks + f, c * blocks + (f + half) % blocks) for c in range(2) for f in range(blocks)
+    ]
+
+    def exchange(array):
+        return lax.all_to_all(array, AXES, 0, 0, axis_index_groups=groups, tiled=True)
+
+    def move(array, pairs):
+        return lax.ppermute(array, AXES, pairs)
+
+    block_shape = (blocks, 2, PLANES, PLANES, ROWS)
+    sent_shape = (blocks, 2, PLANES * PLANES, ROWS)
+    natural_shape = (2, PLANES, ROWS, ROWS)
+    real_shape = (PLANES, ROWS, ROWS)
+
+    def swap_field(array):
+        return exchange(array.reshape(block_shape))
+
+    own = lax.dynamic_slice_in_dim(potential, core * (PLANES // 2), PLANES // 2, 0)
+    own = own.reshape(PLANES // 2, 2, half, PLANES, ROWS).transpose(1, 2, 0, 3, 4)
+    own = jnp.broadcast_to(own[:, None], (2, 2) + own.shape[1:]).reshape(
+        (2 * blocks, PLANES // 2, PLANES, ROWS)
+    )
+    got = lax.all_to_all(own, AXES, 0, 0, tiled=True)
+    got = got.reshape(2, blocks, PLANES // 2, PLANES, ROWS).transpose(3, 1, 0, 2, 4)
+    pot_cols = got.reshape(real_shape)
+    pot_rows = move(potential, regroup)
+
+    shift_x = lattice_unit * ((side.astype(jnp.float32) + 0.5) / 2 - 0.5) + vector_potential
+    shift_yz = jnp.array([lattice_unit * 0.25, -lattice_unit * 0.25], jnp.float32)
+    shifts = jnp.concatenate([shift_x, shift_yz])
+    lines = real_form(*line_matrices(shifts, grid_size)).reshape(-1, 2 * grid_size, 2 * grid_size)
+    back = jnp.transpose(lines, (0, 2, 1))
+    tables = {1.0: side_table(lines, 2), -1.0: side_table(back, 2)}
+    count_x = STEPS * SUB
+    right_z = {
+        1.0: side_table(back[count_x + 1], 0),
+        -1.0: side_table(lines[count_x + 1], 0),
+    }
+
+    angles = table_angles(grid_size)
+    cas = (jnp.cos(angles) + jnp.sin(angles)) / math.sqrt(grid_size)
+    cas_left, cas_right = side_table(cas, 1), side_table(cas, 0)
+    numbers = wave_numbers(lax.iota(jnp.int32, grid_size), grid_size)
+    own_numbers = wave_numbers(place * PLANES + lax.iota(jnp.int32, PLANES), grid_size)
+    squares = (own_numbers * own_numbers)[:, None] + (numbers * numbers)[None, :]
+
+    occupied = occupation.astype(jnp.float32) / 100.0
+    own_weight = lax.dynamic_slice_in_dim(kpoint_weight, side, 1)[0].astype(jnp.float32)
+    weight = own_weight / jnp.sum(kpoint_weight).astype(jnp.float32)
+    factor = (2.0 * weight * occupied).reshape(1, 1)
+
+    adjoint = move(costate.reshape(natural_shape), regroup)
+    xc_rows = move(xc_kernel, regroup)
+
+    def table_x(sign, count):
+        return tables[sign][count if sign > 0 else count_x - 1 - count]
+
+    def table_y(sign):
+        return tables[sign][count_x]
+
+    def middle(sign, field, in_rows, count):
+        if in_rows:
+            tabs = (pot_rows, table_y(sign), table_y(sign))
+        else:
+            tabs = (pot_cols, table_x(sign, count - 1), table_x(sign, count))
+        return run(
+            functools.partial(mid_kernel, sign), [sent_shape], field, *tabs, right_z[sign]
+        )
+
+    sent = run(
+        functools.partial(start_kernel, 1.0),
+        [sent_shape],
+        orbitals.reshape(natural_shape),
+        potential,
+        table_y(1.0),
+        right_z[1.0],
+    )
+    sent = move(sent, regroup)
+    kept = []
+    for count in range(1, count_x):
+        field = swap_field(sent)
+        in_rows = count % 2 == 0
+        if count % SUB == 0:
+            sent, orbital = run(
+                functools.partial(step_kernel, 1.0),
+                [sent_shape, natural_shape],
+                field,
+                pot_rows,
+                table_y(1.0),
+                table_y(1.0),
+                right_z[1.0],
+            )
+            kept.append(orbital)
+        else:
+            sent = middle(1.0, field, in_rows, count)
+    orbital, partial = run(
+        functools.partial(end_kernel, 1.0),
+        [natural_shape, real_shape],
+        swap_field(sent),
+        pot_rows,
+        table_y(1.0),
+        adjoint,
+        factor,
+    )
+    kept.append(orbital)
+
+    for step_index in range(STEPS - 1, -1, -1):
+        density, sent = run(
+            density_kernel,
+            [real_shape, (blocks, PLANES * PLANES, ROWS)],
+            partial,
+            move(partial, across),
+            cas_left,
+            cas_right,
+        )
+        field = exchange(sent.reshape(blocks, PLANES, PLANES, ROWS))
+        sent = run(
+            functools.partial(coulomb_kernel, lattice_unit),
+            [(blocks, PLANES, PLANES, ROWS)],
+            field,
+            squares,
+            cas_left,
+        )
+        field = exchange(sent).reshape(blocks, PLANES * PLANES, ROWS)
+        sent, cross = run(
+            functools.partial(hartree_kernel, -1.0),
+            [sent_shape, real_shape],
+            field,
+            density,
+            xc_rows,
+            kept[step_index],
+            adjoint,
+            pot_rows,
+            cas_left,
+            cas_right,
+            table_y(-1.0),
+            right_z[-1.0],
+        )
+        first = (STEPS - 1 - step_index) * SUB
+        for count in range(first + 1, first + SUB):
+            sent = middle(-1.0, swap_field(sent), count % 2 == 0, count)
+        field = swap_field(sent)
+        if step_index > 0:
+            adjoint, partial = run(
+                functools.partial(end_kernel, -1.0),
+                [natural_shape, real_shape],
+                field,
+                pot_rows,
+                table_y(-1.0),
+                kept[step_index - 1],
+                factor,
+            )
+        else:
+            adjoint = run(
+                functools.partial(final_kernel, -1.0),
+                [natural_shape],
+                field,
+                pot_rows,
+                table_y(-1.0),
+            )
+    result = move(adjoint, regroup).reshape(orbitals.shape)
+    beside = lax.ppermute(cross, "ka", [(0, 1), (1, 0)])
+    return (result, jnp.where(core == side, cross, beside))
+
+
 def solution(mesh):
     placed = (
         P("ka", None, None, "fft", None, None),
@@ -164,8 +593,19 @@
         P(),
         P(),
     )
+
+    def local(*arguments):
+        orbitals, potential = arguments[0], arguments[2]
+        fits = (
+            mesh.shape["ka"] == 2
+            and mesh.shape["fft"] % 2 == 0
+            and orbitals.shape[:2] == (1, 1)
+            and potential.shape == (PLANES, ROWS, ROWS)
+        )
+        return grouped(*arguments) if fits else plain(*arguments)
+
     return jax.shard_map(
-        plain,
+        local,
         mesh=mesh,
         in_specs=placed,
         out_specs=(P("ka", None, None, "fft", None, None), P("fft", None, None)),

time: 833 us -> 606 us (0.73)
  blocking collectives: 390 us -> 229 us
  matrix products: 116 us -> 2.85 us
  waiting for transfers between devices: 129 us -> 184 us
  Pallas kernels: 0 us -> 48.2 us
  local copies, waits for them, and re-layouts: 81 us -> 43.7 us
  other arithmetic: 40.1 us -> 19.2 us
  starting transfers between devices: 45.1 us -> 64 us
  between operations: 17.9 us -> 3.78 us
    all_to_all x14 -> x12, blocking collectives: 390 us -> 229 us  [the longest x11 193 us: exchange(): lax.all_to_all(array, AXES, 0, 0, axis_index_groups=groups, tiled=True)]
    ppermute x0 -> x8, waiting for transfers between devices: none -> 116 us  [the longest x7 114 us: move(): return lax.ppermute(array, AXES, pairs)]
    dot_general x60 -> x0, matrix products: 114 us -> none  [apply(): jnp.einsum(form, matrix, field, precision=lax.Precision.HIGHEST, preferre...]
    pallas_call x0 -> x23, Pallas kernels: none -> 48.2 us  [run(): pl.pallas_call(kernel, out_shape=[jax.ShapeDtypeStruct(shape, jnp.float32...]
    psum x2 -> x0, waiting for transfers between devices: 42.7 us -> none  [plain(): lax.psum(jnp.sum(band_factor[:, None, None, None] * jnp.sum(adjoint * for...]
    transpose x18 -> x2, local copies, waits for them, and re-layouts: 40.3 us -> 1.2 us  [the longest x1 1.18 us: grouped(): got.reshape(2, blocks, PLANES // 2, PLANES, ROWS).transpose(3, 1, 0, 2, 4)]
    another operation x13 -> x0, other arithmetic: 29 us -> none  [the longest x12 27.9 us: spin(): jnp.stack([field[0] * cosine + field[1] * sine, field[1] * cosine - field...]
    ppermute x0 -> x8, starting transfers between devices: none -> 23.4 us  [the longest x7 23.4 us: move(): return lax.ppermute(array, AXES, pairs)]
  transfers between devices with their start and end apart: 9 -> 17, of which waited for: 9 -> 14; matrix products, arithmetic and copies ran while one was open for 4% -> 4% of each run, Pallas kernels for 0% -> 0%
where the time goes in v2:
time: 606 us; the launch traced here: 595 us
  blocking collectives  229 us (38%)
  waiting for transfers between devices  184 us (30%)
  starting transfers between devices  64 us (11%)
  Pallas kernels  48.2 us (8%)
  local copies, waits for them, and re-layouts  43.7 us (7%)
  other arithmetic  19.2 us (3%)
    all_to_all x11, blocking collectives, exchange(): lax.all_to_all(array, AXES, 0, 0, axis_index_groups=groups, tiled=True)  193 us
    ppermute x7, waiting for transfers between devices, move(): return lax.ppermute(array, AXES, pairs)  114 us
    all_to_all x9, waiting for transfers between devices, exchange(): lax.all_to_all(array, AXES, 0, 0, axis_index_groups=groups, tiled=True)  67.9 us
    pallas_call x23, Pallas kernels, run(): pl.pallas_call(kernel, out_shape=[jax.ShapeDtypeStruct(shape, jnp.float32...  48.2 us
    all_to_all x9, starting transfers between devices, exchange(): lax.all_to_all(array, AXES, 0, 0, axis_index_groups=groups, tiled=True)  40.5 us
    all_to_all x1, blocking collectives, grouped(): got = lax.all_to_all(own, AXES, 0, 0, tiled=True)  36.5 us
    ppermute x7, starting transfers between devices, move(): return lax.ppermute(array, AXES, pairs)  23.4 us
    unnamed x75, local copies, waits for them, and re-layouts  22 us
  transfers between devices with their start and end apart: 17, of which 14 were waited for; matrix products, arithmetic and copies ran while one was open for 4% of the time, Pallas kernels for 0%

profile of v2, /device:TPU:1, one launch (start us, length us, event | category | flops | bytes accessed | tf_op | source)
XLA Modules:
  0.0 594.9 jit_solution(17025659120413597734)
XLA Ops:
  9.2 5.2 copy.28
  14.4 4.7 reshape.265
  27.4 5.6 collective-permute-start
  33.1 36.5 %all_to_all.105 = f32[32,4,8,128]{3,2,1,0:T(8,128)} all-to-all(f32[32,4,8,128]{3,2,1,0:T(8,128)S(1)} %bitcast.134), channel_id=1, replica_groups=mesh['ka'=2,'fft'=16] {'ka','fft'}, dimensions={0} | all-to-all | bytes 1048576 | tf_op jit(solution)/shard_map/all_to_all | solution.py:443
  69.6 4.8 all-to-all-start
  76.0 13.1 %all-to-all-done.field_ref = f32[16,2,8,8,128]{4,3,2,1,0:T(8,128)S(1)} async-done(((f32[16,2,8,8,128]{4,3,2,1,0:T(8,128)}), f32[16,2,8,8,128]{4,3,2,1,0:T(8,128)S(1)}, u32[]{:S(2)}, u32[]{:S(2)}) %all-to-all-start) | async-done | bytes 1048608 | tf_op jit(solution)/shard_map/all_to_all | solution.py:425
  92.2 4.5 all-to-all-start.2
  96.7 3.5 collective-permute-start.1
  100.2 14.7 %collective-permute-done.1.pot_ref = f32[8,128,128]{2,1,0:T(8,128)S(1)} collective-permute-done((f32[8,128,128]{2,1,0:T(8,128)S(1)}, f32[8,128,128]{2,1,0:T(8,128)S(1)}, u32[]{:S(2)}, u32[]{:S(2)}) %collective-permute-start.1) | collective-permute-done | bytes 524320 | tf_op jit(solution)/shard_map/ppermute | solution.py:428
  120.0 3.8 all-to-all-start.3
  123.8 3.1 fusion.7
  130.1 8.4 %all-to-all-done.3.field_ref = f32[16,2,8,8,128]{4,3,2,1,0:T(8,128)S(1)} async-done(((f32[16,2,8,8,128]{4,3,2,1,0:T(8,128)}), f32[16,2,8,8,128]{4,3,2,1,0:T(8,128)S(1)}, u32[]{:S(2)}, u32[]{:S(2)}) %all-to-all-start.3) | async-done | bytes 1048608 | tf_op jit(solution)/shard_map/all_to_all | solution.py:425
  141.6 19.1 %all_to_all.106.field_ref = f32[16,2,8,8,128]{4,3,2,1,0:T(8,128)S(1)} all-to-all(f32[16,2,8,8,128]{4,3,2,1,0:T(8,128)S(1)} %bitcast.119), channel_id=1, replica_groups={{0,1,2,3,4,5,6,7,16,17,18,19,20,21,22,23},{8,9,10,11,12,13,14,15,24,25,..., dimensions={0} | all-to-all | bytes 2097152 | tf_op jit(solution)/shard_map/all_to_all | solution.py:425
  163.9 4.7 all-to-all-start.5
  171.7 11.7 %all-to-all-done.5.field_ref = f32[16,2,8,8,128]{4,3,2,1,0:T(8,128)} async-done(((f32[16,2,8,8,128]{4,3,2,1,0:T(8,128)}), f32[16,2,8,8,128]{4,3,2,1,0:T(8,128)}, u32[]{:S(2)}, u32[]{:S(2)}) %all-to-all-start.5) | async-done | bytes 1048608 | tf_op jit(solution)/shard_map/all_to_all | solution.py:425
  184.4 3.3 shard_map.100
  187.7 19.1 %all_to_all.107.field_ref = f32[16,2,8,8,128]{4,3,2,1,0:T(8,128)S(1)} all-to-all(f32[16,2,8,8,128]{4,3,2,1,0:T(8,128)S(1)} %bitcast.120), channel_id=1, replica_groups={{0,1,2,3,4,5,6,7,16,17,18,19,20,21,22,23},{8,9,10,11,12,13,14,15,24,25,..., dimensions={0} | all-to-all | bytes 2097152 | tf_op jit(solution)/shard_map/all_to_all | solution.py:425
  209.9 5.0 all-to-all-start.7
  218.0 11.5 %all-to-all-done.7.field_ref = f32[16,2,8,8,128]{4,3,2,1,0:T(8,128)} async-done(((f32[16,2,8,8,128]{4,3,2,1,0:T(8,128)}), f32[16,2,8,8,128]{4,3,2,1,0:T(8,128)}, u32[]{:S(2)}, u32[]{:S(2)}) %all-to-all-start.7) | async-done | bytes 1048608 | tf_op jit(solution)/shard_map/all_to_all | solution.py:425
  230.5 3.3 shard_map.102
  234.8 4.6 all-to-all-start.8
  239.4 3.1 collective-permute-start.2
  245.7 22.1 %collective-permute-done.2.other_ref.adjoint_ref = f32[2,8,128,128]{3,2,1,0:T(8,128)} collective-permute-done((f32[2,8,128,128]{3,2,1,0:T(8,128)S(1)}, f32[2,8,128,128]{3,2,1,0:T(8,128)}, u32[]{:S(2)}, u32[]{:S(2)}) %collective-permute-start.2) | collective-permute-done | bytes 1048608 | tf_op jit(solution)/shard_map/ppermute | solution.py:428
  267.8 2.7 shard_map.103
  271.8 23.1 %collective-permute-done.3.other_ref = f32[8,128,128]{2,1,0:T(8,128)S(1)} collective-permute-done((f32[8,128,128]{2,1,0:T(8,128)S(1)}, f32[8,128,128]{2,1,0:T(8,128)S(1)}, u32[]{:S(2)}, u32[]{:S(2)}) %collective-permute-start.3) | collective-permute-done | bytes 524320 | tf_op jit(solution)/shard_map/ppermute | solution.py:428
  297.2 4.0 all-to-all-start.9
  301.3 9.2 %all-to-all-done.9.field_ref = f32[16,8,8,128]{3,2,1,0:T(8,128)S(1)} async-done(((f32[16,8,8,128]{3,2,1,0:T(8,128)}), f32[16,8,8,128]{3,2,1,0:T(8,128)S(1)}, u32[]{:S(2)}, u32[]{:S(2)}) %all-to-all-start.9) | async-done | bytes 524320 | tf_op jit(solution)/shard_map/all_to_all | solution.py:425
  311.9 4.6 all-to-all-start.10
  316.4 3.7 collective-permute-start.4
  324.2 9.5 %collective-permute-done.4.xc_ref = f32[8,128,128]{2,1,0:T(8,128)S(1)} collective-permute-done((f32[8,128,128]{2,1,0:T(8,128)}, f32[8,128,128]{2,1,0:T(8,128)S(1)}, u32[]{:S(2)}, u32[]{:S(2)}) %collective-permute-start.4) | collective-permute-done | bytes 524320 | tf_op jit(solution)/shard_map/ppermute | solution.py:428
  337.8 3.8 shard_map.106
  341.7 18.9 %all_to_all.108.field_ref = f32[16,2,8,8,128]{4,3,2,1,0:T(8,128)S(1)} all-to-all(f32[16,2,8,8,128]{4,3,2,1,0:T(8,128)S(1)} %bitcast.129), channel_id=1, replica_groups={{0,1,2,3,4,5,6,7,16,17,18,19,20,21,22,23},{8,9,10,11,12,13,14,15,24,25,..., dimensions={0} | all-to-all | bytes 2097152 | tf_op jit(solution)/shard_map/all_to_all | solution.py:425
  362.7 18.4 %all_to_all.109.field_ref = f32[16,2,8,8,128]{4,3,2,1,0:T(8,128)S(1)} all-to-all(f32[16,2,8,8,128]{4,3,2,1,0:T(8,128)S(1)} %bitcast.121), channel_id=1, replica_groups={{0,1,2,3,4,5,6,7,16,17,18,19,20,21,22,23},{8,9,10,11,12,13,14,15,24,25,..., dimensions={0} | all-to-all | bytes 2097152 | tf_op jit(solution)/shard_map/all_to_all | solution.py:425
  384.2 4.7 all-to-all-start.13
  388.8 3.0 fusion.6
  391.8 11.8 %all-to-all-done.13.field_ref = f32[16,2,8,8,128]{4,3,2,1,0:T(8,128)} async-done(((f32[16,2,8,8,128]{4,3,2,1,0:T(8,128)}), f32[16,2,8,8,128]{4,3,2,1,0:T(8,128)}, u32[]{:S(2)}, u32[]{:S(2)}) %all-to-all-start.13) | async-done | bytes 1048608 | tf_op jit(solution)/shard_map/all_to_all | solution.py:425
  405.6 3.3 shard_map.109
  408.9 19.1 %all_to_all.110.field_ref = f32[16,2,8,8,128]{4,3,2,1,0:T(8,128)S(1)} all-to-all(f32[16,2,8,8,128]{4,3,2,1,0:T(8,128)S(1)} %bitcast.122), channel_id=1, replica_groups={{0,1,2,3,4,5,6,7,16,17,18,19,20,21,22,23},{8,9,10,11,12,13,14,15,24,25,..., dimensions={0} | all-to-all | bytes 2097152 | tf_op jit(solution)/shard_map/all_to_all | solution.py:425
  429.3 2.9 collective-permute-start.5
  432.2 23.6 %collective-permute-done.5.other_ref = f32[8,128,128]{2,1,0:T(8,128)S(1)} collective-permute-done((f32[8,128,128]{2,1,0:T(8,128)S(1)}, f32[8,128,128]{2,1,0:T(8,128)S(1)}, u32[]{:S(2)}, u32[]{:S(2)}) %collective-permute-start.5) | collective-permute-done | bytes 524320 | tf_op jit(solution)/shard_map/ppermute | solution.py:428
  456.4 12.3 %all_to_all.111.field_ref = f32[16,8,8,128]{3,2,1,0:T(8,128)S(1)} all-to-all(f32[16,8,8,128]{3,2,1,0:T(8,128)S(1)} %bitcast.131), channel_id=1, replica_groups={{0,1,2,3,4,5,6,7,16,17,18,19,20,21,22,23},{8,9,10,11,12,13,14,15,24,25,..., dimensions={0} | all-to-all | bytes 1048576 | tf_op jit(solution)/shard_map/all_to_all | solution.py:425
  469.3 12.7 %all_to_all.112 = f32[16,8,8,128]{3,2,1,0:T(8,128)S(1)} all-to-all(f32[16,8,8,128]{3,2,1,0:T(8,128)S(1)} %shard_map.112), channel_id=1, replica_groups={{0,1,2,3,4,5,6,7,16,17,18,19,20,21,22,23},{8,9,10,11,12,13,14,15,24,25,..., dimensions={0} | all-to-all | bytes 1048576 | tf_op jit(solution)/shard_map/all_to_all | solution.py:425
  484.4 18.4 %all_to_all.113.field_ref = f32[16,2,8,8,128]{4,3,2,1,0:T(8,128)S(1)} all-to-all(f32[16,2,8,8,128]{4,3,2,1,0:T(8,128)S(1)} %bitcast.128), channel_id=1, replica_groups={{0,1,2,3,4,5,6,7,16,17,18,19,20,21,22,23},{8,9,10,11,12,13,14,15,24,25,..., dimensions={0} | all-to-all | bytes 2097152 | tf_op jit(solution)/shard_map/all_to_all | solution.py:425
  505.0 18.3 %all_to_all.114.field_ref = f32[16,2,8,8,128]{4,3,2,1,0:T(8,128)S(1)} all-to-all(f32[16,2,8,8,128]{4,3,2,1,0:T(8,128)S(1)} %bitcast.123), channel_id=1, replica_groups={{0,1,2,3,4,5,6,7,16,17,18,19,20,21,22,23},{8,9,10,11,12,13,14,15,24,25,..., dimensions={0} | all-to-all | bytes 2097152 | tf_op jit(solution)/shard_map/all_to_all | solution.py:425
  525.3 18.4 %all_to_all.115.field_ref = f32[16,2,8,8,128]{4,3,2,1,0:T(8,128)S(1)} all-to-all(f32[16,2,8,8,128]{4,3,2,1,0:T(8,128)S(1)} %bitcast.124), channel_id=1, replica_groups={{0,1,2,3,4,5,6,7,16,17,18,19,20,21,22,23},{8,9,10,11,12,13,14,15,24,25,..., dimensions={0} | all-to-all | bytes 2097152 | tf_op jit(solution)/shard_map/all_to_all | solution.py:425
  545.8 18.3 %all_to_all.116.field_ref = f32[16,2,8,8,128]{4,3,2,1,0:T(8,128)S(1)} all-to-all(f32[16,2,8,8,128]{4,3,2,1,0:T(8,128)S(1)} %bitcast.118), channel_id=1, replica_groups={{0,1,2,3,4,5,6,7,16,17,18,19,20,21,22,23},{8,9,10,11,12,13,14,15,24,25,..., dimensions={0} | all-to-all | bytes 2097152 | tf_op jit(solution)/shard_map/all_to_all | solution.py:425
  565.2 4.5 collective-permute-start.6
  572.8 20.7 %collective-permute-done.6 = f32[2,8,128,128]{3,2,1,0:T(8,128)S(1)} collective-permute-done((f32[2,8,128,128]{3,2,1,0:T(8,128)S(1)}, f32[2,8,128,128]{3,2,1,0:T(8,128)S(1)}, u32[]{:S(2)}, u32[]{:S(2)}) %collective-permute-start.6) | collective-permute-done | bytes 1048608 | tf_op jit(solution)/shard_map/ppermute | solution.py:428
  (144 shorter events, 85.7 us)
Async XLA Ops:
  6.0 1.1 copy-start.27
  6.0 1.5 copy-start.28
  21.3 2.2 copy-start.29
  21.4 2.2 copy-start.30
  22.6 1.5 copy-start.21
  23.5 1.1 copy-start.17
  27.4 42.2 %collective-permute-start = (f32[16,2,64,128]{3,2,1,0:T(8,128)}, f32[16,2,64,128]{3,2,1,0:T(8,128)}, u32[]{:S(2)}, u32[]{:S(2)}) collective-permute-start(f32[16,2,64,128]{3,2,1,0:T(8,128)} %shard_map.95), channel_id=1, source_target_pairs={{0,0},{1,1},{2,2},{3,3},{4,4},{5,5},{6,6},{7,7},{8,16},{9,17},{10,... | collective-permute-start | bytes 3145736 | tf_op jit(solution)/shard_map/ppermute | solution.py:428
  69.6 4.9 copy-start.34
  69.6 5.0 copy-start.33
  69.6 19.5 %all-to-all-start = ((f32[16,2,8,8,128]{4,3,2,1,0:T(8,128)}), f32[16,2,8,8,128]{4,3,2,1,0:T(8,128)S(1)}, u32[]{:S(2)}, u32[]{:S(2)}) async-start(f32[16,2,8,8,128]{4,3,2,1,0:T(8,128)} %bitcast.12), calls=%async_computation | async-start | bytes 2097152 | tf_op jit(solution)/shard_map/all_to_all | solution.py:425
  91.2 1.0 copy-start.2
  92.2 4.5 copy-start.18
  92.2 24.8 %all-to-all-start.2 = ((f32[16,2,8,8,128]{4,3,2,1,0:T(8,128)}), f32[16,2,8,8,128]{4,3,2,1,0:T(8,128)S(1)}, u32[]{:S(2)}, u32[]{:S(2)}) async-start(f32[16,2,8,8,128]{4,3,2,1,0:T(8,128)} %bitcast.115), calls=%async_computation.2 | async-start | bytes 2097152 | tf_op jit(solution)/shard_map/all_to_all | solution.py:425
  96.7 18.2 %collective-permute-start.1 = (f32[8,128,128]{2,1,0:T(8,128)S(1)}, f32[8,128,128]{2,1,0:T(8,128)S(1)}, u32[]{:S(2)}, u32[]{:S(2)}) collective-permute-start(f32[8,128,128]{2,1,0:T(8,128)S(1)} %copy-done.18), channel_id=1, source_target_pairs={{0,0},{1,1},{2,2},{3,3},{4,4},{5,5},{6,6},{7,7},{8,16},{9,17},{10,... | collective-permute-start | bytes 1572872 | tf_op jit(solution)/shard_map/ppermute | solution.py:428
  119.1 1.0 copy-start.1
  120.0 18.4 %all-to-all-start.3 = ((f32[16,2,8,8,128]{4,3,2,1,0:T(8,128)}), f32[16,2,8,8,128]{4,3,2,1,0:T(8,128)S(1)}, u32[]{:S(2)}, u32[]{:S(2)}) async-start(f32[16,2,8,8,128]{4,3,2,1,0:T(8,128)} %bitcast.114), calls=%async_computation.3 | async-start | bytes 2097152 | tf_op jit(solution)/shard_map/all_to_all | solution.py:425
  138.5 1.0 copy-start.15
  163.0 1.0 copy-start.22
  163.9 19.4 %all-to-all-start.5 = ((f32[16,2,8,8,128]{4,3,2,1,0:T(8,128)}), f32[16,2,8,8,128]{4,3,2,1,0:T(8,128)}, u32[]{:S(2)}, u32[]{:S(2)}) async-start(f32[16,2,8,8,128]{4,3,2,1,0:T(8,128)} %bitcast.127), calls=%async_computation.5 | async-start | bytes 2097152 | tf_op jit(solution)/shard_map/all_to_all | solution.py:425
  183.4 1.0 copy-start.16
  208.9 1.0 copy-start.4
  209.9 19.6 %all-to-all-start.7 = ((f32[16,2,8,8,128]{4,3,2,1,0:T(8,128)}), f32[16,2,8,8,128]{4,3,2,1,0:T(8,128)}, u32[]{:S(2)}, u32[]{:S(2)}) async-start(f32[16,2,8,8,128]{4,3,2,1,0:T(8,128)} %bitcast.117), calls=%async_computation.7 | async-start | bytes 2097152 | tf_op jit(solution)/shard_map/all_to_all | solution.py:425
  229.5 1.0 copy-start.14
  234.8 4.6 copy-start.35
  234.8 8.3 %copy-start.36 = (s32[2]{0:T(128)S(1)}, s32[2]{0:T(128)}, u32[]{:S(2)}) copy-start(s32[2]{0:T(128)} %param.13) | copy-start | bytes 28
  234.8 33.0 %all-to-all-start.8 = ((f32[16,2,8,8,128]{4,3,2,1,0:T(8,128)}), f32[16,2,8,8,128]{4,3,2,1,0:T(8,128)}, u32[]{:S(2)}, u32[]{:S(2)}) async-start(f32[16,2,8,8,128]{4,3,2,1,0:T(8,128)} %bitcast.113), calls=%async_computation.8 | async-start | bytes 2097152 | tf_op jit(solution)/shard_map/all_to_all | solution.py:425
  239.4 28.4 %collective-permute-start.2 = (f32[2,8,128,128]{3,2,1,0:T(8,128)S(1)}, f32[2,8,128,128]{3,2,1,0:T(8,128)}, u32[]{:S(2)}, u32[]{:S(2)}) collective-permute-start(f32[2,8,128,128]{3,2,1,0:T(8,128)S(1)} %bitcast.138), channel_id=1, source_target_pairs={{0,0},{1,1},{2,2},{3,3},{4,4},{5,5},{6,6},{7,7},{8,16},{9,17},{10,... | collective-permute-start | bytes 3145736 | tf_op jit(solution)/shard_map/ppermute | solution.py:428
  271.5 23.4 %collective-permute-start.3 = (f32[8,128,128]{2,1,0:T(8,128)S(1)}, f32[8,128,128]{2,1,0:T(8,128)S(1)}, u32[]{:S(2)}, u32[]{:S(2)}) collective-permute-start(f32[8,128,128]{2,1,0:T(8,128)S(1)} %get-tuple-element.16.own_ref), channel_id=1, source_target_pairs={{0,8},{1,9},{2,10},{3,11},{4,12},{5,13},{6,14},{7,15},{8,0},{9,1},... | collective-permute-start | bytes 1572872 | tf_op jit(solution)/shard_map/ppermute | solution.py:428
  297.2 13.3 %all-to-all-start.9 = ((f32[16,8,8,128]{3,2,1,0:T(8,128)}), f32[16,8,8,128]{3,2,1,0:T(8,128)S(1)}, u32[]{:S(2)}, u32[]{:S(2)}) async-start(f32[16,8,8,128]{3,2,1,0:T(8,128)} %bitcast.130), calls=%async_computation.9 | async-start | bytes 1048576 | tf_op jit(solution)/shard_map/all_to_all | solution.py:425
  311.9 22.7 %all-to-all-start.10 = ((f32[16,8,8,128]{3,2,1,0:T(8,128)}), f32[16,8,8,128]{3,2,1,0:T(8,128)}, u32[]{:S(2)}, u32[]{:S(2)}) async-start(f32[16,8,8,128]{3,2,1,0:T(8,128)} %shard_map.105), calls=%async_computation.10 | async-start | bytes 1048576 | tf_op jit(solution)/shard_map/all_to_all | solution.py:425
  316.4 17.3 %collective-permute-start.4 = (f32[8,128,128]{2,1,0:T(8,128)}, f32[8,128,128]{2,1,0:T(8,128)S(1)}, u32[]{:S(2)}, u32[]{:S(2)}) collective-permute-start(f32[8,128,128]{2,1,0:T(8,128)} %param.11), channel_id=1, source_target_pairs={{0,0},{1,1},{2,2},{3,3},{4,4},{5,5},{6,6},{7,7},{8,16},{9,17},{10,... | collective-permute-start | bytes 1572872 | tf_op jit(solution)/shard_map/ppermute | solution.py:428
  320.2 1.9 copy-start.26
  322.6 1.2 copy-start.31
  322.6 1.6 copy-start.32
  334.5 1.0 copy-start.6
  335.6 1.2 copy-start.20
  336.8 1.0 copy-start.24
  341.7 18.9 %copy-start.11 = (bf16[256,768]{1,0:T(8,128)(2,1)S(1)}, bf16[256,768]{1,0:T(8,128)(2,1)}, u32[]{:S(2)}) copy-start(bf16[256,768]{1,0:T(8,128)(2,1)} %get-tuple-element.37.first_ref) | copy-start | bytes 1179652
  384.2 19.4 %all-to-all-start.13 = ((f32[16,2,8,8,128]{4,3,2,1,0:T(8,128)}), f32[16,2,8,8,128]{4,3,2,1,0:T(8,128)}, u32[]{:S(2)}, u32[]{:S(2)}) async-start(f32[16,2,8,8,128]{4,3,2,1,0:T(8,128)} %bitcast.116), calls=%async_computation.13 | async-start | bytes 2097152 | tf_op jit(solution)/shard_map/all_to_all | solution.py:425
  403.6 1.0 copy-start.12
  404.6 1.0 copy-start.13
  429.3 26.5 %collective-permute-start.5 = (f32[8,128,128]{2,1,0:T(8,128)S(1)}, f32[8,128,128]{2,1,0:T(8,128)S(1)}, u32[]{:S(2)}, u32[]{:S(2)}) collective-permute-start(f32[8,128,128]{2,1,0:T(8,128)S(1)} %get-tuple-element.22.own_ref), channel_id=1, source_target_pairs={{0,8},{1,9},{2,10},{3,11},{4,12},{5,13},{6,14},{7,15},{8,0},{9,1},... | collective-permute-start | bytes 1572872 | tf_op jit(solution)/shard_map/ppermute | solution.py:428
  468.7 13.2 %copy-start.7 = (f32[8,128,128]{2,1,0:T(8,128)S(1)}, f32[8,128,128]{2,1,0:T(8,128)}, u32[]{:S(2)}) copy-start(f32[8,128,128]{2,1,0:T(8,128)} %copy-done.5) | copy-start | bytes 1572868
  484.4 18.5 %copy-start.9 = (bf16[256,768]{1,0:T(8,128)(2,1)S(1)}, bf16[256,768]{1,0:T(8,128)(2,1)}, u32[]{:S(2)}) copy-start(bf16[256,768]{1,0:T(8,128)(2,1)} %get-tuple-element.32.second_ref) | copy-start | bytes 1179652
  484.4 18.4 %copy-start.10 = (bf16[256,768]{1,0:T(8,128)(2,1)S(1)}, bf16[256,768]{1,0:T(8,128)(2,1)}, u32[]{:S(2)}) copy-start(bf16[256,768]{1,0:T(8,128)(2,1)} %get-tuple-element.33.first_ref) | copy-start | bytes 1179652
  525.3 18.4 %copy-start.8 = (bf16[256,768]{1,0:T(8,128)(2,1)S(1)}, bf16[256,768]{1,0:T(8,128)(2,1)}, u32[]{:S(2)}) copy-start(bf16[256,768]{1,0:T(8,128)(2,1)} %get-tuple-element.31.first_ref) | copy-start | bytes 1179652
  565.2 28.3 %collective-permute-start.6 = (f32[2,8,128,128]{3,2,1,0:T(8,128)S(1)}, f32[2,8,128,128]{3,2,1,0:T(8,128)S(1)}, u32[]{:S(2)}, u32[]{:S(2)}) collective-permute-start(f32[2,8,128,128]{3,2,1,0:T(8,128)S(1)} %shard_map.117), channel_id=1, source_target_pairs={{0,0},{1,1},{2,2},{3,3},{4,4},{5,5},{6,6},{7,7},{8,16},{9,17},{10,... | collective-permute-start | bytes 3145736 | tf_op jit(solution)/shard_map/ppermute | solution.py:428
  569.7 2.2 collective-permute-start.7
  (6 other events, 5.3 us)

commit v3 on v2

--- a/solution.py
+++ b/solution.py
@@ -3,6 +3,7 @@
 
 import jax
 import jax.numpy as jnp
+import numpy as np
 from jax import lax
 from jax.experimental import pallas as pl
 from jax.experimental.pallas import tpu as pltpu
@@ -168,24 +169,69 @@
 
 
 def from_left(table, field):
+    size = table.shape[1] // 2
     high, low = halves_of(field)
     return jnp.dot(
-        table, jnp.concatenate([high, low, high], axis=0), preferred_element_type=jnp.float32
+        jnp.concatenate([table[:, :size], table], axis=1),
+        jnp.concatenate([high, low, high], axis=0),
+        preferred_element_type=jnp.float32,
     )
 
 
 def from_right(field, table):
+    size = table.shape[0] // 2
     high, low = halves_of(field)
     return jnp.dot(
-        jnp.concatenate([high, low, high], axis=1), table, preferred_element_type=jnp.float32
-    )
-
-
-def side_table(matrix, axis):
-    high = lax.reduce_precision(matrix, 8, 7)
-    low = (matrix - high).astype(jnp.bfloat16)
-    high = high.astype(jnp.bfloat16)
-    return jnp.concatenate([high, high, low], axis=axis)
+        jnp.concatenate([high, low, high], axis=1),
+        jnp.concatenate([table[:size], table], axis=0),
+        preferred_element_type=jnp.float32,
+    )
+
+
+def side_by_side(matrix, axis):
+    return jnp.concatenate(halves_of(matrix), axis=axis)
+
+
+def circulant(shift, numbers, cosine, sine):
+    along = shift + numbers
+    phase = 0.5 * sub_time * (along * along)
+    q_real, q_imag = jnp.cos(phase), -jnp.sin(phase)
+    even = q_real * cosine + q_imag * sine
+    odd = q_real * sine - q_imag * cosine
+    spectrum = jnp.concatenate(
+        [jnp.concatenate([even, odd], axis=1), jnp.concatenate([odd, -even], axis=1)], axis=0
+    )
+    upper = jnp.dot(
+        jnp.concatenate([cosine, sine], axis=1),
+        spectrum,
+        precision=highest,
+        preferred_element_type=jnp.float32,
+    ) * (1.0 / ROWS)
+    real_part, minus = upper[:, :ROWS], upper[:, ROWS:]
+    real_turned, minus_turned = real_part.T, minus.T
+    return upper, jnp.concatenate([real_turned, -minus_turned], axis=1)
+
+
+def whole_matrix(upper):
+    real_part, minus = upper[:, :ROWS], upper[:, ROWS:]
+    return jnp.concatenate([upper, jnp.concatenate([-minus, real_part], axis=1)], axis=0)
+
+
+def whole_left(table):
+    return jnp.concatenate(
+        [whole_matrix(table[:, : 2 * ROWS]), whole_matrix(table[:, 2 * ROWS :])], axis=1
+    )
+
+
+def table_kernel(count_x, shift_ref, numbers_ref, lines_ref, *out_refs):
+    numbers, cosine, sine = numbers_ref[...], lines_ref[:, :ROWS], lines_ref[:, ROWS:]
+    for line in range(count_x + 1):
+        matrix, turned = circulant(shift_ref[line], numbers, cosine, sine)
+        out_refs[2 * line][...] = side_by_side(matrix, 1)
+        out_refs[2 * line + 1][...] = side_by_side(turned, 1)
+    matrix, turned = circulant(shift_ref[count_x + 1], numbers, cosine, sine)
+    out_refs[2 * count_x + 2][...] = side_by_side(whole_matrix(turned), 0)
+    out_refs[2 * count_x + 3][...] = side_by_side(whole_matrix(matrix), 0)
 
 
 def cos_sin(angle):
@@ -219,11 +265,30 @@
     return jnp.concatenate([ref[plane] for plane in range(PLANES)], axis=1)
 
 
+def strided(ref, plane):
+    return jnp.concatenate(
+        [ref[block, pl.ds(plane, PLANES, stride=PLANES), :] for block in range(ref.shape[0])],
+        axis=0,
+    )
+
+
+def angles_of(ref):
+    if len(ref.shape) == 3:
+        return jnp.concatenate([strided(ref, plane) for plane in range(PLANES)], axis=1)
+    if ref.shape[2] == PLANES * PLANES:
+        return angles_of(ref.at[:, 2])
+    if len(ref.shape) == 5:
+        return angles_of(ref.at[:, 2])
+    return jnp.concatenate(
+        [ref[:, plane].reshape(ROWS, ROWS) for plane in range(PLANES)], axis=1
+    )
+
+
 def lane(value, plane):
     return value[:, plane * ROWS : (plane + 1) * ROWS]
 
 
-def scatter_planes(real_part, imag_part, right_ref, out_ref):
+def scatter_planes(real_part, imag_part, table, out_ref):
     rows = jnp.concatenate(
         [
             jnp.concatenate([lane(real_part, plane), lane(imag_part, plane)], axis=1)
@@ -231,7 +296,7 @@
         ],
         axis=0,
     )
-    turned = from_right(rows, right_ref[...])
+    turned = from_right(rows, table)
     for plane in range(PLANES):
         for part in range(2):
             piece = turned[plane * ROWS : (plane + 1) * ROWS, part * ROWS : (part + 1) * ROWS]
@@ -242,60 +307,99 @@
 
 
 def mid_kernel(sign, field_ref, pot_ref, first_ref, second_ref, right_ref, out_ref):
-    field = from_left(first_ref[...], gather_planes(field_ref))
-    cosine, sine = cos_sin(sign * sub_time * natural(pot_ref))
+    field = from_left(whole_left(first_ref[...]), gather_planes(field_ref))
+    cosine, sine = cos_sin(sign * sub_time * angles_of(pot_ref))
     real_part, imag_part = rotated(field[:ROWS], field[ROWS:], cosine, sine)
-    field = from_left(second_ref[...], jnp.concatenate([real_part, imag_part], axis=0))
-    scatter_planes(field[:ROWS], field[ROWS:], right_ref, out_ref)
-
-
-def store_natural(ref, part, value):
+    field = from_left(whole_left(second_ref[...]), jnp.concatenate([real_part, imag_part], axis=0))
+    scatter_planes(field[:ROWS], field[ROWS:], right_ref[...], out_ref)
+
+
+def first_mid_kernel(sign, field_ref, first_ref, second_ref, right_ref, out_ref, pot_ref):
+    mid_kernel(sign, field_ref, field_ref, first_ref, second_ref, right_ref, out_ref)
+    pot_ref[...] = field_ref[:, 2]
+
+
+def second_mid_kernel(
+    sign, field_ref, pot_field_ref, first_ref, second_ref, right_ref, out_ref, pot_ref
+):
+    mid_kernel(sign, field_ref, pot_field_ref, first_ref, second_ref, right_ref, out_ref)
+    pot_ref[...] = pot_field_ref[:, 2]
+
+
+def store_natural(ref, value):
     for plane in range(PLANES):
-        ref[part, plane] = lane(value, plane)
+        ref[plane] = lane(value, plane)
 
 
 def step_kernel(
-    sign, field_ref, pot_ref, first_ref, second_ref, right_ref, out_ref, keep_ref
+    sign, field_ref, pot_ref, first_ref, second_ref, right_ref, out_ref, real_ref, imag_ref
 ):
-    field = from_left(first_ref[...], gather_planes(field_ref))
-    cosine, sine = cos_sin(sign * 0.5 * sub_time * natural(pot_ref))
+    field = from_left(whole_left(first_ref[...]), gather_planes(field_ref))
+    cosine, sine = cos_sin(sign * 0.5 * sub_time * angles_of(pot_ref))
     real_part, imag_part = rotated(field[:ROWS], field[ROWS:], cosine, sine)
-    store_natural(keep_ref, 0, real_part)
-    store_natural(keep_ref, 1, imag_part)
+    store_natural(real_ref, real_part)
+    store_natural(imag_ref, imag_part)
     real_part, imag_part = rotated(real_part, imag_part, cosine, sine)
-    field = from_left(second_ref[...], jnp.concatenate([real_part, imag_part], axis=0))
-    scatter_planes(field[:ROWS], field[ROWS:], right_ref, out_ref)
-
-
-def start_kernel(sign, field_ref, pot_ref, second_ref, right_ref, out_ref):
-    cosine, sine = cos_sin(sign * 0.5 * sub_time * natural(pot_ref))
+    field = from_left(whole_left(second_ref[...]), jnp.concatenate([real_part, imag_part], axis=0))
+    scatter_planes(field[:ROWS], field[ROWS:], right_ref[...], out_ref)
+
+
+def start_kernel(
+    unit, field_ref, pot_ref, lines_ref, out_ref, numbers_ref
+):
+    cosine_line, sine_line = lines_ref[:, :ROWS], lines_ref[:, ROWS:]
+    index = lax.broadcasted_iota(jnp.int32, (ROWS, ROWS), 0)
+    numbers = wave_numbers(index, ROWS)
+    numbers_ref[...] = numbers
+    table_y = circulant(0.25 * unit, numbers, cosine_line, sine_line)[0]
+    table_z = circulant(-0.25 * unit, numbers, cosine_line, sine_line)[1]
+    cosine, sine = cos_sin(0.5 * sub_time * natural(pot_ref))
     real_part, imag_part = rotated(
         natural(field_ref.at[0]), natural(field_ref.at[1]), cosine, sine
     )
-    field = from_left(second_ref[...], jnp.concatenate([real_part, imag_part], axis=0))
-    scatter_planes(field[:ROWS], field[ROWS:], right_ref, out_ref)
-
-
-def end_kernel(sign, field_ref, pot_ref, first_ref, other_ref, factor_ref, keep_ref, density_ref):
-    field = from_left(first_ref[...], gather_planes(field_ref))
-    cosine, sine = cos_sin(sign * 0.5 * sub_time * natural(pot_ref))
+    field = from_left(side_by_side(whole_matrix(table_y), 1), jnp.concatenate([real_part, imag_part], axis=0))
+    scatter_planes(field[:ROWS], field[ROWS:], side_by_side(whole_matrix(table_z), 0), out_ref)
+    for plane in range(PLANES):
+        for block in range(out_ref.shape[0]):
+            out_ref[block, 2, pl.ds(plane, PLANES, stride=PLANES), :] = pot_ref[
+                plane, block * PLANES : (block + 1) * PLANES
+            ]
+
+
+def finish(sign, field_ref, pot_ref, first_ref, real_ref, imag_ref):
+    field = from_left(whole_left(first_ref[...]), gather_planes(field_ref))
+    cosine, sine = cos_sin(sign * 0.5 * sub_time * angles_of(pot_ref))
     real_part, imag_part = rotated(field[:ROWS], field[ROWS:], cosine, sine)
-    store_natural(keep_ref, 0, real_part)
-    store_natural(keep_ref, 1, imag_part)
+    store_natural(real_ref, real_part)
+    store_natural(imag_ref, imag_part)
+    return real_part, imag_part
+
+
+def end_kernel(
+    sign,
+    field_ref,
+    pot_ref,
+    first_ref,
+    other_real_ref,
+    other_imag_ref,
+    factor_ref,
+    real_ref,
+    imag_ref,
+    density_ref,
+):
+    real_part, imag_part = finish(sign, field_ref, pot_ref, first_ref, real_ref, imag_ref)
     factor = factor_ref[0, 0]
     for plane in range(PLANES):
         density_ref[plane] = factor * (
-            lane(real_part, plane) * other_ref[0, plane]
-            + lane(imag_part, plane) * other_ref[1, plane]
+            lane(real_part, plane) * other_real_ref[plane]
+            + lane(imag_part, plane) * other_imag_ref[plane]
         )
 
 
-def final_kernel(sign, field_ref, pot_ref, first_ref, keep_ref):
-    field = from_left(first_ref[...], gather_planes(field_ref))
-    cosine, sine = cos_sin(sign * 0.5 * sub_time * natural(pot_ref))
-    real_part, imag_part = rotated(field[:ROWS], field[ROWS:], cosine, sine)
-    store_natural(keep_ref, 0, real_part)
-    store_natural(keep_ref, 1, imag_part)
+def final_kernel(sign, field_ref, pot_ref, first_ref, out_ref):
+    finish(
+        sign, field_ref, pot_ref, first_ref, out_ref.at[0, 0, 0], out_ref.at[0, 0, 1]
+    )
 
 
 def stack_planes(value):
@@ -341,8 +445,10 @@
     field_ref,
     density_ref,
     xc_ref,
-    orbital_ref,
-    adjoint_ref,
+    orbital_real_ref,
+    orbital_imag_ref,
+    adjoint_real_ref,
+    adjoint_imag_ref,
     pot_ref,
     cas_left_ref,
     cas_right_ref,
@@ -351,20 +457,7 @@
     out_ref,
     cross_ref,
 ):
-    blocks = field_ref.shape[0]
-    spectrum = jnp.concatenate(
-        [
-            jnp.concatenate(
-                [
-                    field_ref[block, pl.ds(plane, PLANES, stride=PLANES), :]
-                    for block in range(blocks)
-                ],
-                axis=0,
-            )
-            for plane in range(PLANES)
-        ],
-        axis=1,
-    )
+    spectrum = angles_of(field_ref)
     hartree = from_right(
         stack_planes(from_left(cas_left_ref[...], spectrum)), cas_right_ref[...]
     )
@@ -372,27 +465,29 @@
     for plane in range(PLANES):
         cross = hartree[plane * ROWS : (plane + 1) * ROWS] + xc_ref[plane] * density_ref[plane]
         cross_ref[plane] = cross
-        real_parts.append(adjoint_ref[0, plane] + step_time * cross * orbital_ref[1, plane])
-        imag_parts.append(adjoint_ref[1, plane] - step_time * cross * orbital_ref[0, plane])
-    cosine, sine = cos_sin(sign * 0.5 * sub_time * natural(pot_ref))
+        real_parts.append(adjoint_real_ref[plane] + step_time * cross * orbital_imag_ref[plane])
+        imag_parts.append(adjoint_imag_ref[plane] - step_time * cross * orbital_real_ref[plane])
+    cosine, sine = cos_sin(sign * 0.5 * sub_time * angles_of(pot_ref))
     real_part, imag_part = rotated(
         jnp.concatenate(real_parts, axis=1), jnp.concatenate(imag_parts, axis=1), cosine, sine
     )
-    field = from_left(second_ref[...], jnp.concatenate([real_part, imag_part], axis=0))
-    scatter_planes(field[:ROWS], field[ROWS:], right_ref, out_ref)
+    field = from_left(whole_left(second_ref[...]), jnp.concatenate([real_part, imag_part], axis=0))
+    scatter_planes(field[:ROWS], field[ROWS:], right_ref[...], out_ref)
 
 
 def run(kernel, outputs, *operands):
-    in_specs = [
-        pl.BlockSpec(memory_space=pltpu.SMEM if operand.size == 1 else pltpu.VMEM)
-        for operand in operands
-    ]
     made = pl.pallas_call(
         kernel,
-        out_shape=[jax.ShapeDtypeStruct(shape, jnp.float32) for shape in outputs],
-        in_specs=in_specs,
+        out_shape=[
+            jax.ShapeDtypeStruct(out, jnp.float32) if isinstance(out, tuple) else out
+            for out in outputs
+        ],
+        in_specs=[
+            pl.BlockSpec(memory_space=pltpu.SMEM if operand.size < ROWS else pltpu.VMEM)
+            for operand in operands
+        ],
         out_specs=[pl.BlockSpec(memory_space=pltpu.VMEM) for _ in outputs],
-        compiler_params=pltpu.CompilerParams(vmem_limit_bytes=40 * 2**20),
+        compiler_params=pltpu.CompilerParams(vmem_limit_bytes=24 * 2**20),
     )(*operands)
     return made[0] if len(outputs) == 1 else made
 
@@ -435,31 +530,21 @@
     def swap_field(array):
         return exchange(array.reshape(block_shape))
 
-    own = lax.dynamic_slice_in_dim(potential, core * (PLANES // 2), PLANES // 2, 0)
-    own = own.reshape(PLANES // 2, 2, half, PLANES, ROWS).transpose(1, 2, 0, 3, 4)
-    own = jnp.broadcast_to(own[:, None], (2, 2) + own.shape[1:]).reshape(
-        (2 * blocks, PLANES // 2, PLANES, ROWS)
-    )
-    got = lax.all_to_all(own, AXES, 0, 0, tiled=True)
-    got = got.reshape(2, blocks, PLANES // 2, PLANES, ROWS).transpose(3, 1, 0, 2, 4)
-    pot_cols = got.reshape(real_shape)
-    pot_rows = move(potential, regroup)
+    grid_line = np.arange(grid_size)
+    angles = 2.0 * np.pi / grid_size * (np.outer(grid_line, grid_line) % grid_size)
+    line_pair = jnp.asarray(
+        np.concatenate([np.cos(angles), np.sin(angles)], axis=1).astype(np.float32)
+    )
+    cas = (np.cos(angles) + np.sin(angles)) / math.sqrt(grid_size)
+    cas_high = cas.astype(jnp.bfloat16)
+    cas_low = (cas - cas_high.astype(np.float64)).astype(jnp.bfloat16)
+    cas_left = jnp.asarray(np.concatenate([cas_high, cas_low], axis=1))
+    cas_right = jnp.asarray(np.concatenate([cas_high, cas_low], axis=0))
 
     shift_x = lattice_unit * ((side.astype(jnp.float32) + 0.5) / 2 - 0.5) + vector_potential
     shift_yz = jnp.array([lattice_unit * 0.25, -lattice_unit * 0.25], jnp.float32)
-    shifts = jnp.concatenate([shift_x, shift_yz])
-    lines = real_form(*line_matrices(shifts, grid_size)).reshape(-1, 2 * grid_size, 2 * grid_size)
-    back = jnp.transpose(lines, (0, 2, 1))
-    tables = {1.0: side_table(lines, 2), -1.0: side_table(back, 2)}
     count_x = STEPS * SUB
-    right_z = {
-        1.0: side_table(back[count_x + 1], 0),
-        -1.0: side_table(lines[count_x + 1], 0),
-    }
-
-    angles = table_angles(grid_size)
-    cas = (jnp.cos(angles) + jnp.sin(angles)) / math.sqrt(grid_size)
-    cas_left, cas_right = side_table(cas, 1), side_table(cas, 0)
+
     numbers = wave_numbers(lax.iota(jnp.int32, grid_size), grid_size)
     own_numbers = wave_numbers(place * PLANES + lax.iota(jnp.int32, PLANES), grid_size)
     squares = (own_numbers * own_numbers)[:, None] + (numbers * numbers)[None, :]
@@ -469,8 +554,32 @@
     weight = own_weight / jnp.sum(kpoint_weight).astype(jnp.float32)
     factor = (2.0 * weight * occupied).reshape(1, 1)
 
-    adjoint = move(costate.reshape(natural_shape), regroup)
-    xc_rows = move(xc_kernel, regroup)
+    sent, numbers_full = run(
+        functools.partial(start_kernel, lattice_unit),
+        [(blocks, 3, PLANES * PLANES, ROWS), (ROWS, ROWS)],
+        orbitals.reshape(natural_shape),
+        potential,
+        line_pair,
+    )
+    sent = move(sent, regroup)
+    left_shape = jax.ShapeDtypeStruct((ROWS, 4 * ROWS), jnp.bfloat16)
+    right_shape = jax.ShapeDtypeStruct((4 * ROWS, 2 * ROWS), jnp.bfloat16)
+    made = run(
+        functools.partial(table_kernel, count_x),
+        [left_shape] * (2 * count_x + 2) + [right_shape] * 2,
+        jnp.concatenate([shift_x, shift_yz]),
+        numbers_full,
+        line_pair,
+    )
+    early = (squares, factor, costate[0, 0, 0], costate[0, 0, 1])
+    sent, made, early = lax.optimization_barrier((sent, made, early))
+    squares, factor, costate_real, costate_imag = early
+    tables = {1.0: made[0 : 2 * count_x + 2 : 2], -1.0: made[1 : 2 * count_x + 2 : 2]}
+    right_z = {1.0: made[-2], -1.0: made[-1]}
+
+    def swap_beside(sent, array):
+        sent, array = lax.optimization_barrier((sent, array))
+        return lax.optimization_barrier((swap_field(sent), move(array, regroup)))
 
     def table_x(sign, count):
         return tables[sign][count if sign > 0 else count_x - 1 - count]
@@ -478,32 +587,52 @@
     def table_y(sign):
         return tables[sign][count_x]
 
-    def middle(sign, field, in_rows, count):
+    def middle(sign, field, in_rows, count, pot):
         if in_rows:
-            tabs = (pot_rows, table_y(sign), table_y(sign))
+            tabs = (pot, table_y(sign), table_y(sign))
         else:
-            tabs = (pot_cols, table_x(sign, count - 1), table_x(sign, count))
+            tabs = (pot, table_x(sign, count - 1), table_x(sign, count))
         return run(
             functools.partial(mid_kernel, sign), [sent_shape], field, *tabs, right_z[sign]
         )
 
-    sent = run(
-        functools.partial(start_kernel, 1.0),
-        [sent_shape],
-        orbitals.reshape(natural_shape),
-        potential,
-        table_y(1.0),
-        right_z[1.0],
-    )
-    sent = move(sent, regroup)
     kept = []
     for count in range(1, count_x):
-        field = swap_field(sent)
+        if count == 1:
+            field = exchange(sent.reshape(blocks, 3, PLANES, PLANES, ROWS))
+            pot_sent = sent
+            sent, pot_cols = run(
+                functools.partial(first_mid_kernel, 1.0),
+                [sent_shape, block_shape[:1] + block_shape[2:]],
+                field,
+                table_x(1.0, 0),
+                table_x(1.0, 1),
+                right_z[1.0],
+            )
+            continue
+        if count == 2:
+            field, adjoint_real = swap_beside(sent, costate_real)
+            sent, pot_rows = run(
+                functools.partial(second_mid_kernel, 1.0),
+                [sent_shape, sent_shape[:1] + sent_shape[2:]],
+                field,
+                pot_sent,
+                table_y(1.0),
+                table_y(1.0),
+                right_z[1.0],
+            )
+            continue
+        if count == 3:
+            field, adjoint_imag = swap_beside(sent, costate_imag)
+        elif count == 5:
+            field, xc_rows = swap_beside(sent, xc_kernel)
+        else:
+            field = swap_field(sent)
         in_rows = count % 2 == 0
         if count % SUB == 0:
-            sent, orbital = run(
+            sent, *orbital = run(
                 functools.partial(step_kernel, 1.0),
-                [sent_shape, natural_shape],
+                [sent_shape, real_shape, real_shape],
                 field,
                 pot_rows,
                 table_y(1.0),
@@ -512,14 +641,15 @@
             )
             kept.append(orbital)
         else:
-            sent = middle(1.0, field, in_rows, count)
-    orbital, partial = run(
+            sent = middle(1.0, field, in_rows, count, pot_rows if in_rows else pot_cols)
+    adjoint = [adjoint_real, adjoint_imag]
+    *orbital, partial = run(
         functools.partial(end_kernel, 1.0),
-        [natural_shape, real_shape],
+        [real_shape] * 3,
         swap_field(sent),
         pot_rows,
         table_y(1.0),
-        adjoint,
+        *adjoint,
         factor,
     )
     kept.append(orbital)
@@ -548,8 +678,8 @@
             field,
             density,
             xc_rows,
-            kept[step_index],
-            adjoint,
+            *kept[step_index],
+            *adjoint,
             pot_rows,
             cas_left,
             cas_right,
@@ -558,27 +688,30 @@
         )
         first = (STEPS - 1 - step_index) * SUB
         for count in range(first + 1, first + SUB):
-            sent = middle(-1.0, swap_field(sent), count % 2 == 0, count)
+            in_rows = count % 2 == 0
+            sent = middle(
+                -1.0, swap_field(sent), in_rows, count, pot_rows if in_rows else pot_cols
+            )
         field = swap_field(sent)
         if step_index > 0:
-            adjoint, partial = run(
+            *adjoint, partial = run(
                 functools.partial(end_kernel, -1.0),
-                [natural_shape, real_shape],
+                [real_shape] * 3,
                 field,
                 pot_rows,
                 table_y(-1.0),
-                kept[step_index - 1],
+                *kept[step_index - 1],
                 factor,
             )
         else:
             adjoint = run(
                 functools.partial(final_kernel, -1.0),
-                [natural_shape],
+                [orbitals.shape],
                 field,
                 pot_rows,
                 table_y(-1.0),
             )
-    result = move(adjoint, regroup).reshape(orbitals.shape)
+    result = move(adjoint, regroup)
     beside = lax.ppermute(cross, "ka", [(0, 1), (1, 0)])
     return (result, jnp.where(core == side, cross, beside))
 

time: 606 us -> 562 us (0.927)
  blocking collectives: 229 us -> 296 us
  waiting for transfers between devices: 184 us -> 148 us
  starting transfers between devices: 64 us -> 36.6 us
  local copies, waits for them, and re-layouts: 43.7 us -> 17.2 us
  other arithmetic: 19.2 us -> 1.66 us
    all_to_all x11 -> x17, blocking collectives: 193 us -> 296 us  [exchange(): lax.all_to_all(array, AXES, 0, 0, axis_index_groups=groups, tiled=True)]
    all_to_all x9 -> x3, waiting for transfers between devices: 67.9 us -> 4.83 us  [exchange(): lax.all_to_all(array, AXES, 0, 0, axis_index_groups=groups, tiled=True)]
    all_to_all x1 -> x0, blocking collectives: 36.5 us -> none  [grouped(): got = lax.all_to_all(own, AXES, 0, 0, tiled=True)]
    ppermute x7, waiting for transfers between devices: 114 us -> 141 us  [move(): return lax.ppermute(array, AXES, pairs)]
    all_to_all x9 -> x3, starting transfers between devices: 40.5 us -> 15.5 us  [exchange(): lax.all_to_all(array, AXES, 0, 0, axis_index_groups=groups, tiled=True)]
    unnamed x75 -> x93, local copies, waits for them, and re-layouts: 22 us -> 14 us
    squeeze x4 -> x0, other arithmetic: 8.02 us -> none  [table_x(): return tables[sign][count if sign > 0 else count_x - 1 - count]]
    squeeze x9 -> x1, local copies, waits for them, and re-layouts: 9.75 us -> 2.66 us  [grouped(): early = (squares, factor, costate[0, 0, 0], costate[0, 0, 1])]
  transfers between devices with their start and end apart: 17 -> 11, of which waited for: 14 -> 11; matrix products, arithmetic and copies ran while one was open for 4% -> 1% of each run, Pallas kernels for 0% -> 1%
where the time goes in v3:
time: 562 us; the launch traced here: 552 us
  blocking collectives  296 us (53%)
  waiting for transfers between devices  148 us (26%)
  Pallas kernels  48.9 us (9%)
  starting transfers between devices  36.6 us (7%)
  local copies, waits for them, and re-layouts  17.2 us (3%)
    all_to_all x17, blocking collectives, exchange(): lax.all_to_all(array, AXES, 0, 0, axis_index_groups=groups, tiled=True)  296 us
    ppermute x7, waiting for transfers between devices, move(): return lax.ppermute(array, AXES, pairs)  141 us
    pallas_call x24, Pallas kernels, run(): pl.pallas_call(kernel, out_shape=[jax.ShapeDtypeStruct(out, jnp.float32)...  48.9 us
    ppermute x7, starting transfers between devices, move(): return lax.ppermute(array, AXES, pairs)  21.1 us
    all_to_all x3, starting transfers between devices, exchange(): lax.all_to_all(array, AXES, 0, 0, axis_index_groups=groups, tiled=True)  15.5 us
    unnamed x93, local copies, waits for them, and re-layouts  14 us
  transfers between devices with their start and end apart: 11, of which 11 were waited for; matrix products, arithmetic and copies ran while one was open for 1% of the time, Pallas kernels for 1%

profile of v3, /device:TPU:1, one launch (start us, length us, event | category | flops | bytes accessed | tf_op | source)
XLA Modules:
  0.0 551.6 jit_solution(4886267594625534079)
XLA Ops:
  3.9 3.8 shard_map.122
  7.6 5.6 %collective-permute-start = (f32[16,3,64,128]{3,2,1,0:T(8,128)}, f32[16,3,64,128]{3,2,1,0:T(8,128)S(1)}, u32[]{:S(2)}, u32[]{:S(2)}) collective-permute-start(f32[16,3,64,128]{3,2,1,0:T(8,128)} %get-tuple-element.81), channel_id=1, source_target_pairs={{0,0},{1,1},{2,2},{3,3},{4,4},{5,5},{6,6},{7,7},{8,16},{9,17},{10,... | collective-permute-start | bytes 4718600 | tf_op jit(solution)/shard_map/ppermute | solution.py:523
  16.6 4.4 shard_map.123
  21.3 2.7 slice_bitcast_fusion
  23.9 24.4 %collective-permute-done.pot_field_ref = f32[16,3,64,128]{3,2,1,0:T(8,128)S(1)} collective-permute-done((f32[16,3,64,128]{3,2,1,0:T(8,128)}, f32[16,3,64,128]{3,2,1,0:T(8,128)S(1)}, u32[]{:S(2)}, u32[]{:S(2)}) %collective-permute-start) | collective-permute-done | bytes 1572896 | tf_op jit(solution)/shard_map/ppermute | solution.py:523
  48.5 24.5 %all_to_all.100.field_ref = f32[16,3,8,8,128]{4,3,2,1,0:T(8,128)S(1)} all-to-all(f32[16,3,8,8,128]{4,3,2,1,0:T(8,128)S(1)} %bitcast.28), channel_id=1, replica_groups={{0,1,2,3,4,5,6,7,16,17,18,19,20,21,22,23},{8,9,10,11,12,13,14,15,24,25,..., dimensions={0} | all-to-all | bytes 3145728 | tf_op jit(solution)/shard_map/all_to_all | solution.py:520
  73.0 2.2 shard_map.124
  76.2 4.7 all-to-all-start.1
  80.8 5.3 collective-permute-start.1
  86.1 12.8 %collective-permute-done.1.other_real_ref.adjoint_real_ref = f32[8,128,128]{2,1,0:T(8,128)S(1)} collective-permute-done((f32[8,128,128]{2,1,0:T(8,128)}, f32[8,128,128]{2,1,0:T(8,128)S(1)}, u32[]{:S(2)}, u32[]{:S(2)}) %collective-permute-start.1) | collective-permute-done | bytes 524320 | tf_op jit(solution)/shard_map/ppermute | solution.py:523
  101.2 3.4 shard_map.125
  105.6 6.8 %all-to-all-start.2 = ((f32[16,2,8,8,128]{4,3,2,1,0:T(8,128)}), f32[16,2,8,8,128]{4,3,2,1,0:T(8,128)S(1)}, u32[]{:S(2)}, u32[]{:S(2)}) async-start(f32[16,2,8,8,128]{4,3,2,1,0:T(8,128)} %bitcast.42), calls=%async_computation.2 | async-start | bytes 2097152 | tf_op jit(solution)/shard_map/all_to_all | solution.py:520
  114.4 16.3 %collective-permute-done.2.other_imag_ref.adjoint_imag_ref = f32[8,128,128]{2,1,0:T(8,128)S(1)} collective-permute-done((f32[8,128,128]{2,1,0:T(8,128)}, f32[8,128,128]{2,1,0:T(8,128)S(1)}, u32[]{:S(2)}, u32[]{:S(2)}) %collective-permute-start.2) | collective-permute-done | bytes 524320 | tf_op jit(solution)/shard_map/ppermute | solution.py:523
  134.5 2.2 shard_map.126
  136.7 18.3 %all_to_all.101.field_ref = f32[16,2,8,8,128]{4,3,2,1,0:T(8,128)S(1)} all-to-all(f32[16,2,8,8,128]{4,3,2,1,0:T(8,128)S(1)} %bitcast.31), channel_id=1, replica_groups={{0,1,2,3,4,5,6,7,16,17,18,19,20,21,22,23},{8,9,10,11,12,13,14,15,24,25,..., dimensions={0} | all-to-all | bytes 2097152 | tf_op jit(solution)/shard_map/all_to_all | solution.py:520
  155.0 2.4 shard_map.127
  159.9 4.0 all-to-all-start.4
  163.9 3.9 collective-permute-start.3
  167.8 14.2 %collective-permute-done.3.xc_ref = f32[8,128,128]{2,1,0:T(8,128)S(1)} collective-permute-done((f32[8,128,128]{2,1,0:T(8,128)}, f32[8,128,128]{2,1,0:T(8,128)S(1)}, u32[]{:S(2)}, u32[]{:S(2)}) %collective-permute-start.3) | collective-permute-done | bytes 524320 | tf_op jit(solution)/shard_map/ppermute | solution.py:523
  182.1 2.1 all-to-all-done.4.field_ref
  186.0 2.2 shard_map.128
  188.2 19.3 %all_to_all.102.field_ref = f32[16,2,8,8,128]{4,3,2,1,0:T(8,128)S(1)} all-to-all(f32[16,2,8,8,128]{4,3,2,1,0:T(8,128)S(1)} %bitcast.32), channel_id=1, replica_groups={{0,1,2,3,4,5,6,7,16,17,18,19,20,21,22,23},{8,9,10,11,12,13,14,15,24,25,..., dimensions={0} | all-to-all | bytes 2097152 | tf_op jit(solution)/shard_map/all_to_all | solution.py:520
  207.5 2.2 shard_map.129
  209.8 18.4 %all_to_all.103.field_ref = f32[16,2,8,8,128]{4,3,2,1,0:T(8,128)S(1)} all-to-all(f32[16,2,8,8,128]{4,3,2,1,0:T(8,128)S(1)} %bitcast.36), channel_id=1, replica_groups={{0,1,2,3,4,5,6,7,16,17,18,19,20,21,22,23},{8,9,10,11,12,13,14,15,24,25,..., dimensions={0} | all-to-all | bytes 2097152 | tf_op jit(solution)/shard_map/all_to_all | solution.py:520
  230.3 18.8 %all_to_all.104.field_ref = f32[16,2,8,8,128]{4,3,2,1,0:T(8,128)S(1)} all-to-all(f32[16,2,8,8,128]{4,3,2,1,0:T(8,128)S(1)} %bitcast.30), channel_id=1, replica_groups={{0,1,2,3,4,5,6,7,16,17,18,19,20,21,22,23},{8,9,10,11,12,13,14,15,24,25,..., dimensions={0} | all-to-all | bytes 2097152 | tf_op jit(solution)/shard_map/all_to_all | solution.py:520
  251.2 25.2 %collective-permute-done.4.other_ref = f32[8,128,128]{2,1,0:T(8,128)S(1)} collective-permute-done((f32[8,128,128]{2,1,0:T(8,128)S(1)}, f32[8,128,128]{2,1,0:T(8,128)S(1)}, u32[]{:S(2)}, u32[]{:S(2)}) %collective-permute-start.4) | collective-permute-done | bytes 524320 | tf_op jit(solution)/shard_map/ppermute | solution.py:523
  277.1 12.3 %all_to_all.105.field_ref = f32[16,8,8,128]{3,2,1,0:T(8,128)S(1)} all-to-all(f32[16,8,8,128]{3,2,1,0:T(8,128)S(1)} %bitcast.47), channel_id=1, replica_groups={{0,1,2,3,4,5,6,7,16,17,18,19,20,21,22,23},{8,9,10,11,12,13,14,15,24,25,..., dimensions={0} | all-to-all | bytes 1048576 | tf_op jit(solution)/shard_map/all_to_all | solution.py:520
  289.9 12.7 %all_to_all.106 = f32[16,8,8,128]{3,2,1,0:T(8,128)S(1)} all-to-all(f32[16,8,8,128]{3,2,1,0:T(8,128)S(1)} %shard_map.133), channel_id=1, replica_groups={{0,1,2,3,4,5,6,7,16,17,18,19,20,21,22,23},{8,9,10,11,12,13,14,15,24,25,..., dimensions={0} | all-to-all | bytes 1048576 | tf_op jit(solution)/shard_map/all_to_all | solution.py:520
  302.6 2.5 shard_map.134
  305.1 18.4 %all_to_all.107.field_ref = f32[16,2,8,8,128]{4,3,2,1,0:T(8,128)S(1)} all-to-all(f32[16,2,8,8,128]{4,3,2,1,0:T(8,128)S(1)} %bitcast.45), channel_id=1, replica_groups={{0,1,2,3,4,5,6,7,16,17,18,19,20,21,22,23},{8,9,10,11,12,13,14,15,24,25,..., dimensions={0} | all-to-all | bytes 2097152 | tf_op jit(solution)/shard_map/all_to_all | solution.py:520
  323.6 2.1 shard_map.135
  325.7 18.3 %all_to_all.108.field_ref = f32[16,2,8,8,128]{4,3,2,1,0:T(8,128)S(1)} all-to-all(f32[16,2,8,8,128]{4,3,2,1,0:T(8,128)S(1)} %bitcast.33), channel_id=1, replica_groups={{0,1,2,3,4,5,6,7,16,17,18,19,20,21,22,23},{8,9,10,11,12,13,14,15,24,25,..., dimensions={0} | all-to-all | bytes 2097152 | tf_op jit(solution)/shard_map/all_to_all | solution.py:520
  344.0 2.2 shard_map.136
  346.2 18.4 %all_to_all.109.field_ref = f32[16,2,8,8,128]{4,3,2,1,0:T(8,128)S(1)} all-to-all(f32[16,2,8,8,128]{4,3,2,1,0:T(8,128)S(1)} %bitcast.37), channel_id=1, replica_groups={{0,1,2,3,4,5,6,7,16,17,18,19,20,21,22,23},{8,9,10,11,12,13,14,15,24,25,..., dimensions={0} | all-to-all | bytes 2097152 | tf_op jit(solution)/shard_map/all_to_all | solution.py:520
  364.6 2.1 shard_map.137
  366.7 18.6 %all_to_all.110.field_ref = f32[16,2,8,8,128]{4,3,2,1,0:T(8,128)S(1)} all-to-all(f32[16,2,8,8,128]{4,3,2,1,0:T(8,128)S(1)} %bitcast.34), channel_id=1, replica_groups={{0,1,2,3,4,5,6,7,16,17,18,19,20,21,22,23},{8,9,10,11,12,13,14,15,24,25,..., dimensions={0} | all-to-all | bytes 2097152 | tf_op jit(solution)/shard_map/all_to_all | solution.py:520
  387.2 25.4 %collective-permute-done.5.other_ref = f32[8,128,128]{2,1,0:T(8,128)S(1)} collective-permute-done((f32[8,128,128]{2,1,0:T(8,128)S(1)}, f32[8,128,128]{2,1,0:T(8,128)S(1)}, u32[]{:S(2)}, u32[]{:S(2)}) %collective-permute-start.5) | collective-permute-done | bytes 524320 | tf_op jit(solution)/shard_map/ppermute | solution.py:523
  413.2 12.3 %all_to_all.111.field_ref = f32[16,8,8,128]{3,2,1,0:T(8,128)S(1)} all-to-all(f32[16,8,8,128]{3,2,1,0:T(8,128)S(1)} %bitcast.48), channel_id=1, replica_groups={{0,1,2,3,4,5,6,7,16,17,18,19,20,21,22,23},{8,9,10,11,12,13,14,15,24,25,..., dimensions={0} | all-to-all | bytes 1048576 | tf_op jit(solution)/shard_map/all_to_all | solution.py:520
  426.1 12.7 %all_to_all.112 = f32[16,8,8,128]{3,2,1,0:T(8,128)S(1)} all-to-all(f32[16,8,8,128]{3,2,1,0:T(8,128)S(1)} %shard_map.140), channel_id=1, replica_groups={{0,1,2,3,4,5,6,7,16,17,18,19,20,21,22,23},{8,9,10,11,12,13,14,15,24,25,..., dimensions={0} | all-to-all | bytes 1048576 | tf_op jit(solution)/shard_map/all_to_all | solution.py:520
  438.7 2.5 shard_map.141
  441.3 18.4 %all_to_all.113.field_ref = f32[16,2,8,8,128]{4,3,2,1,0:T(8,128)S(1)} all-to-all(f32[16,2,8,8,128]{4,3,2,1,0:T(8,128)S(1)} %bitcast.44), channel_id=1, replica_groups={{0,1,2,3,4,5,6,7,16,17,18,19,20,21,22,23},{8,9,10,11,12,13,14,15,24,25,..., dimensions={0} | all-to-all | bytes 2097152 | tf_op jit(solution)/shard_map/all_to_all | solution.py:520
  461.9 18.3 %all_to_all.114.field_ref = f32[16,2,8,8,128]{4,3,2,1,0:T(8,128)S(1)} all-to-all(f32[16,2,8,8,128]{4,3,2,1,0:T(8,128)S(1)} %bitcast.35), channel_id=1, replica_groups={{0,1,2,3,4,5,6,7,16,17,18,19,20,21,22,23},{8,9,10,11,12,13,14,15,24,25,..., dimensions={0} | all-to-all | bytes 2097152 | tf_op jit(solution)/shard_map/all_to_all | solution.py:520
  480.1 2.2 shard_map.143
  482.3 18.4 %all_to_all.115.field_ref = f32[16,2,8,8,128]{4,3,2,1,0:T(8,128)S(1)} all-to-all(f32[16,2,8,8,128]{4,3,2,1,0:T(8,128)S(1)} %bitcast.38), channel_id=1, replica_groups={{0,1,2,3,4,5,6,7,16,17,18,19,20,21,22,23},{8,9,10,11,12,13,14,15,24,25,..., dimensions={0} | all-to-all | bytes 2097152 | tf_op jit(solution)/shard_map/all_to_all | solution.py:520
  500.7 2.2 shard_map.144
  502.9 18.2 %all_to_all.116.field_ref = f32[16,2,8,8,128]{4,3,2,1,0:T(8,128)S(1)} all-to-all(f32[16,2,8,8,128]{4,3,2,1,0:T(8,128)S(1)} %bitcast.29), channel_id=1, replica_groups={{0,1,2,3,4,5,6,7,16,17,18,19,20,21,22,23},{8,9,10,11,12,13,14,15,24,25,..., dimensions={0} | all-to-all | bytes 2097152 | tf_op jit(solution)/shard_map/all_to_all | solution.py:520
  522.3 2.8 collective-permute-start.6
  527.9 22.6 %collective-permute-done.6 = f32[1,1,2,8,128,128]{5,4,3,2,1,0:T(8,128)S(1)} collective-permute-done((f32[1,1,2,8,128,128]{5,4,3,2,1,0:T(8,128)S(1)}, f32[1,1,2,8,128,128]{5,4,3,2,1,0:T(8,128)S(1)}, u32[]{:S(2)}, u32[]{:S(2)}) %collective-permute-start.6) | collective-permute-done | bytes 1048608 | tf_op jit(solution)/shard_map/ppermute | solution.py:523
  (117 shorter events, 34.7 us)
Async XLA Ops:
  0.6 15.9 %copy-start.45 = (f32[2]{0:T(128)S(1)}, f32[2]{0:T(128)}, u32[]{:S(2)}) copy-start(f32[2]{0:T(128)} %constant.71.clone) | copy-start | bytes 28
  0.6 13.3 %copy-start.43 = (s32[2]{0:T(128)S(1)}, s32[2]{0:T(128)}, u32[]{:S(2)}) copy-start(s32[2]{0:T(128)} %param.16) | copy-start | bytes 28
  0.7 15.8 %copy-start.44 = (f32[8]{0:T(128)S(1)}, f32[8]{0:T(128)}, u32[]{:S(2)}) copy-start(f32[8]{0:T(128)} %param.15) | copy-start | bytes 100
  0.7 1.2 copy-start.13
  1.9 1.0 copy-start.14
  3.9 12.7 %copy-start.16 = (f32[128,256]{1,0:T(8,128)S(1)}, f32[128,256]{1,0:T(8,128)}, u32[]{:S(2)}) copy-start(f32[128,256]{1,0:T(8,128)} %constant.68.clone.lines_ref) | copy-start | bytes 393220
  7.6 40.8 %collective-permute-start = (f32[16,3,64,128]{3,2,1,0:T(8,128)}, f32[16,3,64,128]{3,2,1,0:T(8,128)S(1)}, u32[]{:S(2)}, u32[]{:S(2)}) collective-permute-start(f32[16,3,64,128]{3,2,1,0:T(8,128)} %get-tuple-element.81), channel_id=1, source_target_pairs={{0,0},{1,1},{2,2},{3,3},{4,4},{5,5},{6,6},{7,7},{8,16},{9,17},{10,... | collective-permute-start | bytes 4718600 | tf_op jit(solution)/shard_map/ppermute | solution.py:523
  21.0 27.3 %copy-start.23 = (bf16[128,512]{1,0:T(8,128)(2,1)}, bf16[128,512]{1,0:T(8,128)(2,1)S(1)}, u32[]{:S(2)}) copy-start(bf16[128,512]{1,0:T(8,128)(2,1)S(1)} %get-tuple-element.155.first_ref) | copy-start | bytes 393220
  21.1 27.3 %copy-start.25 = (bf16[128,512]{1,0:T(8,128)(2,1)}, bf16[128,512]{1,0:T(8,128)(2,1)S(1)}, u32[]{:S(2)}) copy-start(bf16[128,512]{1,0:T(8,128)(2,1)S(1)} %get-tuple-element.145.first_ref) | copy-start | bytes 393220
  21.1 27.3 %copy-start.27 = (bf16[128,512]{1,0:T(8,128)(2,1)}, bf16[128,512]{1,0:T(8,128)(2,1)S(1)}, u32[]{:S(2)}) copy-start(bf16[128,512]{1,0:T(8,128)(2,1)S(1)} %get-tuple-element.144.second_ref) | copy-start | bytes 393220
  21.1 27.3 %copy-start.29 = (bf16[128,512]{1,0:T(8,128)(2,1)}, bf16[128,512]{1,0:T(8,128)(2,1)S(1)}, u32[]{:S(2)}) copy-start(bf16[128,512]{1,0:T(8,128)(2,1)S(1)} %get-tuple-element.143.first_ref) | copy-start | bytes 393220
  21.1 27.3 %copy-start.31 = (bf16[128,512]{1,0:T(8,128)(2,1)}, bf16[128,512]{1,0:T(8,128)(2,1)S(1)}, u32[]{:S(2)}) copy-start(bf16[128,512]{1,0:T(8,128)(2,1)S(1)} %get-tuple-element.128.first_ref) | copy-start | bytes 393220
  21.1 27.3 %copy-start.33 = (bf16[128,512]{1,0:T(8,128)(2,1)}, bf16[128,512]{1,0:T(8,128)(2,1)S(1)}, u32[]{:S(2)}) copy-start(bf16[128,512]{1,0:T(8,128)(2,1)S(1)} %get-tuple-element.129.second_ref) | copy-start | bytes 393220
  21.1 27.3 %copy-start.35 = (bf16[128,512]{1,0:T(8,128)(2,1)}, bf16[128,512]{1,0:T(8,128)(2,1)S(1)}, u32[]{:S(2)}) copy-start(bf16[128,512]{1,0:T(8,128)(2,1)S(1)} %get-tuple-element.126.first_ref) | copy-start | bytes 393220
  21.1 27.3 %copy-start.37 = (bf16[128,512]{1,0:T(8,128)(2,1)}, bf16[128,512]{1,0:T(8,128)(2,1)S(1)}, u32[]{:S(2)}) copy-start(bf16[128,512]{1,0:T(8,128)(2,1)S(1)} %get-tuple-element.127.second_ref) | copy-start | bytes 393220
  21.1 27.3 %copy-start.39 = (bf16[128,512]{1,0:T(8,128)(2,1)}, bf16[128,512]{1,0:T(8,128)(2,1)S(1)}, u32[]{:S(2)}) copy-start(bf16[128,512]{1,0:T(8,128)(2,1)S(1)} %get-tuple-element.119.first_ref) | copy-start | bytes 393220
  21.1 27.3 %copy-start.17 = (bf16[128,512]{1,0:T(8,128)(2,1)}, bf16[128,512]{1,0:T(8,128)(2,1)S(1)}, u32[]{:S(2)}) copy-start(bf16[128,512]{1,0:T(8,128)(2,1)S(1)} %get-tuple-element.158.second_ref) | copy-start | bytes 393220
  21.1 27.3 %copy-start.19 = (bf16[128,512]{1,0:T(8,128)(2,1)}, bf16[128,512]{1,0:T(8,128)(2,1)S(1)}, u32[]{:S(2)}) copy-start(bf16[128,512]{1,0:T(8,128)(2,1)S(1)} %get-tuple-element.157.first_ref) | copy-start | bytes 393220
  21.2 27.3 %copy-start.41 = (bf16[128,512]{1,0:T(8,128)(2,1)}, bf16[128,512]{1,0:T(8,128)(2,1)S(1)}, u32[]{:S(2)}) copy-start(bf16[128,512]{1,0:T(8,128)(2,1)S(1)} %get-tuple-element.120.second_ref) | copy-start | bytes 393220
  21.2 51.8 %copy-start.21 = (bf16[128,512]{1,0:T(8,128)(2,1)}, bf16[128,512]{1,0:T(8,128)(2,1)S(1)}, u32[]{:S(2)}) copy-start(bf16[128,512]{1,0:T(8,128)(2,1)S(1)} %get-tuple-element.156.second_ref) | copy-start | bytes 393220
  75.2 1.0 copy-start.10
  76.2 25.1 %all-to-all-start.1 = ((f32[16,2,8,8,128]{4,3,2,1,0:T(8,128)}), f32[16,2,8,8,128]{4,3,2,1,0:T(8,128)}, u32[]{:S(2)}, u32[]{:S(2)}) async-start(f32[16,2,8,8,128]{4,3,2,1,0:T(8,128)} %bitcast.41), calls=%async_computation.1 | async-start | bytes 2097152 | tf_op jit(solution)/shard_map/all_to_all | solution.py:520
  80.8 18.1 %collective-permute-start.1 = (f32[8,128,128]{2,1,0:T(8,128)}, f32[8,128,128]{2,1,0:T(8,128)S(1)}, u32[]{:S(2)}, u32[]{:S(2)}) collective-permute-start(f32[8,128,128]{2,1,0:T(8,128)} %get-tuple-element.110), channel_id=1, source_target_pairs={{0,0},{1,1},{2,2},{3,3},{4,4},{5,5},{6,6},{7,7},{8,16},{9,17},{10,... | collective-permute-start | bytes 1572872 | tf_op jit(solution)/shard_map/ppermute | solution.py:523
  104.7 1.0 copy-start.11
  105.6 27.1 %all-to-all-start.2 = ((f32[16,2,8,8,128]{4,3,2,1,0:T(8,128)}), f32[16,2,8,8,128]{4,3,2,1,0:T(8,128)S(1)}, u32[]{:S(2)}, u32[]{:S(2)}) async-start(f32[16,2,8,8,128]{4,3,2,1,0:T(8,128)} %bitcast.42), calls=%async_computation.2 | async-start | bytes 2097152 | tf_op jit(solution)/shard_map/all_to_all | solution.py:520
  112.4 18.3 %collective-permute-start.2 = (f32[8,128,128]{2,1,0:T(8,128)}, f32[8,128,128]{2,1,0:T(8,128)S(1)}, u32[]{:S(2)}, u32[]{:S(2)}) collective-permute-start(f32[8,128,128]{2,1,0:T(8,128)} %get-tuple-element.116), channel_id=1, source_target_pairs={{0,0},{1,1},{2,2},{3,3},{4,4},{5,5},{6,6},{7,7},{8,16},{9,17},{10,... | collective-permute-start | bytes 1572872 | tf_op jit(solution)/shard_map/ppermute | solution.py:523
  158.9 1.0 copy-start.12
  159.9 24.3 %all-to-all-start.4 = ((f32[16,2,8,8,128]{4,3,2,1,0:T(8,128)}), f32[16,2,8,8,128]{4,3,2,1,0:T(8,128)S(1)}, u32[]{:S(2)}, u32[]{:S(2)}) async-start(f32[16,2,8,8,128]{4,3,2,1,0:T(8,128)} %bitcast.43), calls=%async_computation.4 | async-start | bytes 2097152 | tf_op jit(solution)/shard_map/all_to_all | solution.py:520
  163.9 18.1 %collective-permute-start.3 = (f32[8,128,128]{2,1,0:T(8,128)}, f32[8,128,128]{2,1,0:T(8,128)S(1)}, u32[]{:S(2)}, u32[]{:S(2)}) collective-permute-start(f32[8,128,128]{2,1,0:T(8,128)} %param.14), channel_id=1, source_target_pairs={{0,0},{1,1},{2,2},{3,3},{4,4},{5,5},{6,6},{7,7},{8,16},{9,17},{10,... | collective-permute-start | bytes 1572872 | tf_op jit(solution)/shard_map/ppermute | solution.py:523
  209.7 18.4 %copy-start.32 = (bf16[128,512]{1,0:T(8,128)(2,1)S(1)}, bf16[128,512]{1,0:T(8,128)(2,1)}, u32[]{:S(2)}) copy-start(bf16[128,512]{1,0:T(8,128)(2,1)} %copy-done.31) | copy-start | bytes 393220
  209.7 18.4 %copy-start.34 = (bf16[128,512]{1,0:T(8,128)(2,1)S(1)}, bf16[128,512]{1,0:T(8,128)(2,1)}, u32[]{:S(2)}) copy-start(bf16[128,512]{1,0:T(8,128)(2,1)} %copy-done.33) | copy-start | bytes 393220
  230.3 18.8 %copy-start.6 = (f32[8,128,128]{2,1,0:T(8,128)S(1)}, f32[8,128,128]{2,1,0:T(8,128)}, u32[]{:S(2)}) copy-start(f32[8,128,128]{2,1,0:T(8,128)} %copy-done.5) | copy-start | bytes 1572868
  230.3 18.8 %copy-start.8 = (f32[8,128,128]{2,1,0:T(8,128)S(1)}, f32[8,128,128]{2,1,0:T(8,128)}, u32[]{:S(2)}) copy-start(f32[8,128,128]{2,1,0:T(8,128)} %copy-done.7) | copy-start | bytes 1572868
  249.1 27.3 %copy-start = (bf16[128,256]{1,0:T(8,128)(2,1)S(1)}, bf16[128,256]{1,0:T(8,128)(2,1)}, u32[]{:S(2)}) copy-start(bf16[128,256]{1,0:T(8,128)(2,1)} %constant.69.clone.left_ref.cas_left_ref) | copy-start | bytes 196612
  249.1 27.3 %copy-start.9 = (bf16[256,128]{1,0:T(8,128)(2,1)S(1)}, bf16[256,128]{1,0:T(8,128)(2,1)}, u32[]{:S(2)}) copy-start(bf16[256,128]{1,0:T(8,128)(2,1)} %constant.70.clone.right_ref.cas_right_ref) | copy-start | bytes 196612
  250.4 26.0 %collective-permute-start.4 = (f32[8,128,128]{2,1,0:T(8,128)S(1)}, f32[8,128,128]{2,1,0:T(8,128)S(1)}, u32[]{:S(2)}, u32[]{:S(2)}) collective-permute-start(f32[8,128,128]{2,1,0:T(8,128)S(1)} %get-tuple-element.133.own_ref), channel_id=1, source_target_pairs={{0,8},{1,9},{2,10},{3,11},{4,12},{5,13},{6,14},{7,15},{8,0},{9,1},... | collective-permute-start | bytes 1572872 | tf_op jit(solution)/shard_map/ppermute | solution.py:523
  305.1 18.5 %copy-start.28 = (bf16[128,512]{1,0:T(8,128)(2,1)S(1)}, bf16[128,512]{1,0:T(8,128)(2,1)}, u32[]{:S(2)}) copy-start(bf16[128,512]{1,0:T(8,128)(2,1)} %copy-done.27) | copy-start | bytes 393220
  305.1 18.4 %copy-start.30 = (bf16[128,512]{1,0:T(8,128)(2,1)S(1)}, bf16[128,512]{1,0:T(8,128)(2,1)}, u32[]{:S(2)}) copy-start(bf16[128,512]{1,0:T(8,128)(2,1)} %copy-done.29) | copy-start | bytes 393220
  346.2 18.4 %copy-start.26 = (bf16[128,512]{1,0:T(8,128)(2,1)S(1)}, bf16[128,512]{1,0:T(8,128)(2,1)}, u32[]{:S(2)}) copy-start(bf16[128,512]{1,0:T(8,128)(2,1)} %copy-done.25) | copy-start | bytes 393220
  366.7 18.6 %copy-start.2 = (f32[8,128,128]{2,1,0:T(8,128)S(1)}, f32[8,128,128]{2,1,0:T(8,128)}, u32[]{:S(2)}) copy-start(f32[8,128,128]{2,1,0:T(8,128)} %copy-done.1) | copy-start | bytes 1572868
  366.7 18.6 %copy-start.4 = (f32[8,128,128]{2,1,0:T(8,128)S(1)}, f32[8,128,128]{2,1,0:T(8,128)}, u32[]{:S(2)}) copy-start(f32[8,128,128]{2,1,0:T(8,128)} %copy-done.3) | copy-start | bytes 1572868
  386.5 26.0 %collective-permute-start.5 = (f32[8,128,128]{2,1,0:T(8,128)S(1)}, f32[8,128,128]{2,1,0:T(8,128)S(1)}, u32[]{:S(2)}, u32[]{:S(2)}) collective-permute-start(f32[8,128,128]{2,1,0:T(8,128)S(1)} %get-tuple-element.149.own_ref), channel_id=1, source_target_pairs={{0,8},{1,9},{2,10},{3,11},{4,12},{5,13},{6,14},{7,15},{8,0},{9,1},... | collective-permute-start | bytes 1572872 | tf_op jit(solution)/shard_map/ppermute | solution.py:523
  441.3 18.5 %copy-start.22 = (bf16[128,512]{1,0:T(8,128)(2,1)S(1)}, bf16[128,512]{1,0:T(8,128)(2,1)}, u32[]{:S(2)}) copy-start(bf16[128,512]{1,0:T(8,128)(2,1)} %copy-done.21) | copy-start | bytes 393220
  441.3 18.4 %copy-start.24 = (bf16[128,512]{1,0:T(8,128)(2,1)S(1)}, bf16[128,512]{1,0:T(8,128)(2,1)}, u32[]{:S(2)}) copy-start(bf16[128,512]{1,0:T(8,128)(2,1)} %copy-done.23) | copy-start | bytes 393220
  482.3 18.4 %copy-start.18 = (bf16[128,512]{1,0:T(8,128)(2,1)S(1)}, bf16[128,512]{1,0:T(8,128)(2,1)}, u32[]{:S(2)}) copy-start(bf16[128,512]{1,0:T(8,128)(2,1)} %copy-done.17) | copy-start | bytes 393220
  482.3 18.4 %copy-start.20 = (bf16[128,512]{1,0:T(8,128)(2,1)S(1)}, bf16[128,512]{1,0:T(8,128)(2,1)}, u32[]{:S(2)}) copy-start(bf16[128,512]{1,0:T(8,128)(2,1)} %copy-done.19) | copy-start | bytes 393220
  522.3 28.2 %collective-permute-start.6 = (f32[1,1,2,8,128,128]{5,4,3,2,1,0:T(8,128)S(1)}, f32[1,1,2,8,128,128]{5,4,3,2,1,0:T(8,128)S(1)}, u32[]{:S(2)}, u32[]{:S(2)}) collective-permute-start(f32[1,1,2,8,128,128]{5,4,3,2,1,0:T(8,128)S(1)} %shard_map.145), channel_id=1, source_target_pairs={{0,0},{1,1},{2,2},{3,3},{4,4},{5,5},{6,6},{7,7},{8,16},{9,17},{10,... | collective-permute-start | bytes 3145736 | tf_op jit(solution)/shard_map/ppermute | solution.py:523
  525.1 2.0 collective-permute-start.7
  (9 other events, 7.7 us)

commit v4 on v3

--- a/solution.py
+++ b/solution.py
@@ -160,6 +160,7 @@
 
 ROWS = 128
 PLANES = 8
+QUARTER = 4
 AXES = ("ka", "fft")
 
 
@@ -236,25 +237,39 @@
 
 def cos_sin(angle):
     square = angle * angle
-    cosine, sine = jnp.full_like(angle, 1.0), jnp.full_like(angle, 1.0)
-    for order in range(12, 0, -2):
-        cosine = 1.0 - cosine * square * (1.0 / (order * (order - 1)))
-        sine = 1.0 - sine * square * (1.0 / (order * (order + 1)))
+    cosine = sine = 1.0
+    for order in range(10, 0, -2):
+        cosine = 1.0 - cosine * (square * (1.0 / (order * (order - 1))))
+        sine = 1.0 - sine * (square * (1.0 / (order * (order + 1))))
     return cosine, sine * angle
 
 
-def rotated(real_part, imag_part, cosine, sine):
-    return real_part * cosine + imag_part * sine, imag_part * cosine - real_part * sine
-
-
-def gather_planes(ref):
+def rotated(sign, real_part, imag_part, cosine, sine):
+    if sign > 0:
+        return real_part * cosine + imag_part * sine, imag_part * cosine - real_part * sine
+    return real_part * cosine - imag_part * sine, imag_part * cosine + real_part * sine
+
+
+def doubled(cosine, sine):
+    return 1.0 - 2.0 * (sine * sine), 2.0 * sine * cosine
+
+
+def place_of(block, blocks):
+    core, rest = divmod(block, blocks // 2)
+    return rest // 2 * 4 + core * 2 + rest % 2
+
+
+def gathered(ref, *index):
     blocks = ref.shape[0]
     return jnp.concatenate(
+        [ref[(place_of(block, blocks),) + index] for block in range(blocks)], axis=0
+    )
+
+
+def gather_planes(ref):
+    return jnp.concatenate(
         [
-            jnp.concatenate(
-                [ref[:, part, plane].reshape(blocks * PLANES, ROWS) for plane in range(PLANES)],
-                axis=1,
-            )
+            jnp.concatenate([gathered(ref, part, plane) for plane in range(PLANES)], axis=1)
             for part in range(2)
         ],
         axis=0,
@@ -265,30 +280,33 @@
     return jnp.concatenate([ref[plane] for plane in range(PLANES)], axis=1)
 
 
-def strided(ref, plane):
-    return jnp.concatenate(
-        [ref[block, pl.ds(plane, PLANES, stride=PLANES), :] for block in range(ref.shape[0])],
-        axis=0,
-    )
-
-
-def angles_of(ref):
-    if len(ref.shape) == 3:
-        return jnp.concatenate([strided(ref, plane) for plane in range(PLANES)], axis=1)
-    if ref.shape[2] == PLANES * PLANES:
-        return angles_of(ref.at[:, 2])
-    if len(ref.shape) == 5:
-        return angles_of(ref.at[:, 2])
-    return jnp.concatenate(
-        [ref[:, plane].reshape(ROWS, ROWS) for plane in range(PLANES)], axis=1
-    )
-
-
 def lane(value, plane):
     return value[:, plane * ROWS : (plane + 1) * ROWS]
 
 
-def scatter_planes(real_part, imag_part, table, out_ref):
+def sources_of(blocks):
+    half = blocks // 2
+    return [
+        block // half * blocks + place_of(core * half + block % half, blocks)
+        for block in range(blocks)
+        for core in range(2)
+    ]
+
+
+def rows_to(out_ref, block, index, plane, piece):
+    if not isinstance(out_ref, tuple):
+        place = place_of(block, out_ref.shape[0])
+        out_ref[(place,) + index + (pl.ds(plane, PLANES, stride=PLANES), slice(None))] = piece
+        return
+    sources = sources_of(out_ref[0].shape[0] // 2)
+    for core in range(2):
+        at = (sources[2 * block + core],) + index
+        out_ref[0][at + (pl.ds(plane, QUARTER, stride=PLANES), slice(None))] = piece[
+            core * QUARTER : (core + 1) * QUARTER
+        ]
+
+
+def turn_z(real_part, imag_part, table):
     rows = jnp.concatenate(
         [
             jnp.concatenate([lane(real_part, plane), lane(imag_part, plane)], axis=1)
@@ -296,34 +314,86 @@
         ],
         axis=0,
     )
-    turned = from_right(rows, table)
+    return from_right(rows, table)
+
+
+def scatter_planes(real_part, imag_part, table, out_ref):
+    blocks = ROWS // PLANES
+    turned = turn_z(real_part, imag_part, table)
     for plane in range(PLANES):
         for part in range(2):
             piece = turned[plane * ROWS : (plane + 1) * ROWS, part * ROWS : (part + 1) * ROWS]
-            for block in range(out_ref.shape[0]):
-                out_ref[block, part, pl.ds(plane, PLANES, stride=PLANES), :] = piece[
-                    block * PLANES : (block + 1) * PLANES
-                ]
-
-
-def mid_kernel(sign, field_ref, pot_ref, first_ref, second_ref, right_ref, out_ref):
-    field = from_left(whole_left(first_ref[...]), gather_planes(field_ref))
-    cosine, sine = cos_sin(sign * sub_time * angles_of(pot_ref))
-    real_part, imag_part = rotated(field[:ROWS], field[ROWS:], cosine, sine)
-    field = from_left(whole_left(second_ref[...]), jnp.concatenate([real_part, imag_part], axis=0))
+            for block in range(blocks):
+                rows_of = piece[block * PLANES : (block + 1) * PLANES]
+                rows_to(out_ref, block, (part,), plane, rows_of)
+
+
+def between(sign, field, cosine, sine, first_ref, second_ref, right_ref, out_ref):
+    field = from_left(whole_left(first_ref[...]), field)
+    real_part, imag_part = rotated(sign, field[:ROWS], field[ROWS:], *doubled(cosine, sine))
+    field = from_left(
+        whole_left(second_ref[...]), jnp.concatenate([real_part, imag_part], axis=0)
+    )
     scatter_planes(field[:ROWS], field[ROWS:], right_ref[...], out_ref)
 
 
-def first_mid_kernel(sign, field_ref, first_ref, second_ref, right_ref, out_ref, pot_ref):
-    mid_kernel(sign, field_ref, field_ref, first_ref, second_ref, right_ref, out_ref)
-    pot_ref[...] = field_ref[:, 2]
+def mid_kernel(
+    sign, field_ref, cosine_ref, sine_ref, first_ref, second_ref, right_ref, out_ref
+):
+    cosine, sine = natural(cosine_ref), natural(sine_ref)
+    field = gather_planes(field_ref)
+    between(sign, field, cosine, sine, first_ref, second_ref, right_ref, out_ref)
+
+
+def first_mid_kernel(
+    sign, field_ref, first_ref, second_ref, right_ref, out_ref, cosine_ref, sine_ref
+):
+    blocks = field_ref.shape[0] // 2
+
+    def part_of(part):
+        return jnp.concatenate(
+            [
+                jnp.concatenate(
+                    [
+                        field_ref[source, part, pl.ds(plane * QUARTER, QUARTER), :]
+                        for source in sources_of(blocks)
+                    ],
+                    axis=0,
+                )
+                for plane in range(PLANES)
+            ],
+            axis=1,
+        )
+
+    pot = part_of(2)
+    for plane in range(PLANES):
+        for block in range(blocks):
+            rows_of = lane(pot, plane)[block * PLANES : (block + 1) * PLANES]
+            rows_to(out_ref, block, (2,), plane, rows_of)
+    cosine, sine = cos_sin(0.5 * sub_time * pot)
+    store_natural(cosine_ref, cosine)
+    store_natural(sine_ref, sine)
+    field = jnp.concatenate([part_of(0), part_of(1)], axis=0)
+    between(sign, field, cosine, sine, first_ref, second_ref, right_ref, out_ref)
 
 
 def second_mid_kernel(
-    sign, field_ref, pot_field_ref, first_ref, second_ref, right_ref, out_ref, pot_ref
+    sign, field_ref, first_ref, second_ref, right_ref, out_ref, cosine_ref, sine_ref
 ):
-    mid_kernel(sign, field_ref, pot_field_ref, first_ref, second_ref, right_ref, out_ref)
-    pot_ref[...] = pot_field_ref[:, 2]
+    pot = jnp.concatenate([gathered(field_ref, 2, plane) for plane in range(PLANES)], axis=1)
+    cosine, sine = cos_sin(0.5 * sub_time * pot)
+    store_natural(cosine_ref, cosine)
+    store_natural(sine_ref, sine)
+    field = gather_planes(field_ref)
+    between(sign, field, cosine, sine, first_ref, second_ref, right_ref, out_ref)
+
+
+def last_mid_kernel(
+    sign, field_ref, cosine_ref, sine_ref, first_ref, second_ref, right_ref, out_ref
+):
+    cosine, sine = natural(cosine_ref), natural(sine_ref)
+    field = gather_planes(field_ref)
+    between(sign, field, cosine, sine, first_ref, second_ref, right_ref, (out_ref,))
 
 
 def store_natural(ref, value):
@@ -331,54 +401,107 @@
         ref[plane] = lane(value, plane)
 
 
-def step_kernel(
-    sign, field_ref, pot_ref, first_ref, second_ref, right_ref, out_ref, real_ref, imag_ref
-):
+def finish(sign, field_ref, cosine, sine, first_ref, real_ref, imag_ref):
     field = from_left(whole_left(first_ref[...]), gather_planes(field_ref))
-    cosine, sine = cos_sin(sign * 0.5 * sub_time * angles_of(pot_ref))
-    real_part, imag_part = rotated(field[:ROWS], field[ROWS:], cosine, sine)
+    real_part, imag_part = rotated(sign, field[:ROWS], field[ROWS:], cosine, sine)
     store_natural(real_ref, real_part)
     store_natural(imag_ref, imag_part)
-    real_part, imag_part = rotated(real_part, imag_part, cosine, sine)
-    field = from_left(whole_left(second_ref[...]), jnp.concatenate([real_part, imag_part], axis=0))
-    scatter_planes(field[:ROWS], field[ROWS:], right_ref[...], out_ref)
+    return real_part, imag_part
+
+
+def begin(sign, real_part, imag_part, cosine, sine, second, right, out_ref):
+    real_part, imag_part = rotated(sign, real_part, imag_part, cosine, sine)
+    field = from_left(second, jnp.concatenate([real_part, imag_part], axis=0))
+    scatter_planes(field[:ROWS], field[ROWS:], right, out_ref)
+
+
+def step_kernel(
+    sign,
+    field_ref,
+    cosine_ref,
+    sine_ref,
+    first_ref,
+    second_ref,
+    right_ref,
+    out_ref,
+    real_ref,
+    imag_ref,
+):
+    cosine, sine = natural(cosine_ref), natural(sine_ref)
+    parts = finish(sign, field_ref, cosine, sine, first_ref, real_ref, imag_ref)
+    begin(sign, *parts, cosine, sine, whole_left(second_ref[...]), right_ref[...], out_ref)
+
+
+def plane_order(core):
+    return [core * QUARTER + number for number in range(QUARTER)] + [
+        (1 - core) * QUARTER + number for number in range(QUARTER)
+    ]
 
 
 def start_kernel(
-    unit, field_ref, pot_ref, lines_ref, out_ref, numbers_ref
+    unit, field_ref, pot_ref, lines_ref, keep_ref, give_ref, numbers_ref, field, pot, lines, sems
 ):
-    cosine_line, sine_line = lines_ref[:, :ROWS], lines_ref[:, ROWS:]
+    copies = [
+        pltpu.make_async_copy(source, target, sems.at[number])
+        for number, (source, target) in enumerate(
+            ((lines_ref, lines), (pot_ref, pot), (field_ref, field))
+        )
+    ]
+    for copy in copies:
+        copy.start()
+    order = plane_order(lax.axis_index("ka"))
     index = lax.broadcasted_iota(jnp.int32, (ROWS, ROWS), 0)
     numbers = wave_numbers(index, ROWS)
     numbers_ref[...] = numbers
+    copies[0].wait()
+    cosine_line, sine_line = lines[:, :ROWS], lines[:, ROWS:]
     table_y = circulant(0.25 * unit, numbers, cosine_line, sine_line)[0]
     table_z = circulant(-0.25 * unit, numbers, cosine_line, sine_line)[1]
-    cosine, sine = cos_sin(0.5 * sub_time * natural(pot_ref))
+    copies[1].wait()
+    blocks = ROWS // PLANES
+
+    def put(ref, part, plane, piece):
+        for block in range(blocks):
+            ref[place_of(block, blocks), part, pl.ds(plane, PLANES, stride=QUARTER), :] = piece[
+                block * PLANES : (block + 1) * PLANES
+            ]
+
+    for number in range(QUARTER):
+        put(keep_ref, 2, number, pot[order[number]])
+    cosine, sine = cos_sin(
+        0.5 * sub_time * jnp.concatenate([pot[plane] for plane in order], axis=1)
+    )
+    copies[2].wait()
     real_part, imag_part = rotated(
-        natural(field_ref.at[0]), natural(field_ref.at[1]), cosine, sine
-    )
-    field = from_left(side_by_side(whole_matrix(table_y), 1), jnp.concatenate([real_part, imag_part], axis=0))
-    scatter_planes(field[:ROWS], field[ROWS:], side_by_side(whole_matrix(table_z), 0), out_ref)
-    for plane in range(PLANES):
-        for block in range(out_ref.shape[0]):
-            out_ref[block, 2, pl.ds(plane, PLANES, stride=PLANES), :] = pot_ref[
-                plane, block * PLANES : (block + 1) * PLANES
-            ]
-
-
-def finish(sign, field_ref, pot_ref, first_ref, real_ref, imag_ref):
-    field = from_left(whole_left(first_ref[...]), gather_planes(field_ref))
-    cosine, sine = cos_sin(sign * 0.5 * sub_time * angles_of(pot_ref))
-    real_part, imag_part = rotated(field[:ROWS], field[ROWS:], cosine, sine)
-    store_natural(real_ref, real_part)
-    store_natural(imag_ref, imag_part)
-    return real_part, imag_part
+        1.0,
+        jnp.concatenate([field[0, 0, 0, plane] for plane in order], axis=1),
+        jnp.concatenate([field[0, 0, 1, plane] for plane in order], axis=1),
+        cosine,
+        sine,
+    )
+    turned = from_left(
+        side_by_side(whole_matrix(table_y), 1), jnp.concatenate([real_part, imag_part], axis=0)
+    )
+    turned = turn_z(turned[:ROWS], turned[ROWS:], side_by_side(whole_matrix(table_z), 0))
+    for number in range(PLANES):
+        ref = keep_ref if number < QUARTER else give_ref
+        for part in range(2):
+            piece = turned[number * ROWS : (number + 1) * ROWS, part * ROWS : (part + 1) * ROWS]
+            put(ref, part, number % QUARTER, piece)
+
+
+def join_kernel(keep_ref, got_ref, out_ref):
+    core = lax.axis_index("ka")
+    out_ref[core] = keep_ref[...]
+    out_ref[1 - core, :, 0:2] = got_ref[...]
+    out_ref[1 - core, :, 2] = keep_ref[:, 2]
 
 
 def end_kernel(
     sign,
     field_ref,
-    pot_ref,
+    cosine_ref,
+    sine_ref,
     first_ref,
     other_real_ref,
     other_imag_ref,
@@ -387,7 +510,10 @@
     imag_ref,
     density_ref,
 ):
-    real_part, imag_part = finish(sign, field_ref, pot_ref, first_ref, real_ref, imag_ref)
+    cosine, sine = natural(cosine_ref), natural(sine_ref)
+    real_part, imag_part = finish(
+        sign, field_ref, cosine, sine, first_ref, real_ref, imag_ref
+    )
     factor = factor_ref[0, 0]
     for plane in range(PLANES):
         density_ref[plane] = factor * (
@@ -396,10 +522,34 @@
         )
 
 
-def final_kernel(sign, field_ref, pot_ref, first_ref, out_ref):
-    finish(
-        sign, field_ref, pot_ref, first_ref, out_ref.at[0, 0, 0], out_ref.at[0, 0, 1]
-    )
+def final_kernel(sign, field_ref, got_ref, pot_ref, first_ref, out_ref):
+    core = lax.axis_index("ka")
+    order = plane_order(core)
+    blocks = got_ref.shape[0]
+
+    def part_of(part):
+        planes = []
+        for number in range(PLANES):
+            at = (part, pl.ds(number % QUARTER * PLANES, PLANES), slice(None))
+            rows = [
+                field_ref[(core, place_of(block, blocks)) + at]
+                if number < QUARTER
+                else got_ref[(place_of(block, blocks),) + at]
+                for block in range(blocks)
+            ]
+            planes.append(jnp.concatenate(rows, axis=0))
+        return jnp.concatenate(planes, axis=1)
+
+    cosine, sine = cos_sin(
+        0.5 * sub_time * jnp.concatenate([pot_ref[plane] for plane in order], axis=1)
+    )
+    field = from_left(
+        whole_left(first_ref[...]), jnp.concatenate([part_of(0), part_of(1)], axis=0)
+    )
+    real_part, imag_part = rotated(sign, field[:ROWS], field[ROWS:], cosine, sine)
+    for number, plane in enumerate(order):
+        out_ref[0, 0, 0, plane] = lane(real_part, number)
+        out_ref[0, 0, 1, plane] = lane(imag_part, number)
 
 
 def stack_planes(value):
@@ -408,22 +558,17 @@
 
 def density_kernel(own_ref, other_ref, left_ref, right_ref, density_ref, out_ref):
     density = natural(own_ref) + natural(other_ref)
-    for plane in range(PLANES):
-        density_ref[plane] = lane(density, plane)
+    store_natural(density_ref, density)
     spectrum = from_right(stack_planes(from_left(left_ref[...], density)), right_ref[...])
     for plane in range(PLANES):
-        for block in range(out_ref.shape[0]):
+        for block in range(ROWS // PLANES):
             start = plane * ROWS + block * PLANES
-            out_ref[block, pl.ds(plane, PLANES, stride=PLANES), :] = spectrum[
-                start : start + PLANES
-            ]
+            rows_to(out_ref, block, (), plane, spectrum[start : start + PLANES])
 
 
 def coulomb_kernel(unit, field_ref, square_ref, left_ref, out_ref):
     blocks = field_ref.shape[0]
-    rows = jnp.concatenate(
-        [field_ref[:, line].reshape(ROWS, ROWS) for line in range(PLANES)], axis=1
-    )
+    rows = jnp.concatenate([gathered(field_ref, line) for line in range(PLANES)], axis=1)
     rows = from_left(left_ref[...], rows)
     index = lax.broadcasted_iota(jnp.int32, (ROWS, ROWS), 0)
     number = unit * jnp.where(index < ROWS // 2, index, index - ROWS).astype(jnp.float32)
@@ -432,12 +577,14 @@
     for line in range(PLANES):
         square = along + square_ref[pl.ds(line, 1), :]
         nonzero = square > 0
-        parts.append(
-            lane(rows, line) * jnp.where(nonzero, 4.0 * math.pi / jnp.where(nonzero, square, 1.0), 0.0)
-        )
+        inverse = jnp.where(nonzero, 4.0 * math.pi / jnp.where(nonzero, square, 1.0), 0.0)
+        parts.append(lane(rows, line) * inverse)
     rows = from_left(left_ref[...], jnp.concatenate(parts, axis=1))
     for line in range(PLANES):
-        out_ref[:, line] = lane(rows, line).reshape(blocks, PLANES, ROWS)
+        for block in range(blocks):
+            out_ref[place_of(block, blocks), line] = lane(rows, line)[
+                block * PLANES : (block + 1) * PLANES
+            ]
 
 
 def hartree_kernel(
@@ -449,7 +596,8 @@
     orbital_imag_ref,
     adjoint_real_ref,
     adjoint_imag_ref,
-    pot_ref,
+    cosine_ref,
+    sine_ref,
     cas_left_ref,
     cas_right_ref,
     second_ref,
@@ -457,7 +605,10 @@
     out_ref,
     cross_ref,
 ):
-    spectrum = angles_of(field_ref)
+    spectrum = jnp.concatenate(
+        [gathered(field_ref, pl.ds(plane, PLANES, stride=PLANES)) for plane in range(PLANES)],
+        axis=1,
+    )
     hartree = from_right(
         stack_planes(from_left(cas_left_ref[...], spectrum)), cas_right_ref[...]
     )
@@ -467,15 +618,19 @@
         cross_ref[plane] = cross
         real_parts.append(adjoint_real_ref[plane] + step_time * cross * orbital_imag_ref[plane])
         imag_parts.append(adjoint_imag_ref[plane] - step_time * cross * orbital_real_ref[plane])
-    cosine, sine = cos_sin(sign * 0.5 * sub_time * angles_of(pot_ref))
-    real_part, imag_part = rotated(
-        jnp.concatenate(real_parts, axis=1), jnp.concatenate(imag_parts, axis=1), cosine, sine
-    )
-    field = from_left(whole_left(second_ref[...]), jnp.concatenate([real_part, imag_part], axis=0))
-    scatter_planes(field[:ROWS], field[ROWS:], right_ref[...], out_ref)
-
-
-def run(kernel, outputs, *operands):
+    begin(
+        sign,
+        jnp.concatenate(real_parts, axis=1),
+        jnp.concatenate(imag_parts, axis=1),
+        natural(cosine_ref),
+        natural(sine_ref),
+        whole_left(second_ref[...]),
+        right_ref[...],
+        out_ref,
+    )
+
+
+def run(kernel, outputs, *operands, space=pltpu.VMEM, scratch=()):
     made = pl.pallas_call(
         kernel,
         out_shape=[
@@ -483,10 +638,11 @@
             for out in outputs
         ],
         in_specs=[
-            pl.BlockSpec(memory_space=pltpu.SMEM if operand.size < ROWS else pltpu.VMEM)
+            pl.BlockSpec(memory_space=pltpu.SMEM if operand.size < ROWS else space)
             for operand in operands
         ],
         out_specs=[pl.BlockSpec(memory_space=pltpu.VMEM) for _ in outputs],
+        scratch_shapes=list(scratch),
         compiler_params=pltpu.CompilerParams(vmem_limit_bytes=24 * 2**20),
     )(*operands)
     return made[0] if len(outputs) == 1 else made
@@ -504,9 +660,13 @@
     place = core * half + fft_index % half
     lattice_unit = 2.0 * math.pi / (grid_size * spacing)
 
-    groups = [
-        [c * blocks + h * half + j for c in range(2) for j in range(half)] for h in range(2)
-    ]
+    groups = []
+    for h in range(2):
+        devices = [c * blocks + h * half + j for c in range(2) for j in range(half)]
+        group = [0] * blocks
+        for block, device in enumerate(devices):
+            group[place_of(block, blocks)] = device
+        groups.append(group)
     regroup = []
     for c in range(2):
         for f in range(blocks):
@@ -519,6 +679,11 @@
     def exchange(array):
         return lax.all_to_all(array, AXES, 0, 0, axis_index_groups=groups, tiled=True)
 
+    def exchange_all(array):
+        return lax.all_to_all(
+            array, AXES, 0, 0, axis_index_groups=[groups[0] + groups[1]], tiled=True
+        )
+
     def move(array, pairs):
         return lax.ppermute(array, AXES, pairs)
 
@@ -554,14 +719,32 @@
     weight = own_weight / jnp.sum(kpoint_weight).astype(jnp.float32)
     factor = (2.0 * weight * occupied).reshape(1, 1)
 
-    sent, numbers_full = run(
+    keep, give, numbers_full = run(
         functools.partial(start_kernel, lattice_unit),
-        [(blocks, 3, PLANES * PLANES, ROWS), (ROWS, ROWS)],
-        orbitals.reshape(natural_shape),
+        [
+            (blocks, 3, PLANES * QUARTER, ROWS),
+            (blocks, 2, PLANES * QUARTER, ROWS),
+            (ROWS, ROWS),
+        ],
+        orbitals,
         potential,
         line_pair,
-    )
-    sent = move(sent, regroup)
+        space=pltpu.HBM,
+        scratch=[
+            pltpu.VMEM(orbitals.shape, jnp.float32),
+            pltpu.VMEM(real_shape, jnp.float32),
+            pltpu.VMEM((ROWS, 2 * ROWS), jnp.float32),
+            pltpu.SemaphoreType.DMA((3,)),
+        ],
+    )
+    cores = [(0, 1), (1, 0)]
+    sent = run(
+        join_kernel,
+        [(2, blocks, 3, PLANES * QUARTER, ROWS)],
+        keep,
+        lax.ppermute(give, "ka", cores),
+    )
+    field = exchange_all(sent.reshape(2 * blocks, 3, PLANES * QUARTER, ROWS))
     left_shape = jax.ShapeDtypeStruct((ROWS, 4 * ROWS), jnp.bfloat16)
     right_shape = jax.ShapeDtypeStruct((4 * ROWS, 2 * ROWS), jnp.bfloat16)
     made = run(
@@ -571,83 +754,69 @@
         numbers_full,
         line_pair,
     )
-    early = (squares, factor, costate[0, 0, 0], costate[0, 0, 1])
-    sent, made, early = lax.optimization_barrier((sent, made, early))
-    squares, factor, costate_real, costate_imag = early
+    early = (squares, factor, jnp.stack([costate[0, 0, 0], costate[0, 0, 1], xc_kernel]))
+    field, made, early = lax.optimization_barrier((field, made, early))
+    squares, factor, moving = early
     tables = {1.0: made[0 : 2 * count_x + 2 : 2], -1.0: made[1 : 2 * count_x + 2 : 2]}
     right_z = {1.0: made[-2], -1.0: made[-1]}
 
-    def swap_beside(sent, array):
-        sent, array = lax.optimization_barrier((sent, array))
-        return lax.optimization_barrier((swap_field(sent), move(array, regroup)))
-
     def table_x(sign, count):
         return tables[sign][count if sign > 0 else count_x - 1 - count]
 
     def table_y(sign):
         return tables[sign][count_x]
 
-    def middle(sign, field, in_rows, count, pot):
-        if in_rows:
-            tabs = (pot, table_y(sign), table_y(sign))
-        else:
-            tabs = (pot, table_x(sign, count - 1), table_x(sign, count))
+    def tables_of(sign, count):
+        if count % 2 == 0:
+            return table_y(sign), table_y(sign), right_z[sign]
+        return table_x(sign, count - 1), table_x(sign, count), right_z[sign]
+
+    def middle(sign, field, count):
+        waves = waves_rows if count % 2 == 0 else waves_cols
         return run(
-            functools.partial(mid_kernel, sign), [sent_shape], field, *tabs, right_z[sign]
+            functools.partial(mid_kernel, sign),
+            [sent_shape],
+            field,
+            *waves,
+            *tables_of(sign, count),
         )
 
+    sent, *waves_cols = run(
+        functools.partial(first_mid_kernel, 1.0),
+        [(blocks, 3) + sent_shape[2:], real_shape, real_shape],
+        field,
+        *tables_of(1.0, 1),
+    )
+    sent, moving = lax.optimization_barrier((sent, moving))
+    moving = move(moving, regroup)
+    sent, *waves_rows = run(
+        functools.partial(second_mid_kernel, 1.0),
+        [sent_shape, real_shape, real_shape],
+        exchange(sent.reshape(blocks, 3, PLANES, PLANES, ROWS)),
+        *tables_of(1.0, 2),
+    )
+    sent = middle(1.0, swap_field(sent), 3)
+    sent, moving = lax.optimization_barrier((sent, moving))
     kept = []
-    for count in range(1, count_x):
-        if count == 1:
-            field = exchange(sent.reshape(blocks, 3, PLANES, PLANES, ROWS))
-            pot_sent = sent
-            sent, pot_cols = run(
-                functools.partial(first_mid_kernel, 1.0),
-                [sent_shape, block_shape[:1] + block_shape[2:]],
-                field,
-                table_x(1.0, 0),
-                table_x(1.0, 1),
-                right_z[1.0],
-            )
-            continue
-        if count == 2:
-            field, adjoint_real = swap_beside(sent, costate_real)
-            sent, pot_rows = run(
-                functools.partial(second_mid_kernel, 1.0),
-                [sent_shape, sent_shape[:1] + sent_shape[2:]],
-                field,
-                pot_sent,
-                table_y(1.0),
-                table_y(1.0),
-                right_z[1.0],
-            )
-            continue
-        if count == 3:
-            field, adjoint_imag = swap_beside(sent, costate_imag)
-        elif count == 5:
-            field, xc_rows = swap_beside(sent, xc_kernel)
-        else:
-            field = swap_field(sent)
-        in_rows = count % 2 == 0
+    for count in range(4, count_x):
+        field = swap_field(sent)
         if count % SUB == 0:
             sent, *orbital = run(
                 functools.partial(step_kernel, 1.0),
                 [sent_shape, real_shape, real_shape],
                 field,
-                pot_rows,
-                table_y(1.0),
-                table_y(1.0),
-                right_z[1.0],
+                *waves_rows,
+                *tables_of(1.0, count),
             )
             kept.append(orbital)
         else:
-            sent = middle(1.0, field, in_rows, count, pot_rows if in_rows else pot_cols)
-    adjoint = [adjoint_real, adjoint_imag]
+            sent = middle(1.0, field, count)
+    adjoint, xc_rows = [moving[0], moving[1]], moving[2]
     *orbital, partial = run(
         functools.partial(end_kernel, 1.0),
         [real_shape] * 3,
         swap_field(sent),
-        pot_rows,
+        *waves_rows,
         table_y(1.0),
         *adjoint,
         factor,
@@ -680,38 +849,44 @@
             xc_rows,
             *kept[step_index],
             *adjoint,
-            pot_rows,
+            *waves_rows,
             cas_left,
             cas_right,
             table_y(-1.0),
             right_z[-1.0],
         )
         first = (STEPS - 1 - step_index) * SUB
-        for count in range(first + 1, first + SUB):
-            in_rows = count % 2 == 0
-            sent = middle(
-                -1.0, swap_field(sent), in_rows, count, pot_rows if in_rows else pot_cols
-            )
+        for count in range(first + 1, first + SUB - 1):
+            sent = middle(-1.0, swap_field(sent), count)
         field = swap_field(sent)
         if step_index > 0:
+            sent = middle(-1.0, field, first + SUB - 1)
             *adjoint, partial = run(
                 functools.partial(end_kernel, -1.0),
                 [real_shape] * 3,
-                field,
-                pot_rows,
+                swap_field(sent),
+                *waves_rows,
                 table_y(-1.0),
                 *kept[step_index - 1],
                 factor,
             )
-        else:
-            adjoint = run(
-                functools.partial(final_kernel, -1.0),
-                [orbitals.shape],
-                field,
-                pot_rows,
-                table_y(-1.0),
-            )
-    result = move(adjoint, regroup)
+    sent = run(
+        functools.partial(last_mid_kernel, -1.0),
+        [(2 * blocks, 2, PLANES * QUARTER, ROWS)],
+        field,
+        *waves_cols,
+        *tables_of(-1.0, count_x - 1),
+    )
+    field = exchange_all(sent).reshape(2, blocks, 2, PLANES * QUARTER, ROWS)
+    give = lax.dynamic_index_in_dim(field, 1 - core, 0, keepdims=False)
+    result = run(
+        functools.partial(final_kernel, -1.0),
+        [orbitals.shape],
+        field,
+        lax.ppermute(give, "ka", cores),
+        potential,
+        table_y(-1.0),
+    )
     beside = lax.ppermute(cross, "ka", [(0, 1), (1, 0)])
     return (result, jnp.where(core == side, cross, beside))
 

time: 562 us -> 525 us (0.934)
  blocking collectives: 296 us -> 272 us
  starting transfers between devices: 36.6 us -> 29.3 us
    ppermute x7 -> x3, waiting for transfers between devices: 141 us -> 59 us  [move(): return lax.ppermute(array, AXES, pairs)]
    all_to_all x0 -> x2, waiting for transfers between devices: none -> 50.5 us  [exchange_all(): lax.all_to_all(array, AXES, 0, 0, axis_index_groups=[groups[0] + groups[1...]
    all_to_all x3 -> x2, waiting for transfers between devices: 4.83 us -> 30.2 us  [exchange(): lax.all_to_all(array, AXES, 0, 0, axis_index_groups=groups, tiled=True)]
    all_to_all x17 -> x16, blocking collectives: 296 us -> 272 us  [exchange(): lax.all_to_all(array, AXES, 0, 0, axis_index_groups=groups, tiled=True)]
    ppermute x7 -> x3, starting transfers between devices: 21.1 us -> 8.05 us  [move(): return lax.ppermute(array, AXES, pairs)]
    all_to_all x0 -> x2, starting transfers between devices: none -> 11.3 us  [exchange_all(): lax.all_to_all(array, AXES, 0, 0, axis_index_groups=[groups[0] + groups[1...]
    all_to_all x3 -> x2, starting transfers between devices: 15.5 us -> 9.02 us  [exchange(): lax.all_to_all(array, AXES, 0, 0, axis_index_groups=groups, tiled=True)]
    pallas_call x24 -> x25, Pallas kernels: 48.9 us -> 45.1 us  [run(): pl.pallas_call(kernel, out_shape=[jax.ShapeDtypeStruct(out, jnp.float32)...]
  transfers between devices with their start and end apart: 11 -> 10, of which waited for: 11 -> 9; matrix products, arithmetic and copies ran while one was open for 1% -> 2% of each run, Pallas kernels for 1% -> 1%
where the time goes in v4:
time: 525 us; the launch traced here: 515 us
  blocking collectives  272 us (52%)
  waiting for transfers between devices  143 us (27%)
  Pallas kernels  45.1 us (9%)
  starting transfers between devices  29.3 us (6%)
  local copies, waits for them, and re-layouts  18.8 us (4%)
    all_to_all x16, blocking collectives, exchange(): lax.all_to_all(array, AXES, 0, 0, axis_index_groups=groups, tiled=True)  272 us
    ppermute x3, waiting for transfers between devices, move(): return lax.ppermute(array, AXES, pairs)  59 us
    all_to_all x2, waiting for transfers between devices, exchange_all(): lax.all_to_all(array, AXES, 0, 0, axis_index_groups=[groups[0] + groups[1...  50.5 us
    pallas_call x25, Pallas kernels, run(): pl.pallas_call(kernel, out_shape=[jax.ShapeDtypeStruct(out, jnp.float32)...  45.1 us
    all_to_all x2, waiting for transfers between devices, exchange(): lax.all_to_all(array, AXES, 0, 0, axis_index_groups=groups, tiled=True)  30.2 us
    unnamed x84, local copies, waits for them, and re-layouts  13.3 us
    all_to_all x2, starting transfers between devices, exchange_all(): lax.all_to_all(array, AXES, 0, 0, axis_index_groups=[groups[0] + groups[1...  11.3 us
  transfers between devices with their start and end apart: 10, of which 9 were waited for; matrix products, arithmetic and copies ran while one was open for 2% of the time, Pallas kernels for 1%

profile of v4, /device:TPU:1, one launch (start us, length us, event | category | flops | bytes accessed | tf_op | source)
XLA Modules:
  0.0 515.5 jit_solution(13669454628356149011)
XLA Ops:
  3.8 3.2 shard_map.122
  7.1 1.9 collective-permute-done.got_ref
  10.3 7.1 %all-to-all-start = ((f32[32,3,32,128]{3,2,1,0:T(8,128)}), f32[32,3,32,128]{3,2,1,0:T(8,128)S(1)}, u32[]{:S(2)}, u32[]{:S(2)}) async-start(f32[32,3,32,128]{3,2,1,0:T(8,128)} %bitcast), calls=%async_computation | async-start | bytes 3145728 | tf_op jit(solution)/shard_map/all_to_all | solution.py:683
  20.8 4.4 shard_map.124
  27.0 2.3 pad_maximum_fusion
  29.4 24.9 %all-to-all-done.field_ref = f32[32,3,32,128]{3,2,1,0:T(8,128)S(1)} async-done(((f32[32,3,32,128]{3,2,1,0:T(8,128)}), f32[32,3,32,128]{3,2,1,0:T(8,128)S(1)}, u32[]{:S(2)}, u32[]{:S(2)}) %all-to-all-start) | async-done | bytes 1572896 | tf_op jit(solution)/shard_map/all_to_all | solution.py:683
  56.9 2.3 shard_map.125
  59.1 24.9 %all_to_all.100.field_ref = f32[16,3,8,8,128]{4,3,2,1,0:T(8,128)S(1)} all-to-all(f32[16,3,8,8,128]{4,3,2,1,0:T(8,128)S(1)} %bitcast.49), channel_id=1, replica_groups={{0,1,16,17,2,3,18,19,4,5,20,21,6,7,22,23},{8,9,24,25,10,11,26,27,12,13,..., dimensions={0} | all-to-all | bytes 3145728 | tf_op jit(solution)/shard_map/all_to_all | solution.py:680
  84.0 2.1 shard_map.126
  87.2 4.3 all-to-all-start.2
  91.5 3.2 collective-permute-start.1
  94.7 19.1 %all-to-all-done.2.field_ref = f32[16,2,8,8,128]{4,3,2,1,0:T(8,128)} async-done(((f32[16,2,8,8,128]{4,3,2,1,0:T(8,128)}), f32[16,2,8,8,128]{4,3,2,1,0:T(8,128)}, u32[]{:S(2)}, u32[]{:S(2)}) %all-to-all-start.2) | async-done | bytes 1048608 | tf_op jit(solution)/shard_map/all_to_all | solution.py:680
  115.6 2.9 shard_map.127
  118.5 12.8 %collective-permute-done.1 = f32[3,8,128,128]{3,2,1,0:T(8,128)} collective-permute-done((f32[3,8,128,128]{3,2,1,0:T(8,128)}, f32[3,8,128,128]{3,2,1,0:T(8,128)}, u32[]{:S(2)}, u32[]{:S(2)}) %collective-permute-start.1) | collective-permute-done | bytes 1572896 | tf_op jit(solution)/shard_map/ppermute | solution.py:688
  131.3 18.5 %all_to_all.101.field_ref = f32[16,2,8,8,128]{4,3,2,1,0:T(8,128)S(1)} all-to-all(f32[16,2,8,8,128]{4,3,2,1,0:T(8,128)S(1)} %bitcast.39), channel_id=1, replica_groups={{0,1,16,17,2,3,18,19,4,5,20,21,6,7,22,23},{8,9,24,25,10,11,26,27,12,13,..., dimensions={0} | all-to-all | bytes 2097152 | tf_op jit(solution)/shard_map/all_to_all | solution.py:680
  149.8 1.8 shard_map.128
  152.4 17.8 %all_to_all.102.field_ref = f32[16,2,8,8,128]{4,3,2,1,0:T(8,128)S(1)} all-to-all(f32[16,2,8,8,128]{4,3,2,1,0:T(8,128)S(1)} %bitcast.53), channel_id=1, replica_groups={{0,1,16,17,2,3,18,19,4,5,20,21,6,7,22,23},{8,9,24,25,10,11,26,27,12,13,..., dimensions={0} | all-to-all | bytes 2097152 | tf_op jit(solution)/shard_map/all_to_all | solution.py:680
  171.9 17.6 %all_to_all.103.field_ref = f32[16,2,8,8,128]{4,3,2,1,0:T(8,128)S(1)} all-to-all(f32[16,2,8,8,128]{4,3,2,1,0:T(8,128)S(1)} %bitcast.40), channel_id=1, replica_groups={{0,1,16,17,2,3,18,19,4,5,20,21,6,7,22,23},{8,9,24,25,10,11,26,27,12,13,..., dimensions={0} | all-to-all | bytes 2097152 | tf_op jit(solution)/shard_map/all_to_all | solution.py:680
  189.5 1.7 shard_map.130
  191.2 17.6 %all_to_all.104.field_ref = f32[16,2,8,8,128]{4,3,2,1,0:T(8,128)S(1)} all-to-all(f32[16,2,8,8,128]{4,3,2,1,0:T(8,128)S(1)} %bitcast.45), channel_id=1, replica_groups={{0,1,16,17,2,3,18,19,4,5,20,21,6,7,22,23},{8,9,24,25,10,11,26,27,12,13,..., dimensions={0} | all-to-all | bytes 2097152 | tf_op jit(solution)/shard_map/all_to_all | solution.py:680
  208.8 1.7 shard_map.131
  211.4 4.7 all-to-all-start.7
  216.1 2.5 slice_bitcast_fusion
  218.6 11.1 %all-to-all-done.7.field_ref = f32[16,2,8,8,128]{4,3,2,1,0:T(8,128)} async-done(((f32[16,2,8,8,128]{4,3,2,1,0:T(8,128)}), f32[16,2,8,8,128]{4,3,2,1,0:T(8,128)}, u32[]{:S(2)}, u32[]{:S(2)}) %all-to-all-start.7) | async-done | bytes 1048608 | tf_op jit(solution)/shard_map/all_to_all | solution.py:680
  231.9 2.0 shard_map.132
  233.9 2.4 collective-permute-start.2
  236.3 22.6 %collective-permute-done.2.other_ref = f32[8,128,128]{2,1,0:T(8,128)S(1)} collective-permute-done((f32[8,128,128]{2,1,0:T(8,128)S(1)}, f32[8,128,128]{2,1,0:T(8,128)S(1)}, u32[]{:S(2)}, u32[]{:S(2)}) %collective-permute-start.2) | collective-permute-done | bytes 524320 | tf_op jit(solution)/shard_map/ppermute | solution.py:688
  259.6 14.9 %all_to_all.105.field_ref = f32[16,8,8,128]{3,2,1,0:T(8,128)S(1)} all-to-all(f32[16,8,8,128]{3,2,1,0:T(8,128)S(1)} %bitcast.54), channel_id=1, replica_groups={{0,1,16,17,2,3,18,19,4,5,20,21,6,7,22,23},{8,9,24,25,10,11,26,27,12,13,..., dimensions={0} | all-to-all | bytes 1048576 | tf_op jit(solution)/shard_map/all_to_all | solution.py:680
  275.1 12.0 %all_to_all.106 = f32[16,8,8,128]{3,2,1,0:T(8,128)S(1)} all-to-all(f32[16,8,8,128]{3,2,1,0:T(8,128)S(1)} %shard_map.134), channel_id=1, replica_groups={{0,1,16,17,2,3,18,19,4,5,20,21,6,7,22,23},{8,9,24,25,10,11,26,27,12,13,..., dimensions={0} | all-to-all | bytes 1048576 | tf_op jit(solution)/shard_map/all_to_all | solution.py:680
  287.1 2.0 shard_map.135
  289.1 17.8 %all_to_all.107.field_ref = f32[16,2,8,8,128]{4,3,2,1,0:T(8,128)S(1)} all-to-all(f32[16,2,8,8,128]{4,3,2,1,0:T(8,128)S(1)} %bitcast.52), channel_id=1, replica_groups={{0,1,16,17,2,3,18,19,4,5,20,21,6,7,22,23},{8,9,24,25,10,11,26,27,12,13,..., dimensions={0} | all-to-all | bytes 2097152 | tf_op jit(solution)/shard_map/all_to_all | solution.py:680
  308.6 17.7 %all_to_all.108.field_ref = f32[16,2,8,8,128]{4,3,2,1,0:T(8,128)S(1)} all-to-all(f32[16,2,8,8,128]{4,3,2,1,0:T(8,128)S(1)} %bitcast.41), channel_id=1, replica_groups={{0,1,16,17,2,3,18,19,4,5,20,21,6,7,22,23},{8,9,24,25,10,11,26,27,12,13,..., dimensions={0} | all-to-all | bytes 2097152 | tf_op jit(solution)/shard_map/all_to_all | solution.py:680
  327.9 17.8 %all_to_all.109.field_ref = f32[16,2,8,8,128]{4,3,2,1,0:T(8,128)S(1)} all-to-all(f32[16,2,8,8,128]{4,3,2,1,0:T(8,128)S(1)} %bitcast.46), channel_id=1, replica_groups={{0,1,16,17,2,3,18,19,4,5,20,21,6,7,22,23},{8,9,24,25,10,11,26,27,12,13,..., dimensions={0} | all-to-all | bytes 2097152 | tf_op jit(solution)/shard_map/all_to_all | solution.py:680
  345.7 1.7 shard_map.138
  347.4 17.8 %all_to_all.110.field_ref = f32[16,2,8,8,128]{4,3,2,1,0:T(8,128)S(1)} all-to-all(f32[16,2,8,8,128]{4,3,2,1,0:T(8,128)S(1)} %bitcast.42), channel_id=1, replica_groups={{0,1,16,17,2,3,18,19,4,5,20,21,6,7,22,23},{8,9,24,25,10,11,26,27,12,13,..., dimensions={0} | all-to-all | bytes 2097152 | tf_op jit(solution)/shard_map/all_to_all | solution.py:680
  365.9 2.5 collective-permute-start.3
  368.4 23.6 %collective-permute-done.3.other_ref = f32[8,128,128]{2,1,0:T(8,128)S(1)} collective-permute-done((f32[8,128,128]{2,1,0:T(8,128)S(1)}, f32[8,128,128]{2,1,0:T(8,128)S(1)}, u32[]{:S(2)}, u32[]{:S(2)}) %collective-permute-start.3) | collective-permute-done | bytes 524320 | tf_op jit(solution)/shard_map/ppermute | solution.py:688
  392.6 12.2 %all_to_all.111.field_ref = f32[16,8,8,128]{3,2,1,0:T(8,128)S(1)} all-to-all(f32[16,8,8,128]{3,2,1,0:T(8,128)S(1)} %bitcast.55), channel_id=1, replica_groups={{0,1,16,17,2,3,18,19,4,5,20,21,6,7,22,23},{8,9,24,25,10,11,26,27,12,13,..., dimensions={0} | all-to-all | bytes 1048576 | tf_op jit(solution)/shard_map/all_to_all | solution.py:680
  405.4 12.2 %all_to_all.112 = f32[16,8,8,128]{3,2,1,0:T(8,128)S(1)} all-to-all(f32[16,8,8,128]{3,2,1,0:T(8,128)S(1)} %shard_map.141), channel_id=1, replica_groups={{0,1,16,17,2,3,18,19,4,5,20,21,6,7,22,23},{8,9,24,25,10,11,26,27,12,13,..., dimensions={0} | all-to-all | bytes 1048576 | tf_op jit(solution)/shard_map/all_to_all | solution.py:680
  417.6 2.0 shard_map.142
  420.4 18.2 %all_to_all.113.field_ref = f32[16,2,8,8,128]{4,3,2,1,0:T(8,128)S(1)} all-to-all(f32[16,2,8,8,128]{4,3,2,1,0:T(8,128)S(1)} %bitcast.51), channel_id=1, replica_groups={{0,1,16,17,2,3,18,19,4,5,20,21,6,7,22,23},{8,9,24,25,10,11,26,27,12,13,..., dimensions={0} | all-to-all | bytes 2097152 | tf_op jit(solution)/shard_map/all_to_all | solution.py:680
  438.6 1.6 shard_map.143
  440.2 17.6 %all_to_all.114.field_ref = f32[16,2,8,8,128]{4,3,2,1,0:T(8,128)S(1)} all-to-all(f32[16,2,8,8,128]{4,3,2,1,0:T(8,128)S(1)} %bitcast.43), channel_id=1, replica_groups={{0,1,16,17,2,3,18,19,4,5,20,21,6,7,22,23},{8,9,24,25,10,11,26,27,12,13,..., dimensions={0} | all-to-all | bytes 2097152 | tf_op jit(solution)/shard_map/all_to_all | solution.py:680
  459.6 17.6 %all_to_all.115.field_ref = f32[16,2,8,8,128]{4,3,2,1,0:T(8,128)S(1)} all-to-all(f32[16,2,8,8,128]{4,3,2,1,0:T(8,128)S(1)} %bitcast.44), channel_id=1, replica_groups={{0,1,16,17,2,3,18,19,4,5,20,21,6,7,22,23},{8,9,24,25,10,11,26,27,12,13,..., dimensions={0} | all-to-all | bytes 2097152 | tf_op jit(solution)/shard_map/all_to_all | solution.py:680
  477.2 2.6 shard_map.145
  479.8 4.2 all-to-all-start.19
  484.3 25.7 %all-to-all-done.19 = f32[32,2,32,128]{3,2,1,0:T(8,128)S(1)} async-done(((f32[32,2,32,128]{3,2,1,0:T(8,128)}), f32[32,2,32,128]{3,2,1,0:T(8,128)S(1)}, u32[]{:S(2)}, u32[]{:S(2)}) %all-to-all-start.19) | async-done | bytes 1048608 | tf_op jit(solution)/shard_map/all_to_all | solution.py:683
  513.0 2.0 shard_map.146
  (109 shorter events, 30.8 us)
Async XLA Ops:
  0.6 1.0 copy-start.8
  1.7 1.2 copy-start.16
  7.0 2.0 collective-permute-start
  10.3 7.8 %copy-start.39 = (s32[2]{0:T(128)S(1)}, s32[2]{0:T(128)}, u32[]{:S(2)}) copy-start(s32[2]{0:T(128)} %param.16) | copy-start | bytes 28
  10.3 10.4 %copy-start.40 = (f32[8]{0:T(128)S(1)}, f32[8]{0:T(128)}, u32[]{:S(2)}) copy-start(f32[8]{0:T(128)} %param.15) | copy-start | bytes 100
  10.3 10.4 %copy-start.41 = (f32[2]{0:T(128)S(1)}, f32[2]{0:T(128)}, u32[]{:S(2)}) copy-start(f32[2]{0:T(128)} %constant.77.clone) | copy-start | bytes 28
  10.3 10.5 %copy-start.20 = (f32[128,256]{1,0:T(8,128)S(1)}, f32[128,256]{1,0:T(8,128)}, u32[]{:S(2)}) copy-start(f32[128,256]{1,0:T(8,128)} %constant.74.clone.lines_ref) | copy-start | bytes 393220
  10.3 44.0 %all-to-all-start = ((f32[32,3,32,128]{3,2,1,0:T(8,128)}), f32[32,3,32,128]{3,2,1,0:T(8,128)S(1)}, u32[]{:S(2)}, u32[]{:S(2)}) async-start(f32[32,3,32,128]{3,2,1,0:T(8,128)} %bitcast), calls=%async_computation | async-start | bytes 3145728 | tf_op jit(solution)/shard_map/all_to_all | solution.py:683
  25.2 4.0 copy-start.21
  25.2 4.0 copy-start.23
  25.3 4.0 copy-start.25
  25.3 4.0 copy-start.27
  25.3 4.0 copy-start.29
  25.3 4.0 copy-start.31
  25.3 4.0 copy-start.33
  25.3 4.0 copy-start.35
  25.3 4.0 copy-start.37
  54.3 1.2 copy-start
  55.5 1.4 copy-start.1
  86.2 1.0 copy-start.15
  87.2 26.6 %all-to-all-start.2 = ((f32[16,2,8,8,128]{4,3,2,1,0:T(8,128)}), f32[16,2,8,8,128]{4,3,2,1,0:T(8,128)}, u32[]{:S(2)}, u32[]{:S(2)}) async-start(f32[16,2,8,8,128]{4,3,2,1,0:T(8,128)} %bitcast.50), calls=%async_computation.2 | async-start | bytes 2097152 | tf_op jit(solution)/shard_map/all_to_all | solution.py:680
  91.5 39.8 %collective-permute-start.1 = (f32[3,8,128,128]{3,2,1,0:T(8,128)}, f32[3,8,128,128]{3,2,1,0:T(8,128)}, u32[]{:S(2)}, u32[]{:S(2)}) collective-permute-start(f32[3,8,128,128]{3,2,1,0:T(8,128)} %pad_maximum_fusion), channel_id=1, source_target_pairs={{0,0},{1,1},{2,2},{3,3},{4,4},{5,5},{6,6},{7,7},{8,16},{9,17},{10,... | collective-permute-start | bytes 4718600 | tf_op jit(solution)/shard_map/ppermute | solution.py:688
  113.8 0.9 copy-start.36
  152.4 19.4 %copy-start.12 = (f32[8,128,128]{2,1,0:T(8,128)}, f32[8,128,128]{2,1,0:T(8,128)S(1)}, u32[]{:S(2)}) copy-start(f32[8,128,128]{2,1,0:T(8,128)S(1)} %get-tuple-element.136.other_imag_ref.orbital_imag_ref) | copy-start | bytes 1572868
  152.4 17.8 %copy-start.32 = (bf16[128,512]{1,0:T(8,128)(2,1)S(1)}, bf16[128,512]{1,0:T(8,128)(2,1)}, u32[]{:S(2)}) copy-start(bf16[128,512]{1,0:T(8,128)(2,1)} %copy-done.31) | copy-start | bytes 393220
  152.4 17.8 %copy-start.34 = (bf16[128,512]{1,0:T(8,128)(2,1)S(1)}, bf16[128,512]{1,0:T(8,128)(2,1)}, u32[]{:S(2)}) copy-start(bf16[128,512]{1,0:T(8,128)(2,1)} %copy-done.33) | copy-start | bytes 393220
  210.5 1.0 copy-start.6
  211.4 18.3 %all-to-all-start.7 = ((f32[16,2,8,8,128]{4,3,2,1,0:T(8,128)}), f32[16,2,8,8,128]{4,3,2,1,0:T(8,128)}, u32[]{:S(2)}, u32[]{:S(2)}) async-start(f32[16,2,8,8,128]{4,3,2,1,0:T(8,128)} %bitcast.38), calls=%async_computation.7 | async-start | bytes 2097152 | tf_op jit(solution)/shard_map/all_to_all | solution.py:680
  229.8 1.0 copy-start.2
  230.8 1.0 copy-start.4
  231.9 27.0 %copy-start.7 = (bf16[128,256]{1,0:T(8,128)(2,1)S(1)}, bf16[128,256]{1,0:T(8,128)(2,1)}, u32[]{:S(2)}) copy-start(bf16[128,256]{1,0:T(8,128)(2,1)} %constant.75.clone.left_ref.cas_left_ref) | copy-start | bytes 196612
  231.9 27.0 %copy-start.14 = (bf16[256,128]{1,0:T(8,128)(2,1)S(1)}, bf16[256,128]{1,0:T(8,128)(2,1)}, u32[]{:S(2)}) copy-start(bf16[256,128]{1,0:T(8,128)(2,1)} %constant.76.clone.right_ref.cas_right_ref) | copy-start | bytes 196612
  233.9 25.0 %collective-permute-start.2 = (f32[8,128,128]{2,1,0:T(8,128)S(1)}, f32[8,128,128]{2,1,0:T(8,128)S(1)}, u32[]{:S(2)}, u32[]{:S(2)}) collective-permute-start(f32[8,128,128]{2,1,0:T(8,128)S(1)} %get-tuple-element.122.own_ref), channel_id=1, source_target_pairs={{0,8},{1,9},{2,10},{3,11},{4,12},{5,13},{6,14},{7,15},{8,0},{9,1},... | collective-permute-start | bytes 1572872 | tf_op jit(solution)/shard_map/ppermute | solution.py:688
  259.6 27.5 %copy-start.3 = (f32[8,128,128]{2,1,0:T(8,128)S(1)}, f32[8,128,128]{2,1,0:T(8,128)}, u32[]{:S(2)}) copy-start(f32[8,128,128]{2,1,0:T(8,128)} %get-tuple-element.149.other_imag_ref.adjoint_imag_ref) | copy-start | bytes 1572868
  259.6 27.5 %copy-start.5 = (f32[8,128,128]{2,1,0:T(8,128)S(1)}, f32[8,128,128]{2,1,0:T(8,128)}, u32[]{:S(2)}) copy-start(f32[8,128,128]{2,1,0:T(8,128)} %get-tuple-element.150.other_real_ref.adjoint_real_ref) | copy-start | bytes 1572868
  289.1 17.8 %copy-start.28 = (bf16[128,512]{1,0:T(8,128)(2,1)S(1)}, bf16[128,512]{1,0:T(8,128)(2,1)}, u32[]{:S(2)}) copy-start(bf16[128,512]{1,0:T(8,128)(2,1)} %copy-done.27) | copy-start | bytes 393220
  289.1 17.8 %copy-start.30 = (bf16[128,512]{1,0:T(8,128)(2,1)S(1)}, bf16[128,512]{1,0:T(8,128)(2,1)}, u32[]{:S(2)}) copy-start(bf16[128,512]{1,0:T(8,128)(2,1)} %copy-done.29) | copy-start | bytes 393220
  327.9 17.8 %copy-start.24 = (bf16[128,512]{1,0:T(8,128)(2,1)S(1)}, bf16[128,512]{1,0:T(8,128)(2,1)}, u32[]{:S(2)}) copy-start(bf16[128,512]{1,0:T(8,128)(2,1)} %copy-done.23) | copy-start | bytes 393220
  327.9 17.8 %copy-start.26 = (bf16[128,512]{1,0:T(8,128)(2,1)S(1)}, bf16[128,512]{1,0:T(8,128)(2,1)}, u32[]{:S(2)}) copy-start(bf16[128,512]{1,0:T(8,128)(2,1)} %copy-done.25) | copy-start | bytes 393220
  347.4 17.8 %copy-start.11 = (f32[8,128,128]{2,1,0:T(8,128)S(1)}, f32[8,128,128]{2,1,0:T(8,128)}, u32[]{:S(2)}) copy-start(f32[8,128,128]{2,1,0:T(8,128)} %copy-done.10) | copy-start | bytes 1572868
  347.4 17.8 %copy-start.13 = (f32[8,128,128]{2,1,0:T(8,128)S(1)}, f32[8,128,128]{2,1,0:T(8,128)}, u32[]{:S(2)}) copy-start(f32[8,128,128]{2,1,0:T(8,128)} %copy-done.12) | copy-start | bytes 1572868
  365.9 26.0 %collective-permute-start.3 = (f32[8,128,128]{2,1,0:T(8,128)S(1)}, f32[8,128,128]{2,1,0:T(8,128)S(1)}, u32[]{:S(2)}, u32[]{:S(2)}) collective-permute-start(f32[8,128,128]{2,1,0:T(8,128)S(1)} %get-tuple-element.137.own_ref), channel_id=1, source_target_pairs={{0,8},{1,9},{2,10},{3,11},{4,12},{5,13},{6,14},{7,15},{8,0},{9,1},... | collective-permute-start | bytes 1572872 | tf_op jit(solution)/shard_map/ppermute | solution.py:688
  420.4 18.2 %copy-start.22 = (bf16[128,512]{1,0:T(8,128)(2,1)S(1)}, bf16[128,512]{1,0:T(8,128)(2,1)}, u32[]{:S(2)}) copy-start(bf16[128,512]{1,0:T(8,128)(2,1)} %copy-done.21) | copy-start | bytes 393220
  479.8 4.2 copy-start.18
  479.8 30.2 %all-to-all-start.19 = ((f32[32,2,32,128]{3,2,1,0:T(8,128)}), f32[32,2,32,128]{3,2,1,0:T(8,128)S(1)}, u32[]{:S(2)}, u32[]{:S(2)}) async-start(f32[32,2,32,128]{3,2,1,0:T(8,128)} %shard_map.145), calls=%async_computation.19 | async-start | bytes 2097152 | tf_op jit(solution)/shard_map/all_to_all | solution.py:683
  484.0 29.1 %copy-start.9 = (f32[8,128,128]{2,1,0:T(8,128)S(1)}, f32[8,128,128]{2,1,0:T(8,128)}, u32[]{:S(2)}) copy-start(f32[8,128,128]{2,1,0:T(8,128)} %pot_ref.3) | copy-start | bytes 1572868
  484.0 27.3 %collective-permute-start.5 = (f32[8,128,128]{2,1,0:T(8,128)S(1)}, f32[8,128,128]{2,1,0:T(8,128)S(1)}, u32[]{:S(2)}, u32[]{:S(2)}) collective-permute-start(f32[8,128,128]{2,1,0:T(8,128)S(1)} %copy-done.18), channel_id=1, source_target_pairs={{0,16},{16,0},{1,17},{17,1},{2,18},{18,2},{3,19},{19,3},{4,20},{20... | collective-permute-start | bytes 1572872 | tf_op jit(solution)/shard_map/ppermute | solution.py:890
  510.8 2.2 collective-permute-start.4
  (4 other events, 3.4 us)

commit v5 on v4

--- a/solution.py
+++ b/solution.py
@@ -345,35 +345,42 @@
     between(sign, field, cosine, sine, first_ref, second_ref, right_ref, out_ref)
 
 
+def gather_all(field_ref, part):
+    return jnp.concatenate(
+        [
+            jnp.concatenate(
+                [
+                    field_ref[source, part, pl.ds(plane * QUARTER, QUARTER), :]
+                    for source in sources_of(field_ref.shape[0] // 2)
+                ],
+                axis=0,
+            )
+            for plane in range(PLANES)
+        ],
+        axis=1,
+    )
+
+
 def first_mid_kernel(
     sign, field_ref, first_ref, second_ref, right_ref, out_ref, cosine_ref, sine_ref
 ):
-    blocks = field_ref.shape[0] // 2
-
-    def part_of(part):
-        return jnp.concatenate(
-            [
-                jnp.concatenate(
-                    [
-                        field_ref[source, part, pl.ds(plane * QUARTER, QUARTER), :]
-                        for source in sources_of(blocks)
-                    ],
-                    axis=0,
-                )
-                for plane in range(PLANES)
-            ],
-            axis=1,
-        )
-
-    pot = part_of(2)
+    pot = gather_all(field_ref, 2)
     for plane in range(PLANES):
-        for block in range(blocks):
+        for block in range(ROWS // PLANES):
             rows_of = lane(pot, plane)[block * PLANES : (block + 1) * PLANES]
             rows_to(out_ref, block, (2,), plane, rows_of)
     cosine, sine = cos_sin(0.5 * sub_time * pot)
     store_natural(cosine_ref, cosine)
     store_natural(sine_ref, sine)
-    field = jnp.concatenate([part_of(0), part_of(1)], axis=0)
+    field = jnp.concatenate([gather_all(field_ref, 0), gather_all(field_ref, 1)], axis=0)
+    between(sign, field, cosine, sine, first_ref, second_ref, right_ref, out_ref)
+
+
+def all_mid_kernel(
+    sign, field_ref, cosine_ref, sine_ref, first_ref, second_ref, right_ref, out_ref
+):
+    cosine, sine = natural(cosine_ref), natural(sine_ref)
+    field = jnp.concatenate([gather_all(field_ref, 0), gather_all(field_ref, 1)], axis=0)
     between(sign, field, cosine, sine, first_ref, second_ref, right_ref, out_ref)
 
 
@@ -436,6 +443,25 @@
     return [core * QUARTER + number for number in range(QUARTER)] + [
         (1 - core) * QUARTER + number for number in range(QUARTER)
     ]
+
+
+def put_rows(ref, part, plane, piece):
+    blocks = ref.shape[0]
+    for block in range(blocks):
+        ref[place_of(block, blocks), part, pl.ds(plane, PLANES, stride=QUARTER), :] = piece[
+            block * PLANES : (block + 1) * PLANES
+        ]
+
+
+def begin_all(sign, real_part, imag_part, cosine, sine, second, right, keep_ref, give_ref):
+    real_part, imag_part = rotated(sign, real_part, imag_part, cosine, sine)
+    field = from_left(second, jnp.concatenate([real_part, imag_part], axis=0))
+    turned = turn_z(field[:ROWS], field[ROWS:], right)
+    for number in range(PLANES):
+        ref = keep_ref if number < QUARTER else give_ref
+        for part in range(2):
+            piece = turned[number * ROWS : (number + 1) * ROWS, part * ROWS : (part + 1) * ROWS]
+            put_rows(ref, part, number % QUARTER, piece)
 
 
 def start_kernel(
@@ -458,43 +484,31 @@
     table_y = circulant(0.25 * unit, numbers, cosine_line, sine_line)[0]
     table_z = circulant(-0.25 * unit, numbers, cosine_line, sine_line)[1]
     copies[1].wait()
-    blocks = ROWS // PLANES
-
-    def put(ref, part, plane, piece):
-        for block in range(blocks):
-            ref[place_of(block, blocks), part, pl.ds(plane, PLANES, stride=QUARTER), :] = piece[
-                block * PLANES : (block + 1) * PLANES
-            ]
-
     for number in range(QUARTER):
-        put(keep_ref, 2, number, pot[order[number]])
+        put_rows(keep_ref, 2, number, pot[order[number]])
     cosine, sine = cos_sin(
         0.5 * sub_time * jnp.concatenate([pot[plane] for plane in order], axis=1)
     )
     copies[2].wait()
-    real_part, imag_part = rotated(
+    begin_all(
         1.0,
         jnp.concatenate([field[0, 0, 0, plane] for plane in order], axis=1),
         jnp.concatenate([field[0, 0, 1, plane] for plane in order], axis=1),
         cosine,
         sine,
-    )
-    turned = from_left(
-        side_by_side(whole_matrix(table_y), 1), jnp.concatenate([real_part, imag_part], axis=0)
-    )
-    turned = turn_z(turned[:ROWS], turned[ROWS:], side_by_side(whole_matrix(table_z), 0))
-    for number in range(PLANES):
-        ref = keep_ref if number < QUARTER else give_ref
-        for part in range(2):
-            piece = turned[number * ROWS : (number + 1) * ROWS, part * ROWS : (part + 1) * ROWS]
-            put(ref, part, number % QUARTER, piece)
+        side_by_side(whole_matrix(table_y), 1),
+        side_by_side(whole_matrix(table_z), 0),
+        keep_ref,
+        give_ref,
+    )
 
 
 def join_kernel(keep_ref, got_ref, out_ref):
     core = lax.axis_index("ka")
     out_ref[core] = keep_ref[...]
     out_ref[1 - core, :, 0:2] = got_ref[...]
-    out_ref[1 - core, :, 2] = keep_ref[:, 2]
+    if keep_ref.shape[1] > 2:
+        out_ref[1 - core, :, 2] = keep_ref[:, 2]
 
 
 def end_kernel(
@@ -522,7 +536,7 @@
         )
 
 
-def final_kernel(sign, field_ref, got_ref, pot_ref, first_ref, out_ref):
+def finish_all(sign, field_ref, got_ref, pot_ref, first_ref):
     core = lax.axis_index("ka")
     order = plane_order(core)
     blocks = got_ref.shape[0]
@@ -546,10 +560,124 @@
     field = from_left(
         whole_left(first_ref[...]), jnp.concatenate([part_of(0), part_of(1)], axis=0)
     )
-    real_part, imag_part = rotated(sign, field[:ROWS], field[ROWS:], cosine, sine)
+    return order, rotated(sign, field[:ROWS], field[ROWS:], cosine, sine)
+
+
+def final_kernel(sign, field_ref, got_ref, pot_ref, first_ref, out_ref):
+    order, (real_part, imag_part) = finish_all(sign, field_ref, got_ref, pot_ref, first_ref)
     for number, plane in enumerate(order):
         out_ref[0, 0, 0, plane] = lane(real_part, number)
         out_ref[0, 0, 1, plane] = lane(imag_part, number)
+
+
+def end_all_kernel(
+    sign,
+    field_ref,
+    got_ref,
+    pot_ref,
+    first_ref,
+    other_ref,
+    factor_ref,
+    real_ref,
+    imag_ref,
+    density_ref,
+):
+    order, (real_part, imag_part) = finish_all(sign, field_ref, got_ref, pot_ref, first_ref)
+    factor = factor_ref[0, 0]
+    for number, plane in enumerate(order):
+        real_ref[plane] = lane(real_part, number)
+        imag_ref[plane] = lane(imag_part, number)
+        density_ref[plane] = factor * (
+            lane(real_part, number) * other_ref[0, 0, 0, plane]
+            + lane(imag_part, number) * other_ref[0, 0, 1, plane]
+        )
+
+
+def density_all_kernel(
+    own_ref, other_ref, left_ref, right_ref, density_ref, out_ref, whole_ref
+):
+    density = natural(own_ref) + natural(other_ref)
+    store_natural(density_ref, density)
+    spectrum = from_right(stack_planes(from_left(left_ref[...], density)), right_ref[...])
+    for plane in range(PLANES):
+        for block in range(ROWS // PLANES):
+            start = plane * ROWS + block * PLANES
+            whole_ref[block, pl.ds(plane, PLANES, stride=PLANES), :] = spectrum[
+                start : start + PLANES
+            ]
+    size = QUARTER * PLANES
+    start = pl.multiple_of(lax.axis_index("ka") * size, size)
+    out_ref[...] = whole_ref[:, pl.ds(start, size), :]
+
+
+def hartree_all_kernel(
+    sign,
+    field_ref,
+    got_ref,
+    density_ref,
+    xc_ref,
+    orbital_real_ref,
+    orbital_imag_ref,
+    adjoint_ref,
+    pot_ref,
+    cas_left_ref,
+    cas_right_ref,
+    second_ref,
+    right_ref,
+    keep_ref,
+    give_ref,
+    rows_ref,
+):
+    core = lax.axis_index("ka")
+    rows_ref[core] = field_ref[...]
+    rows_ref[1 - core] = got_ref[...]
+    spectrum = jnp.concatenate(
+        [
+            jnp.concatenate(
+                [
+                    rows_ref[number, block, pl.ds(plane, QUARTER, stride=PLANES), :]
+                    for block in range(field_ref.shape[0])
+                    for number in range(2)
+                ],
+                axis=0,
+            )
+            for plane in range(PLANES)
+        ],
+        axis=1,
+    )
+    hartree = from_right(
+        stack_planes(from_left(cas_left_ref[...], spectrum)), cas_right_ref[...]
+    )
+    for plane in range(PLANES):
+        rows_ref[plane // QUARTER, pl.ds(plane % QUARTER * QUARTER, QUARTER)] = (
+            hartree[plane * ROWS : (plane + 1) * ROWS]
+        ).reshape(QUARTER, QUARTER * PLANES, ROWS)
+    order = plane_order(core)
+    real_parts, imag_parts = [], []
+    for number, plane in enumerate(order):
+        at = core if number < QUARTER else 1 - core
+        own = rows_ref[at, pl.ds(number % QUARTER * QUARTER, QUARTER)].reshape(ROWS, ROWS)
+        cross = own + xc_ref[plane] * density_ref[plane]
+        real_parts.append(
+            adjoint_ref[0, 0, 0, plane] + step_time * cross * orbital_imag_ref[plane]
+        )
+        imag_parts.append(
+            adjoint_ref[0, 0, 1, plane] - step_time * cross * orbital_real_ref[plane]
+        )
+    cosine, sine = cos_sin(
+        0.5 * sub_time * jnp.concatenate([pot_ref[plane] for plane in order], axis=1)
+    )
+    begin_all(
+        sign,
+        jnp.concatenate(real_parts, axis=1),
+        jnp.concatenate(imag_parts, axis=1),
+        cosine,
+        sine,
+        whole_left(second_ref[...]),
+        right_ref[...],
+        keep_ref,
+        give_ref,
+    )
 
 
 def stack_planes(value):
@@ -566,25 +694,30 @@
             rows_to(out_ref, block, (), plane, spectrum[start : start + PLANES])
 
 
-def coulomb_kernel(unit, field_ref, square_ref, left_ref, out_ref):
-    blocks = field_ref.shape[0]
-    rows = jnp.concatenate([gathered(field_ref, line) for line in range(PLANES)], axis=1)
+def coulomb_kernel(unit, placed, field_ref, square_ref, left_ref, out_ref):
+    blocks, lines = field_ref.shape[:2]
+    places = [place_of(block, blocks) if placed else block for block in range(blocks)]
+    rows = jnp.concatenate(
+        [
+            jnp.concatenate([field_ref[place, line] for place in places], axis=0)
+            for line in range(lines)
+        ],
+        axis=1,
+    )
     rows = from_left(left_ref[...], rows)
     index = lax.broadcasted_iota(jnp.int32, (ROWS, ROWS), 0)
     number = unit * jnp.where(index < ROWS // 2, index, index - ROWS).astype(jnp.float32)
     along = number * number
     parts = []
-    for line in range(PLANES):
+    for line in range(lines):
         square = along + square_ref[pl.ds(line, 1), :]
         nonzero = square > 0
         inverse = jnp.where(nonzero, 4.0 * math.pi / jnp.where(nonzero, square, 1.0), 0.0)
         parts.append(lane(rows, line) * inverse)
     rows = from_left(left_ref[...], jnp.concatenate(parts, axis=1))
-    for line in range(PLANES):
-        for block in range(blocks):
-            out_ref[place_of(block, blocks), line] = lane(rows, line)[
-                block * PLANES : (block + 1) * PLANES
-            ]
+    for line in range(lines):
+        for block, place in enumerate(places):
+            out_ref[place, line] = lane(rows, line)[block * PLANES : (block + 1) * PLANES]
 
 
 def hartree_kernel(
@@ -679,10 +812,25 @@
     def exchange(array):
         return lax.all_to_all(array, AXES, 0, 0, axis_index_groups=groups, tiled=True)
 
+    def exchange_whole(array):
+        return lax.all_to_all(array, "fft", 0, 0, tiled=True)
+
     def exchange_all(array):
         return lax.all_to_all(
             array, AXES, 0, 0, axis_index_groups=[groups[0] + groups[1]], tiled=True
         )
+
+    def other_core(array):
+        return lax.ppermute(array, "ka", [(0, 1), (1, 0)])
+
+    def to_halves(keep, give):
+        sent = run(join_kernel, [(2,) + keep.shape], keep, other_core(give))
+        return exchange_all(sent.reshape((2 * blocks,) + keep.shape[1:]))
+
+    def from_halves(sent):
+        field = exchange_all(sent).reshape(2, blocks, 2, PLANES * QUARTER, ROWS)
+        give = lax.dynamic_index_in_dim(field, 1 - core, 0, keepdims=False)
+        return field, other_core(give)
 
     def move(array, pairs):
         return lax.ppermute(array, AXES, pairs)
@@ -711,13 +859,19 @@
     count_x = STEPS * SUB
 
     numbers = wave_numbers(lax.iota(jnp.int32, grid_size), grid_size)
-    own_numbers = wave_numbers(place * PLANES + lax.iota(jnp.int32, PLANES), grid_size)
-    squares = (own_numbers * own_numbers)[:, None] + (numbers * numbers)[None, :]
-
-    occupied = occupation.astype(jnp.float32) / 100.0
-    own_weight = lax.dynamic_slice_in_dim(kpoint_weight, side, 1)[0].astype(jnp.float32)
-    weight = own_weight / jnp.sum(kpoint_weight).astype(jnp.float32)
-    factor = (2.0 * weight * occupied).reshape(1, 1)
+    def squares_of(first, count):
+        own = wave_numbers(first + lax.iota(jnp.int32, count), grid_size)
+        return (own * own)[:, None] + (numbers * numbers)[None, :]
+
+    squares = squares_of(place * PLANES, PLANES)
+    squares_all = squares_of(fft_index * PLANES + core * QUARTER, QUARTER)
+
+    def factor_of(k_index):
+        own_weight = lax.dynamic_slice_in_dim(kpoint_weight, k_index, 1)[0].astype(jnp.float32)
+        weight = own_weight / jnp.sum(kpoint_weight).astype(jnp.float32)
+        return (2.0 * weight * occupation.astype(jnp.float32) / 100.0).reshape(1, 1)
+
+    factor, factor_all = factor_of(side), factor_of(core)
 
     keep, give, numbers_full = run(
         functools.partial(start_kernel, lattice_unit),
@@ -737,14 +891,7 @@
             pltpu.SemaphoreType.DMA((3,)),
         ],
     )
-    cores = [(0, 1), (1, 0)]
-    sent = run(
-        join_kernel,
-        [(2, blocks, 3, PLANES * QUARTER, ROWS)],
-        keep,
-        lax.ppermute(give, "ka", cores),
-    )
-    field = exchange_all(sent.reshape(2 * blocks, 3, PLANES * QUARTER, ROWS))
+    field = to_halves(keep, give)
     left_shape = jax.ShapeDtypeStruct((ROWS, 4 * ROWS), jnp.bfloat16)
     right_shape = jax.ShapeDtypeStruct((4 * ROWS, 2 * ROWS), jnp.bfloat16)
     made = run(
@@ -754,9 +901,9 @@
         numbers_full,
         line_pair,
     )
-    early = (squares, factor, jnp.stack([costate[0, 0, 0], costate[0, 0, 1], xc_kernel]))
-    field, made, early = lax.optimization_barrier((field, made, early))
-    squares, factor, moving = early
+    early = (squares, squares_all, factor, factor_all)
+    made, early = lax.optimization_barrier((made, early))
+    squares, squares_all, factor, factor_all = early
     tables = {1.0: made[0 : 2 * count_x + 2 : 2], -1.0: made[1 : 2 * count_x + 2 : 2]}
     right_z = {1.0: made[-2], -1.0: made[-1]}
 
@@ -787,8 +934,6 @@
         field,
         *tables_of(1.0, 1),
     )
-    sent, moving = lax.optimization_barrier((sent, moving))
-    moving = move(moving, regroup)
     sent, *waves_rows = run(
         functools.partial(second_mid_kernel, 1.0),
         [sent_shape, real_shape, real_shape],
@@ -796,9 +941,10 @@
         *tables_of(1.0, 2),
     )
     sent = middle(1.0, swap_field(sent), 3)
-    sent, moving = lax.optimization_barrier((sent, moving))
     kept = []
-    for count in range(4, count_x):
+    all_shape = (2 * blocks, 2, PLANES * QUARTER, ROWS)
+    keep_shape = (blocks, 2, PLANES * QUARTER, ROWS)
+    for count in range(4, count_x - 1):
         field = swap_field(sent)
         if count % SUB == 0:
             sent, *orbital = run(
@@ -811,53 +957,106 @@
             kept.append(orbital)
         else:
             sent = middle(1.0, field, count)
-    adjoint, xc_rows = [moving[0], moving[1]], moving[2]
+    sent = run(
+        functools.partial(last_mid_kernel, 1.0),
+        [all_shape],
+        swap_field(sent),
+        *waves_cols,
+        *tables_of(1.0, count_x - 1),
+    )
     *orbital, partial = run(
-        functools.partial(end_kernel, 1.0),
+        functools.partial(end_all_kernel, 1.0),
         [real_shape] * 3,
-        swap_field(sent),
-        *waves_rows,
+        *from_halves(sent),
+        potential,
         table_y(1.0),
-        *adjoint,
-        factor,
-    )
-    kept.append(orbital)
-
+        costate,
+        factor_all,
+    )
+
+    density, sent = run(
+        density_all_kernel,
+        [real_shape, (blocks, QUARTER * PLANES, ROWS)],
+        partial,
+        other_core(partial),
+        cas_left,
+        cas_right,
+        scratch=[pltpu.VMEM((blocks, PLANES * PLANES, ROWS), jnp.float32)],
+    )
+    field = exchange_whole(sent.reshape(blocks, QUARTER, PLANES, ROWS))
+    sent = run(
+        functools.partial(coulomb_kernel, lattice_unit, False),
+        [(blocks, QUARTER, PLANES, ROWS)],
+        field,
+        squares_all,
+        cas_left,
+    )
+    field = exchange_whole(sent)
+    field = field.reshape(blocks, QUARTER * PLANES, ROWS)
+    keep, give = run(
+        functools.partial(hartree_all_kernel, -1.0),
+        [keep_shape, keep_shape],
+        field,
+        other_core(field),
+        density,
+        xc_kernel,
+        *orbital,
+        costate,
+        potential,
+        cas_left,
+        cas_right,
+        table_y(-1.0),
+        right_z[-1.0],
+        scratch=[pltpu.VMEM((2, blocks, QUARTER * PLANES, ROWS), jnp.float32)],
+    )
+    sent = run(
+        functools.partial(all_mid_kernel, -1.0),
+        [sent_shape],
+        to_halves(keep, give),
+        *waves_cols,
+        *tables_of(-1.0, 1),
+    )
     for step_index in range(STEPS - 1, -1, -1):
-        density, sent = run(
-            density_kernel,
-            [real_shape, (blocks, PLANES * PLANES, ROWS)],
-            partial,
-            move(partial, across),
-            cas_left,
-            cas_right,
-        )
-        field = exchange(sent.reshape(blocks, PLANES, PLANES, ROWS))
-        sent = run(
-            functools.partial(coulomb_kernel, lattice_unit),
-            [(blocks, PLANES, PLANES, ROWS)],
-            field,
-            squares,
-            cas_left,
-        )
-        field = exchange(sent).reshape(blocks, PLANES * PLANES, ROWS)
-        sent, cross = run(
-            functools.partial(hartree_kernel, -1.0),
-            [sent_shape, real_shape],
-            field,
-            density,
-            xc_rows,
-            *kept[step_index],
-            *adjoint,
-            *waves_rows,
-            cas_left,
-            cas_right,
-            table_y(-1.0),
-            right_z[-1.0],
-        )
         first = (STEPS - 1 - step_index) * SUB
-        for count in range(first + 1, first + SUB - 1):
-            sent = middle(-1.0, swap_field(sent), count)
+        if step_index < STEPS - 1:
+            density, sent = run(
+                density_kernel,
+                [real_shape, (blocks, PLANES * PLANES, ROWS)],
+                partial,
+                move(partial, across),
+                cas_left,
+                cas_right,
+            )
+            field = exchange(sent.reshape(blocks, PLANES, PLANES, ROWS))
+            sent = run(
+                functools.partial(coulomb_kernel, lattice_unit, True),
+                [(blocks, PLANES, PLANES, ROWS)],
+                field,
+                squares,
+                cas_left,
+            )
+            field = exchange(sent).reshape(blocks, PLANES * PLANES, ROWS)
+            sent, cross = run(
+                functools.partial(hartree_kernel, -1.0),
+                [sent_shape, real_shape],
+                field,
+                density,
+                xc_rows,
+                *kept[step_index],
+                *adjoint,
+                *waves_rows,
+                cas_left,
+                cas_right,
+                table_y(-1.0),
+                right_z[-1.0],
+            )
+            sent = middle(-1.0, swap_field(sent), first + 1)
+            field = swap_field(sent)
+        else:
+            sent, xc_rows = lax.optimization_barrier((sent, xc_kernel))
+            field = swap_field(sent)
+            field, xc_rows = lax.optimization_barrier((field, move(xc_rows, regroup)))
+        sent = middle(-1.0, field, first + 2)
         field = swap_field(sent)
         if step_index > 0:
             sent = middle(-1.0, field, first + SUB - 1)
@@ -872,23 +1071,19 @@
             )
     sent = run(
         functools.partial(last_mid_kernel, -1.0),
-        [(2 * blocks, 2, PLANES * QUARTER, ROWS)],
+        [all_shape],
         field,
         *waves_cols,
         *tables_of(-1.0, count_x - 1),
     )
-    field = exchange_all(sent).reshape(2, blocks, 2, PLANES * QUARTER, ROWS)
-    give = lax.dynamic_index_in_dim(field, 1 - core, 0, keepdims=False)
     result = run(
         functools.partial(final_kernel, -1.0),
         [orbitals.shape],
-        field,
-        lax.ppermute(give, "ka", cores),
+        *from_halves(sent),
         potential,
         table_y(-1.0),
     )
-    beside = lax.ppermute(cross, "ka", [(0, 1), (1, 0)])
-    return (result, jnp.where(core == side, cross, beside))
+    return (result, jnp.where(core == side, cross, other_core(cross)))
 
 
 def solution(mesh):

time: 525 us -> 511 us (0.973)
  waiting for transfers between devices: 143 us -> 122 us
  blocking collectives: 272 us -> 282 us
    all_to_all x0 -> x3, blocking collectives: none -> 52.9 us  [the longest x1 28.4 us: exchange_all(): lax.all_to_all(array, AXES, 0, 0, axis_index_groups=[groups[0] + groups[1...]
    all_to_all x16 -> x13, blocking collectives: 272 us -> 229 us  [exchange(): lax.all_to_all(array, AXES, 0, 0, axis_index_groups=groups, tiled=True)]
    all_to_all x2 -> x1, waiting for transfers between devices: 30.2 us -> 0.01 us  [exchange(): lax.all_to_all(array, AXES, 0, 0, axis_index_groups=groups, tiled=True)]
    all_to_all x2 -> x3, waiting for transfers between devices: 50.5 us -> 72.7 us  [exchange_all(): lax.all_to_all(array, AXES, 0, 0, axis_index_groups=[groups[0] + groups[1...]
    ppermute x3 -> x2, waiting for transfers between devices: 59 us -> 40.5 us  [move(): return lax.ppermute(array, AXES, pairs)]
    ppermute x3 -> x7, waiting for transfers between devices: 2.75 us -> 8.52 us  [other_core(): return lax.ppermute(array, 'ka', [(0, 1), (1, 0)])]
    unnamed x84 -> x94, local copies, waits for them, and re-layouts: 13.3 us -> 17.5 us
    all_to_all x2 -> x3, starting transfers between devices: 11.3 us -> 13.4 us  [exchange_all(): lax.all_to_all(array, AXES, 0, 0, axis_index_groups=[groups[0] + groups[1...]
  transfers between devices with their start and end apart: 10 -> 13, of which waited for: 9 -> 11; matrix products, arithmetic and copies ran while one was open for 2% -> 1% of each run, Pallas kernels for 1% -> 1%
where the time goes in v5:
time: 511 us; the launch traced here: 502 us
  blocking collectives  282 us (55%)
  waiting for transfers between devices  122 us (24%)
  Pallas kernels  44.5 us (9%)
  starting transfers between devices  27.9 us (5%)
  local copies, waits for them, and re-layouts  20.1 us (4%)
    all_to_all x13, blocking collectives, exchange(): lax.all_to_all(array, AXES, 0, 0, axis_index_groups=groups, tiled=True)  229 us
    all_to_all x3, waiting for transfers between devices, exchange_all(): lax.all_to_all(array, AXES, 0, 0, axis_index_groups=[groups[0] + groups[1...  72.7 us
    pallas_call x26, Pallas kernels, run(): pl.pallas_call(kernel, out_shape=[jax.ShapeDtypeStruct(out, jnp.float32)...  44.5 us
    ppermute x2, waiting for transfers between devices, move(): return lax.ppermute(array, AXES, pairs)  40.5 us
    all_to_all x1, blocking collectives, exchange_all(): lax.all_to_all(array, AXES, 0, 0, axis_index_groups=[groups[0] + groups[1...  28.4 us
    all_to_all x2, blocking collectives, exchange_whole(): return lax.all_to_all(array, 'fft', 0, 0, tiled=True)  24.4 us
    unnamed x94, local copies, waits for them, and re-layouts  17.5 us
    all_to_all x3, starting transfers between devices, exchange_all(): lax.all_to_all(array, AXES, 0, 0, axis_index_groups=[groups[0] + groups[1...  13.4 us
  transfers between devices with their start and end apart: 13, of which 11 were waited for; matrix products, arithmetic and copies ran while one was open for 1% of the time, Pallas kernels for 1%

profile of v5, /device:TPU:1, one launch (start us, length us, event | category | flops | bytes accessed | tf_op | source)
XLA Modules:
  0.0 502.4 jit_solution(5199738265119746889)
XLA Ops:
  3.8 3.2 shard_map.122
  7.1 1.9 collective-permute-done.got_ref
  10.3 7.1 %all-to-all-start = ((f32[32,3,32,128]{3,2,1,0:T(8,128)}), f32[32,3,32,128]{3,2,1,0:T(8,128)S(1)}, u32[]{:S(2)}, u32[]{:S(2)}) async-start(f32[32,3,32,128]{3,2,1,0:T(8,128)} %bitcast), calls=%async_computation | async-start | bytes 3145728 | tf_op jit(solution)/shard_map/all_to_all | solution.py:819
  21.5 4.4 shard_map.124
  33.3 21.0 %all-to-all-done.field_ref = f32[32,3,32,128]{3,2,1,0:T(8,128)S(1)} async-done(((f32[32,3,32,128]{3,2,1,0:T(8,128)}), f32[32,3,32,128]{3,2,1,0:T(8,128)S(1)}, u32[]{:S(2)}, u32[]{:S(2)}) %all-to-all-start) | async-done | bytes 1572896 | tf_op jit(solution)/shard_map/all_to_all | solution.py:819
  56.9 2.3 shard_map.125
  59.1 24.9 %all_to_all.100.field_ref = f32[16,3,8,8,128]{4,3,2,1,0:T(8,128)S(1)} all-to-all(f32[16,3,8,8,128]{4,3,2,1,0:T(8,128)S(1)} %bitcast.42), channel_id=1, replica_groups={{0,1,16,17,2,3,18,19,4,5,20,21,6,7,22,23},{8,9,24,25,10,11,26,27,12,13,..., dimensions={0} | all-to-all | bytes 3145728 | tf_op jit(solution)/shard_map/all_to_all | solution.py:813
  84.1 2.1 shard_map.126
  86.2 17.8 %all_to_all.101.field_ref = f32[16,2,8,8,128]{4,3,2,1,0:T(8,128)S(1)} all-to-all(f32[16,2,8,8,128]{4,3,2,1,0:T(8,128)S(1)} %bitcast.46), channel_id=1, replica_groups={{0,1,16,17,2,3,18,19,4,5,20,21,6,7,22,23},{8,9,24,25,10,11,26,27,12,13,..., dimensions={0} | all-to-all | bytes 2097152 | tf_op jit(solution)/shard_map/all_to_all | solution.py:813
  104.0 1.6 shard_map.127
  105.6 17.6 %all_to_all.102.field_ref = f32[16,2,8,8,128]{4,3,2,1,0:T(8,128)S(1)} all-to-all(f32[16,2,8,8,128]{4,3,2,1,0:T(8,128)S(1)} %bitcast.33), channel_id=1, replica_groups={{0,1,16,17,2,3,18,19,4,5,20,21,6,7,22,23},{8,9,24,25,10,11,26,27,12,13,..., dimensions={0} | all-to-all | bytes 2097152 | tf_op jit(solution)/shard_map/all_to_all | solution.py:813
  123.3 1.8 shard_map.128
  125.1 17.8 %all_to_all.103.field_ref = f32[16,2,8,8,128]{4,3,2,1,0:T(8,128)S(1)} all-to-all(f32[16,2,8,8,128]{4,3,2,1,0:T(8,128)S(1)} %bitcast.47), channel_id=1, replica_groups={{0,1,16,17,2,3,18,19,4,5,20,21,6,7,22,23},{8,9,24,25,10,11,26,27,12,13,..., dimensions={0} | all-to-all | bytes 2097152 | tf_op jit(solution)/shard_map/all_to_all | solution.py:813
  142.9 1.6 shard_map.129
  144.5 17.6 %all_to_all.104.field_ref = f32[16,2,8,8,128]{4,3,2,1,0:T(8,128)S(1)} all-to-all(f32[16,2,8,8,128]{4,3,2,1,0:T(8,128)S(1)} %bitcast.34), channel_id=1, replica_groups={{0,1,16,17,2,3,18,19,4,5,20,21,6,7,22,23},{8,9,24,25,10,11,26,27,12,13,..., dimensions={0} | all-to-all | bytes 2097152 | tf_op jit(solution)/shard_map/all_to_all | solution.py:813
  162.2 1.6 shard_map.130
  163.8 17.8 %all_to_all.105.field_ref = f32[16,2,8,8,128]{4,3,2,1,0:T(8,128)S(1)} all-to-all(f32[16,2,8,8,128]{4,3,2,1,0:T(8,128)S(1)} %bitcast.38), channel_id=1, replica_groups={{0,1,16,17,2,3,18,19,4,5,20,21,6,7,22,23},{8,9,24,25,10,11,26,27,12,13,..., dimensions={0} | all-to-all | bytes 2097152 | tf_op jit(solution)/shard_map/all_to_all | solution.py:813
  181.6 1.6 shard_map.131
  184.2 3.7 all-to-all-start.7
  187.9 26.0 %all-to-all-done.7 = f32[32,2,32,128]{3,2,1,0:T(8,128)} async-done(((f32[32,2,32,128]{3,2,1,0:T(8,128)}), f32[32,2,32,128]{3,2,1,0:T(8,128)}, u32[]{:S(2)}, u32[]{:S(2)}) %all-to-all-start.7) | async-done | bytes 1048608 | tf_op jit(solution)/shard_map/all_to_all | solution.py:819
  217.2 2.3 shard_map.132
  222.2 12.5 %all_to_all.106.field_ref = f32[16,4,8,128]{3,2,1,0:T(8,128)S(1)} all-to-all(f32[16,4,8,128]{3,2,1,0:T(8,128)S(1)} %bitcast.49), channel_id=1, replica_groups=mesh['ka'=2,'fft'=16] {'fft'}, dimensions={0} | all-to-all | bytes 524288 | tf_op jit(solution)/shard_map/all_to_all | solution.py:816
  235.2 11.9 %all_to_all.107 = f32[16,4,8,128]{3,2,1,0:T(8,128)S(1)} all-to-all(f32[16,4,8,128]{3,2,1,0:T(8,128)S(1)} %shard_map.134), channel_id=1, replica_groups=mesh['ka'=2,'fft'=16] {'fft'}, dimensions={0} | all-to-all | bytes 524288 | tf_op jit(solution)/shard_map/all_to_all | solution.py:816
  247.1 3.3 collective-permute-start.3
  251.5 2.5 shard_map.135
  254.4 1.5 collective-permute-done.4.got_ref
  256.1 28.4 %all_to_all.108.field_ref = f32[32,2,32,128]{3,2,1,0:T(8,128)S(1)} all-to-all(f32[32,2,32,128]{3,2,1,0:T(8,128)S(1)} %bitcast.40), channel_id=1, replica_groups={{0,1,16,17,2,3,18,19,4,5,20,21,6,7,22,23,8,9,24,25,10,11,26,27,12,13,28..., dimensions={0} | all-to-all | bytes 2097152 | tf_op jit(solution)/shard_map/all_to_all | solution.py:819
  284.5 1.7 shard_map.137
  287.2 4.6 all-to-all-start.11
  291.8 3.5 collective-permute-start.5
  295.3 15.2 %collective-permute-done.5.xc_ref = f32[8,128,128]{2,1,0:T(8,128)S(1)} collective-permute-done((f32[8,128,128]{2,1,0:T(8,128)}, f32[8,128,128]{2,1,0:T(8,128)S(1)}, u32[]{:S(2)}, u32[]{:S(2)}) %collective-permute-start.5) | collective-permute-done | bytes 524320 | tf_op jit(solution)/shard_map/ppermute | solution.py:836
  311.2 2.9 shard_map.138
  314.1 20.4 %all_to_all.109.field_ref = f32[16,2,8,8,128]{4,3,2,1,0:T(8,128)S(1)} all-to-all(f32[16,2,8,8,128]{4,3,2,1,0:T(8,128)S(1)} %bitcast.39), channel_id=1, replica_groups={{0,1,16,17,2,3,18,19,4,5,20,21,6,7,22,23},{8,9,24,25,10,11,26,27,12,13,..., dimensions={0} | all-to-all | bytes 2097152 | tf_op jit(solution)/shard_map/all_to_all | solution.py:813
  334.5 1.6 shard_map.139
  336.2 17.8 %all_to_all.110.field_ref = f32[16,2,8,8,128]{4,3,2,1,0:T(8,128)S(1)} all-to-all(f32[16,2,8,8,128]{4,3,2,1,0:T(8,128)S(1)} %bitcast.35), channel_id=1, replica_groups={{0,1,16,17,2,3,18,19,4,5,20,21,6,7,22,23},{8,9,24,25,10,11,26,27,12,13,..., dimensions={0} | all-to-all | bytes 2097152 | tf_op jit(solution)/shard_map/all_to_all | solution.py:813
  355.3 25.4 %collective-permute-done.6.other_ref = f32[8,128,128]{2,1,0:T(8,128)S(1)} collective-permute-done((f32[8,128,128]{2,1,0:T(8,128)S(1)}, f32[8,128,128]{2,1,0:T(8,128)S(1)}, u32[]{:S(2)}, u32[]{:S(2)}) %collective-permute-start.6) | collective-permute-done | bytes 524320 | tf_op jit(solution)/shard_map/ppermute | solution.py:836
  381.4 12.5 %all_to_all.111.field_ref = f32[16,8,8,128]{3,2,1,0:T(8,128)S(1)} all-to-all(f32[16,8,8,128]{3,2,1,0:T(8,128)S(1)} %bitcast.48), channel_id=1, replica_groups={{0,1,16,17,2,3,18,19,4,5,20,21,6,7,22,23},{8,9,24,25,10,11,26,27,12,13,..., dimensions={0} | all-to-all | bytes 1048576 | tf_op jit(solution)/shard_map/all_to_all | solution.py:813
  394.5 12.0 %all_to_all.112 = f32[16,8,8,128]{3,2,1,0:T(8,128)S(1)} all-to-all(f32[16,8,8,128]{3,2,1,0:T(8,128)S(1)} %shard_map.142), channel_id=1, replica_groups={{0,1,16,17,2,3,18,19,4,5,20,21,6,7,22,23},{8,9,24,25,10,11,26,27,12,13,..., dimensions={0} | all-to-all | bytes 1048576 | tf_op jit(solution)/shard_map/all_to_all | solution.py:813
  406.4 2.0 shard_map.143
  409.2 17.8 %all_to_all.113.field_ref = f32[16,2,8,8,128]{4,3,2,1,0:T(8,128)S(1)} all-to-all(f32[16,2,8,8,128]{4,3,2,1,0:T(8,128)S(1)} %bitcast.45), channel_id=1, replica_groups={{0,1,16,17,2,3,18,19,4,5,20,21,6,7,22,23},{8,9,24,25,10,11,26,27,12,13,..., dimensions={0} | all-to-all | bytes 2097152 | tf_op jit(solution)/shard_map/all_to_all | solution.py:813
  427.0 1.6 shard_map.144
  428.6 17.6 %all_to_all.114.field_ref = f32[16,2,8,8,128]{4,3,2,1,0:T(8,128)S(1)} all-to-all(f32[16,2,8,8,128]{4,3,2,1,0:T(8,128)S(1)} %bitcast.36), channel_id=1, replica_groups={{0,1,16,17,2,3,18,19,4,5,20,21,6,7,22,23},{8,9,24,25,10,11,26,27,12,13,..., dimensions={0} | all-to-all | bytes 2097152 | tf_op jit(solution)/shard_map/all_to_all | solution.py:813
  446.3 1.6 shard_map.145
  447.9 17.7 %all_to_all.115.field_ref = f32[16,2,8,8,128]{4,3,2,1,0:T(8,128)S(1)} all-to-all(f32[16,2,8,8,128]{4,3,2,1,0:T(8,128)S(1)} %bitcast.37), channel_id=1, replica_groups={{0,1,16,17,2,3,18,19,4,5,20,21,6,7,22,23},{8,9,24,25,10,11,26,27,12,13,..., dimensions={0} | all-to-all | bytes 2097152 | tf_op jit(solution)/shard_map/all_to_all | solution.py:813
  465.6 1.6 shard_map.146
  468.2 2.6 all-to-all-start.19
  471.3 25.7 %all-to-all-done.19 = f32[32,2,32,128]{3,2,1,0:T(8,128)S(1)} async-done(((f32[32,2,32,128]{3,2,1,0:T(8,128)}), f32[32,2,32,128]{3,2,1,0:T(8,128)S(1)}, u32[]{:S(2)}, u32[]{:S(2)}) %all-to-all-start.19) | async-done | bytes 1048608 | tf_op jit(solution)/shard_map/all_to_all | solution.py:819
  500.0 2.0 shard_map.147
  (126 shorter events, 34.5 us)
Async XLA Ops:
  0.6 1.0 copy-start
  1.7 1.2 copy-start.14
  2.9 0.9 copy-start.20
  7.0 2.0 collective-permute-start
  10.3 7.8 %copy-start.44 = (s32[2]{0:T(128)S(1)}, s32[2]{0:T(128)}, u32[]{:S(2)}) copy-start(s32[2]{0:T(128)} %param.16) | copy-start | bytes 28
  10.3 11.1 %copy-start.45 = (f32[8]{0:T(128)S(1)}, f32[8]{0:T(128)}, u32[]{:S(2)}) copy-start(f32[8]{0:T(128)} %param.15) | copy-start | bytes 100
  10.3 11.1 %copy-start.46 = (f32[2]{0:T(128)S(1)}, f32[2]{0:T(128)}, u32[]{:S(2)}) copy-start(f32[2]{0:T(128)} %constant.86.clone) | copy-start | bytes 28
  10.3 11.2 %copy-start.21 = (f32[128,256]{1,0:T(8,128)S(1)}, f32[128,256]{1,0:T(8,128)}, u32[]{:S(2)}) copy-start(f32[128,256]{1,0:T(8,128)} %constant.83.clone.lines_ref) | copy-start | bytes 393220
  10.3 44.0 %all-to-all-start = ((f32[32,3,32,128]{3,2,1,0:T(8,128)}), f32[32,3,32,128]{3,2,1,0:T(8,128)S(1)}, u32[]{:S(2)}, u32[]{:S(2)}) async-start(f32[32,3,32,128]{3,2,1,0:T(8,128)} %bitcast), calls=%async_computation | async-start | bytes 3145728 | tf_op jit(solution)/shard_map/all_to_all | solution.py:819
  54.3 1.2 copy-start.2
  55.5 1.4 copy-start.3
  86.2 17.8 %copy-start.41 = (bf16[128,512]{1,0:T(8,128)(2,1)S(1)}, bf16[128,512]{1,0:T(8,128)(2,1)}, u32[]{:S(2)}) copy-start(bf16[128,512]{1,0:T(8,128)(2,1)} %copy-done.40) | copy-start | bytes 393220
  86.2 17.8 %copy-start.43 = (bf16[128,512]{1,0:T(8,128)(2,1)S(1)}, bf16[128,512]{1,0:T(8,128)(2,1)}, u32[]{:S(2)}) copy-start(bf16[128,512]{1,0:T(8,128)(2,1)} %copy-done.42) | copy-start | bytes 393220
  125.1 19.5 %copy-start.9 = (f32[8,128,128]{2,1,0:T(8,128)}, f32[8,128,128]{2,1,0:T(8,128)S(1)}, u32[]{:S(2)}) copy-start(f32[8,128,128]{2,1,0:T(8,128)S(1)} %get-tuple-element.134.other_real_ref.orbital_real_ref) | copy-start | bytes 1572868
  125.1 19.5 %copy-start.11 = (f32[8,128,128]{2,1,0:T(8,128)}, f32[8,128,128]{2,1,0:T(8,128)S(1)}, u32[]{:S(2)}) copy-start(f32[8,128,128]{2,1,0:T(8,128)S(1)} %get-tuple-element.135.other_imag_ref.orbital_imag_ref) | copy-start | bytes 1572868
  125.1 17.8 %copy-start.37 = (bf16[128,512]{1,0:T(8,128)(2,1)S(1)}, bf16[128,512]{1,0:T(8,128)(2,1)}, u32[]{:S(2)}) copy-start(bf16[128,512]{1,0:T(8,128)(2,1)} %copy-done.36) | copy-start | bytes 393220
  125.1 17.8 %copy-start.39 = (bf16[128,512]{1,0:T(8,128)(2,1)S(1)}, bf16[128,512]{1,0:T(8,128)(2,1)}, u32[]{:S(2)}) copy-start(bf16[128,512]{1,0:T(8,128)(2,1)} %copy-done.38) | copy-start | bytes 393220
  163.8 17.8 %copy-start.35 = (bf16[128,512]{1,0:T(8,128)(2,1)S(1)}, bf16[128,512]{1,0:T(8,128)(2,1)}, u32[]{:S(2)}) copy-start(bf16[128,512]{1,0:T(8,128)(2,1)} %copy-done.34) | copy-start | bytes 393220
  183.2 1.0 copy-start.4
  184.2 33.0 %copy-start.1 = (f32[8,128,128]{2,1,0:T(8,128)S(1)}, f32[8,128,128]{2,1,0:T(8,128)}, u32[]{:S(2)}) copy-start(f32[8,128,128]{2,1,0:T(8,128)} %pot_ref.7) | copy-start | bytes 1572868
  184.2 29.7 %all-to-all-start.7 = ((f32[32,2,32,128]{3,2,1,0:T(8,128)}), f32[32,2,32,128]{3,2,1,0:T(8,128)}, u32[]{:S(2)}, u32[]{:S(2)}) async-start(f32[32,2,32,128]{3,2,1,0:T(8,128)} %copy-done.4), calls=%async_computation.7 | async-start | bytes 2097152 | tf_op jit(solution)/shard_map/all_to_all | solution.py:819
  213.9 3.3 copy-start.7
  215.1 6.4 %copy-start.8 = (bf16[128,256]{1,0:T(8,128)(2,1)S(1)}, bf16[128,256]{1,0:T(8,128)(2,1)}, u32[]{:S(2)}) copy-start(bf16[128,256]{1,0:T(8,128)(2,1)} %constant.84.clone.left_ref.cas_left_ref) | copy-start | bytes 196612
  215.1 6.4 %copy-start.13 = (bf16[256,128]{1,0:T(8,128)(2,1)S(1)}, bf16[256,128]{1,0:T(8,128)(2,1)}, u32[]{:S(2)}) copy-start(bf16[256,128]{1,0:T(8,128)(2,1)} %constant.85.clone.right_ref.cas_right_ref) | copy-start | bytes 196612
  215.1 2.1 collective-permute-start.1
  219.5 32.0 %copy-start.15 = (f32[8,128,128]{2,1,0:T(8,128)S(1)}, f32[8,128,128]{2,1,0:T(8,128)}, u32[]{:S(2)}) copy-start(f32[8,128,128]{2,1,0:T(8,128)} %xc_ref.1) | copy-start | bytes 1572868
  219.5 2.0 collective-permute-start.2
  247.1 4.5 collective-permute-start.3
  254.0 2.0 collective-permute-start.4
  256.1 28.5 %copy-start.31 = (bf16[128,512]{1,0:T(8,128)(2,1)S(1)}, bf16[128,512]{1,0:T(8,128)(2,1)}, u32[]{:S(2)}) copy-start(bf16[128,512]{1,0:T(8,128)(2,1)} %copy-done.30) | copy-start | bytes 393220
  256.1 28.5 %copy-start.33 = (bf16[128,512]{1,0:T(8,128)(2,1)S(1)}, bf16[128,512]{1,0:T(8,128)(2,1)}, u32[]{:S(2)}) copy-start(bf16[128,512]{1,0:T(8,128)(2,1)} %copy-done.32) | copy-start | bytes 393220
  286.2 1.0 copy-start.6
  287.2 24.0 %all-to-all-start.11 = ((f32[16,2,8,8,128]{4,3,2,1,0:T(8,128)}), f32[16,2,8,8,128]{4,3,2,1,0:T(8,128)}, u32[]{:S(2)}, u32[]{:S(2)}) async-start(f32[16,2,8,8,128]{4,3,2,1,0:T(8,128)} %bitcast.32), calls=%async_computation.11 | async-start | bytes 2097152 | tf_op jit(solution)/shard_map/all_to_all | solution.py:813
  291.8 18.7 %collective-permute-start.5 = (f32[8,128,128]{2,1,0:T(8,128)}, f32[8,128,128]{2,1,0:T(8,128)S(1)}, u32[]{:S(2)}, u32[]{:S(2)}) collective-permute-start(f32[8,128,128]{2,1,0:T(8,128)} %xc_ref.1), channel_id=1, source_target_pairs={{0,0},{1,1},{2,2},{3,3},{4,4},{5,5},{6,6},{7,7},{8,16},{9,17},{10,... | collective-permute-start | bytes 1572872 | tf_op jit(solution)/shard_map/ppermute | solution.py:836
  310.4 0.8 copy-start.16
  314.1 20.4 %copy-start.27 = (bf16[128,512]{1,0:T(8,128)(2,1)S(1)}, bf16[128,512]{1,0:T(8,128)(2,1)}, u32[]{:S(2)}) copy-start(bf16[128,512]{1,0:T(8,128)(2,1)} %copy-done.26) | copy-start | bytes 393220
  314.1 20.4 %copy-start.29 = (bf16[128,512]{1,0:T(8,128)(2,1)S(1)}, bf16[128,512]{1,0:T(8,128)(2,1)}, u32[]{:S(2)}) copy-start(bf16[128,512]{1,0:T(8,128)(2,1)} %copy-done.28) | copy-start | bytes 393220
  336.1 17.8 %copy-start.10 = (f32[8,128,128]{2,1,0:T(8,128)S(1)}, f32[8,128,128]{2,1,0:T(8,128)}, u32[]{:S(2)}) copy-start(f32[8,128,128]{2,1,0:T(8,128)} %copy-done.9) | copy-start | bytes 1572868
  336.2 17.8 %copy-start.12 = (f32[8,128,128]{2,1,0:T(8,128)S(1)}, f32[8,128,128]{2,1,0:T(8,128)}, u32[]{:S(2)}) copy-start(f32[8,128,128]{2,1,0:T(8,128)} %copy-done.11) | copy-start | bytes 1572868
  354.7 26.0 %collective-permute-start.6 = (f32[8,128,128]{2,1,0:T(8,128)S(1)}, f32[8,128,128]{2,1,0:T(8,128)S(1)}, u32[]{:S(2)}, u32[]{:S(2)}) collective-permute-start(f32[8,128,128]{2,1,0:T(8,128)S(1)} %get-tuple-element.137.own_ref), channel_id=1, source_target_pairs={{0,8},{1,9},{2,10},{3,11},{4,12},{5,13},{6,14},{7,15},{8,0},{9,1},... | collective-permute-start | bytes 1572872 | tf_op jit(solution)/shard_map/ppermute | solution.py:836
  381.4 25.1 %copy-start.17 = (f32[8,128,128]{2,1,0:T(8,128)S(1)}, f32[8,128,128]{2,1,0:T(8,128)}, u32[]{:S(2)}) copy-start(f32[8,128,128]{2,1,0:T(8,128)} %copy-done.16) | copy-start | bytes 1572868
  409.2 17.8 %copy-start.23 = (bf16[128,512]{1,0:T(8,128)(2,1)S(1)}, bf16[128,512]{1,0:T(8,128)(2,1)}, u32[]{:S(2)}) copy-start(bf16[128,512]{1,0:T(8,128)(2,1)} %copy-done.22) | copy-start | bytes 393220
  409.2 17.8 %copy-start.25 = (bf16[128,512]{1,0:T(8,128)(2,1)S(1)}, bf16[128,512]{1,0:T(8,128)(2,1)}, u32[]{:S(2)}) copy-start(bf16[128,512]{1,0:T(8,128)(2,1)} %copy-done.24) | copy-start | bytes 393220
  467.2 1.0 copy-start.5
  468.2 2.6 copy-start.19
  468.2 28.8 %all-to-all-start.19 = ((f32[32,2,32,128]{3,2,1,0:T(8,128)}), f32[32,2,32,128]{3,2,1,0:T(8,128)S(1)}, u32[]{:S(2)}, u32[]{:S(2)}) async-start(f32[32,2,32,128]{3,2,1,0:T(8,128)} %copy-done.5), calls=%async_computation.19 | async-start | bytes 2097152 | tf_op jit(solution)/shard_map/all_to_all | solution.py:819
  470.8 27.4 %collective-permute-start.8 = (f32[8,128,128]{2,1,0:T(8,128)S(1)}, f32[8,128,128]{2,1,0:T(8,128)S(1)}, u32[]{:S(2)}, u32[]{:S(2)}) collective-permute-start(f32[8,128,128]{2,1,0:T(8,128)S(1)} %copy-done.19), channel_id=1, source_target_pairs={{0,16},{16,0},{1,17},{17,1},{2,18},{18,2},{3,19},{19,3},{4,20},{20... | collective-permute-start | bytes 1572872 | tf_op jit(solution)/shard_map/ppermute | solution.py:824
  497.8 2.2 collective-permute-start.7
  (12 other events, 8.0 us)

commit v6 on v5

--- a/solution.py
+++ b/solution.py
@@ -224,15 +224,29 @@
     )
 
 
-def table_kernel(count_x, shift_ref, numbers_ref, lines_ref, *out_refs):
-    numbers, cosine, sine = numbers_ref[...], lines_ref[:, :ROWS], lines_ref[:, ROWS:]
-    for line in range(count_x + 1):
+def table_kernel(shift_ref, lines_ref, *out_refs):
+    numbers = wave_numbers(lax.broadcasted_iota(jnp.int32, (ROWS, ROWS), 0), ROWS)
+    cosine, sine = lines_ref[:, :ROWS], lines_ref[:, ROWS:]
+    for line in range(len(out_refs) // 2):
         matrix, turned = circulant(shift_ref[line], numbers, cosine, sine)
         out_refs[2 * line][...] = side_by_side(matrix, 1)
         out_refs[2 * line + 1][...] = side_by_side(turned, 1)
-    matrix, turned = circulant(shift_ref[count_x + 1], numbers, cosine, sine)
-    out_refs[2 * count_x + 2][...] = side_by_side(whole_matrix(turned), 0)
-    out_refs[2 * count_x + 3][...] = side_by_side(whole_matrix(matrix), 0)
+
+
+def constant_circulant(shift, grid_size):
+    grid_line = np.arange(grid_size)
+    signed_line = np.where(grid_line < grid_size // 2, grid_line, grid_line - grid_size)
+    along = shift + 2.0 * math.pi / (grid_size * spacing) * signed_line
+    waves = np.exp(2j * np.pi / grid_size * (np.outer(grid_line, grid_line) % grid_size))
+    line = (waves * np.exp(-0.5j * sub_time * along * along)) @ waves.conj() / grid_size
+    whole = np.block([[line.real, -line.imag], [line.imag, line.real]])
+    return whole, whole.T
+
+
+def constant_table(matrix, axis):
+    high = matrix.astype(jnp.bfloat16)
+    low = (matrix - high.astype(np.float64)).astype(jnp.bfloat16)
+    return jnp.asarray(np.concatenate([high, low], axis=axis))
 
 
 def cos_sin(angle):
@@ -284,10 +298,16 @@
     return value[:, plane * ROWS : (plane + 1) * ROWS]
 
 
+def core_place(block, blocks):
+    core, chip = divmod(block, blocks // 2)
+    bits = (blocks // 2).bit_length() - 1
+    return core, sum((chip >> bit & 1) << (bits - 1 - bit) for bit in range(bits))
+
+
 def sources_of(blocks):
     half = blocks // 2
     return [
-        block // half * blocks + place_of(core * half + block % half, blocks)
+        (core * 2 + block // half) * half + core_place(block % half, blocks)[1]
         for block in range(blocks)
         for core in range(2)
     ]
@@ -310,7 +330,7 @@
     rows = jnp.concatenate(
         [
             jnp.concatenate([lane(real_part, plane), lane(imag_part, plane)], axis=1)
-            for plane in range(PLANES)
+            for plane in range(real_part.shape[1] // ROWS)
         ],
         axis=0,
     )
@@ -445,70 +465,66 @@
     ]
 
 
-def put_rows(ref, part, plane, piece):
-    blocks = ref.shape[0]
-    for block in range(blocks):
-        ref[place_of(block, blocks), part, pl.ds(plane, PLANES, stride=QUARTER), :] = piece[
-            block * PLANES : (block + 1) * PLANES
-        ]
-
-
-def begin_all(sign, real_part, imag_part, cosine, sine, second, right, keep_ref, give_ref):
+def begin_some(sign, real_part, imag_part, cosine, sine, second, right, out_ref):
     real_part, imag_part = rotated(sign, real_part, imag_part, cosine, sine)
     field = from_left(second, jnp.concatenate([real_part, imag_part], axis=0))
     turned = turn_z(field[:ROWS], field[ROWS:], right)
-    for number in range(PLANES):
-        ref = keep_ref if number < QUARTER else give_ref
+    for number in range(QUARTER):
         for part in range(2):
             piece = turned[number * ROWS : (number + 1) * ROWS, part * ROWS : (part + 1) * ROWS]
-            put_rows(ref, part, number % QUARTER, piece)
+            put_rows(out_ref, (part,), number, piece)
+
+
+def put_rows(ref, index, number, piece):
+    blocks = ROWS // PLANES
+    for block in range(blocks):
+        at = core_place(block, blocks) + index
+        ref[at + (pl.ds(number, PLANES, stride=QUARTER), slice(None))] = piece[
+            block * PLANES : (block + 1) * PLANES
+        ]
 
 
 def start_kernel(
-    unit, field_ref, pot_ref, lines_ref, keep_ref, give_ref, numbers_ref, field, pot, lines, sems
+    given, field_ref, pot_ref, second_ref, right_ref, out_ref, field, pot, second, right, sems
 ):
     copies = [
         pltpu.make_async_copy(source, target, sems.at[number])
         for number, (source, target) in enumerate(
-            ((lines_ref, lines), (pot_ref, pot), (field_ref, field))
+            ((pot_ref, pot), (field_ref, field), (second_ref, second), (right_ref, right))
         )
     ]
     for copy in copies:
         copy.start()
-    order = plane_order(lax.axis_index("ka"))
-    index = lax.broadcasted_iota(jnp.int32, (ROWS, ROWS), 0)
-    numbers = wave_numbers(index, ROWS)
-    numbers_ref[...] = numbers
+    order = plane_order(lax.axis_index("ka"))[given * QUARTER : (given + 1) * QUARTER]
     copies[0].wait()
-    cosine_line, sine_line = lines[:, :ROWS], lines[:, ROWS:]
-    table_y = circulant(0.25 * unit, numbers, cosine_line, sine_line)[0]
-    table_z = circulant(-0.25 * unit, numbers, cosine_line, sine_line)[1]
-    copies[1].wait()
-    for number in range(QUARTER):
-        put_rows(keep_ref, 2, number, pot[order[number]])
+    if out_ref.shape[2] > 2:
+        for number, plane in enumerate(order):
+            put_rows(out_ref, (2,), number, pot[plane])
     cosine, sine = cos_sin(
         0.5 * sub_time * jnp.concatenate([pot[plane] for plane in order], axis=1)
     )
-    copies[2].wait()
-    begin_all(
+    for copy in copies[1:]:
+        copy.wait()
+    begin_some(
         1.0,
         jnp.concatenate([field[0, 0, 0, plane] for plane in order], axis=1),
         jnp.concatenate([field[0, 0, 1, plane] for plane in order], axis=1),
         cosine,
         sine,
-        side_by_side(whole_matrix(table_y), 1),
-        side_by_side(whole_matrix(table_z), 0),
-        keep_ref,
-        give_ref,
+        whole_left(second[...]),
+        right[...],
+        out_ref,
     )
 
 
 def join_kernel(keep_ref, got_ref, out_ref):
     core = lax.axis_index("ka")
-    out_ref[core] = keep_ref[...]
-    out_ref[1 - core, :, 0:2] = got_ref[...]
-    if keep_ref.shape[1] > 2:
-        out_ref[1 - core, :, 2] = keep_ref[:, 2]
+    parts = got_ref.shape[2]
+    for to in range(2):
+        out_ref[to, core] = keep_ref[to]
+        out_ref[to, 1 - core, :, 0:parts] = got_ref[to]
+        if keep_ref.shape[2] > parts:
+            out_ref[to, 1 - core, :, parts] = keep_ref[to, :, parts]
 
 
 def end_kernel(
@@ -539,17 +555,15 @@
 def finish_all(sign, field_ref, got_ref, pot_ref, first_ref):
     core = lax.axis_index("ka")
     order = plane_order(core)
-    blocks = got_ref.shape[0]
+    blocks = ROWS // PLANES
 
     def part_of(part):
         planes = []
         for number in range(PLANES):
             at = (part, pl.ds(number % QUARTER * PLANES, PLANES), slice(None))
             rows = [
-                field_ref[(core, place_of(block, blocks)) + at]
-                if number < QUARTER
-                else got_ref[(place_of(block, blocks),) + at]
-                for block in range(blocks)
+                field_ref[(to, core, chip) + at] if number < QUARTER else got_ref[(to, chip) + at]
+                for to, chip in (core_place(block, blocks) for block in range(blocks))
             ]
             planes.append(jnp.concatenate(rows, axis=0))
         return jnp.concatenate(planes, axis=1)
@@ -612,6 +626,7 @@
 
 def hartree_all_kernel(
     sign,
+    given,
     field_ref,
     got_ref,
     density_ref,
@@ -624,11 +639,11 @@
     cas_right_ref,
     second_ref,
     right_ref,
-    keep_ref,
-    give_ref,
+    out_ref,
     rows_ref,
 ):
     core = lax.axis_index("ka")
+    order = plane_order(core)[given * QUARTER : (given + 1) * QUARTER]
     rows_ref[core] = field_ref[...]
     rows_ref[1 - core] = got_ref[...]
     spectrum = jnp.concatenate(
@@ -641,23 +656,18 @@
                 ],
                 axis=0,
             )
-            for plane in range(PLANES)
+            for plane in order
         ],
         axis=1,
     )
     hartree = from_right(
         stack_planes(from_left(cas_left_ref[...], spectrum)), cas_right_ref[...]
     )
-    for plane in range(PLANES):
-        rows_ref[plane // QUARTER, pl.ds(plane % QUARTER * QUARTER, QUARTER)] = (
-            hartree[plane * ROWS : (plane + 1) * ROWS]
-        ).reshape(QUARTER, QUARTER * PLANES, ROWS)
-    order = plane_order(core)
     real_parts, imag_parts = [], []
     for number, plane in enumerate(order):
-        at = core if number < QUARTER else 1 - core
-        own = rows_ref[at, pl.ds(number % QUARTER * QUARTER, QUARTER)].reshape(ROWS, ROWS)
-        cross = own + xc_ref[plane] * density_ref[plane]
+        cross = (
+            hartree[number * ROWS : (number + 1) * ROWS] + xc_ref[plane] * density_ref[plane]
+        )
         real_parts.append(
             adjoint_ref[0, 0, 0, plane] + step_time * cross * orbital_imag_ref[plane]
         )
@@ -667,7 +677,7 @@
     cosine, sine = cos_sin(
         0.5 * sub_time * jnp.concatenate([pot_ref[plane] for plane in order], axis=1)
     )
-    begin_all(
+    begin_some(
         sign,
         jnp.concatenate(real_parts, axis=1),
         jnp.concatenate(imag_parts, axis=1),
@@ -675,13 +685,13 @@
         sine,
         whole_left(second_ref[...]),
         right_ref[...],
-        keep_ref,
-        give_ref,
+        out_ref,
     )
 
 
 def stack_planes(value):
-    return jnp.concatenate([lane(value, plane) for plane in range(PLANES)], axis=0)
+    planes = value.shape[1] // ROWS
+    return jnp.concatenate([lane(value, plane) for plane in range(planes)], axis=0)
 
 
 def density_kernel(own_ref, other_ref, left_ref, right_ref, density_ref, out_ref):
@@ -800,6 +810,9 @@
         for block, device in enumerate(devices):
             group[place_of(block, blocks)] = device
         groups.append(group)
+    everyone = [0] * (2 * blocks)
+    for number, source in enumerate(sources_of(blocks)):
+        everyone[source] = number % 2 * blocks + number // 2
     regroup = []
     for c in range(2):
         for f in range(blocks):
@@ -817,19 +830,21 @@
 
     def exchange_all(array):
         return lax.all_to_all(
-            array, AXES, 0, 0, axis_index_groups=[groups[0] + groups[1]], tiled=True
+            array, AXES, 0, 0, axis_index_groups=[everyone], tiled=True
         )
 
     def other_core(array):
         return lax.ppermute(array, "ka", [(0, 1), (1, 0)])
 
-    def to_halves(keep, give):
-        sent = run(join_kernel, [(2,) + keep.shape], keep, other_core(give))
-        return exchange_all(sent.reshape((2 * blocks,) + keep.shape[1:]))
+    def joined(keep, give):
+        return run(join_kernel, [(2,) + keep.shape], keep, other_core(give))
+
+    def to_halves(sent):
+        return exchange_all(sent.reshape((2 * blocks,) + sent.shape[3:]))
 
     def from_halves(sent):
-        field = exchange_all(sent).reshape(2, blocks, 2, PLANES * QUARTER, ROWS)
-        give = lax.dynamic_index_in_dim(field, 1 - core, 0, keepdims=False)
+        field = exchange_all(sent).reshape(2, 2, half, 2, PLANES * QUARTER, ROWS)
+        give = lax.dynamic_index_in_dim(field, 1 - core, 1, keepdims=False)
         return field, other_core(give)
 
     def move(array, pairs):
@@ -849,13 +864,13 @@
         np.concatenate([np.cos(angles), np.sin(angles)], axis=1).astype(np.float32)
     )
     cas = (np.cos(angles) + np.sin(angles)) / math.sqrt(grid_size)
-    cas_high = cas.astype(jnp.bfloat16)
-    cas_low = (cas - cas_high.astype(np.float64)).astype(jnp.bfloat16)
-    cas_left = jnp.asarray(np.concatenate([cas_high, cas_low], axis=1))
-    cas_right = jnp.asarray(np.concatenate([cas_high, cas_low], axis=0))
+    cas_left, cas_right = constant_table(cas, 1), constant_table(cas, 0)
+    line_y = constant_circulant(0.25 * lattice_unit, grid_size)
+    line_z = constant_circulant(-0.25 * lattice_unit, grid_size)
+    tables_y = {1.0: constant_table(line_y[0][:ROWS], 1), -1.0: constant_table(line_y[1][:ROWS], 1)}
+    right_z = {1.0: constant_table(line_z[1], 0), -1.0: constant_table(line_z[0], 0)}
 
     shift_x = lattice_unit * ((side.astype(jnp.float32) + 0.5) / 2 - 0.5) + vector_potential
-    shift_yz = jnp.array([lattice_unit * 0.25, -lattice_unit * 0.25], jnp.float32)
     count_x = STEPS * SUB
 
     numbers = wave_numbers(lax.iota(jnp.int32, grid_size), grid_size)
@@ -873,45 +888,44 @@
 
     factor, factor_all = factor_of(side), factor_of(core)
 
-    keep, give, numbers_full = run(
-        functools.partial(start_kernel, lattice_unit),
-        [
-            (blocks, 3, PLANES * QUARTER, ROWS),
-            (blocks, 2, PLANES * QUARTER, ROWS),
-            (ROWS, ROWS),
-        ],
-        orbitals,
-        potential,
-        line_pair,
-        space=pltpu.HBM,
-        scratch=[
-            pltpu.VMEM(orbitals.shape, jnp.float32),
-            pltpu.VMEM(real_shape, jnp.float32),
-            pltpu.VMEM((ROWS, 2 * ROWS), jnp.float32),
-            pltpu.SemaphoreType.DMA((3,)),
-        ],
-    )
-    field = to_halves(keep, give)
-    left_shape = jax.ShapeDtypeStruct((ROWS, 4 * ROWS), jnp.bfloat16)
-    right_shape = jax.ShapeDtypeStruct((4 * ROWS, 2 * ROWS), jnp.bfloat16)
+    def start(given, parts):
+        return run(
+            functools.partial(start_kernel, given),
+            [(2, half, parts, PLANES * QUARTER, ROWS)],
+            orbitals,
+            potential,
+            tables_y[1.0],
+            right_z[1.0],
+            space=pltpu.HBM,
+            scratch=[
+                pltpu.VMEM(orbitals.shape, jnp.float32),
+                pltpu.VMEM(real_shape, jnp.float32),
+                pltpu.VMEM(tables_y[1.0].shape, jnp.bfloat16),
+                pltpu.VMEM(right_z[1.0].shape, jnp.bfloat16),
+                pltpu.SemaphoreType.DMA((4,)),
+            ],
+        )
+
+    give = start(1, 2)
+    sent = joined(start(0, 3), give)
+    sent, shift_x = lax.optimization_barrier((sent, shift_x))
+    field = to_halves(sent)
     made = run(
-        functools.partial(table_kernel, count_x),
-        [left_shape] * (2 * count_x + 2) + [right_shape] * 2,
-        jnp.concatenate([shift_x, shift_yz]),
-        numbers_full,
+        table_kernel,
+        [jax.ShapeDtypeStruct((ROWS, 4 * ROWS), jnp.bfloat16)] * (2 * count_x),
+        shift_x,
         line_pair,
     )
     early = (squares, squares_all, factor, factor_all)
     made, early = lax.optimization_barrier((made, early))
     squares, squares_all, factor, factor_all = early
-    tables = {1.0: made[0 : 2 * count_x + 2 : 2], -1.0: made[1 : 2 * count_x + 2 : 2]}
-    right_z = {1.0: made[-2], -1.0: made[-1]}
+    tables_x = {1.0: made[::2], -1.0: made[1::2]}
 
     def table_x(sign, count):
-        return tables[sign][count if sign > 0 else count_x - 1 - count]
+        return tables_x[sign][count if sign > 0 else count_x - 1 - count]
 
     def table_y(sign):
-        return tables[sign][count_x]
+        return tables_y[sign]
 
     def tables_of(sign, count):
         if count % 2 == 0:
@@ -943,7 +957,6 @@
     sent = middle(1.0, swap_field(sent), 3)
     kept = []
     all_shape = (2 * blocks, 2, PLANES * QUARTER, ROWS)
-    keep_shape = (blocks, 2, PLANES * QUARTER, ROWS)
     for count in range(4, count_x - 1):
         field = swap_field(sent)
         if count % SUB == 0:
@@ -993,26 +1006,31 @@
     )
     field = exchange_whole(sent)
     field = field.reshape(blocks, QUARTER * PLANES, ROWS)
-    keep, give = run(
-        functools.partial(hartree_all_kernel, -1.0),
-        [keep_shape, keep_shape],
-        field,
-        other_core(field),
-        density,
-        xc_kernel,
-        *orbital,
-        costate,
-        potential,
-        cas_left,
-        cas_right,
-        table_y(-1.0),
-        right_z[-1.0],
-        scratch=[pltpu.VMEM((2, blocks, QUARTER * PLANES, ROWS), jnp.float32)],
-    )
+    got = other_core(field)
+
+    def restart(given):
+        return run(
+            functools.partial(hartree_all_kernel, -1.0, given),
+            [(2, half, 2, PLANES * QUARTER, ROWS)],
+            field,
+            got,
+            density,
+            xc_kernel,
+            *orbital,
+            costate,
+            potential,
+            cas_left,
+            cas_right,
+            table_y(-1.0),
+            right_z[-1.0],
+            scratch=[pltpu.VMEM((2, blocks, QUARTER * PLANES, ROWS), jnp.float32)],
+        )
+
+    give = restart(1)
     sent = run(
         functools.partial(all_mid_kernel, -1.0),
         [sent_shape],
-        to_halves(keep, give),
+        to_halves(joined(restart(0), give)),
         *waves_cols,
         *tables_of(-1.0, 1),
     )

time: 511 us -> 510 us (level)
    pallas_call x26 -> x28, Pallas kernels: 44.5 us -> 47.6 us  [run(): pl.pallas_call(kernel, out_shape=[jax.ShapeDtypeStruct(out, jnp.float32)...]
where the time goes in v6:
time: 510 us; the launch traced here: 500 us
  blocking collectives  281 us (55%)
  waiting for transfers between devices  121 us (24%)
  Pallas kernels  47.6 us (9%)
  starting transfers between devices  27.9 us (5%)
  local copies, waits for them, and re-layouts  16.9 us (3%)
    all_to_all x13, blocking collectives, exchange(): lax.all_to_all(array, AXES, 0, 0, axis_index_groups=groups, tiled=True)  229 us
    all_to_all x3, waiting for transfers between devices, exchange_all(): lax.all_to_all(array, AXES, 0, 0, axis_index_groups=[everyone], tiled=True)  74.8 us
    pallas_call x28, Pallas kernels, run(): pl.pallas_call(kernel, out_shape=[jax.ShapeDtypeStruct(out, jnp.float32)...  47.6 us
    ppermute x2, waiting for transfers between devices, move(): return lax.ppermute(array, AXES, pairs)  40.5 us
    all_to_all x1, blocking collectives, exchange_all(): lax.all_to_all(array, AXES, 0, 0, axis_index_groups=[everyone], tiled=True)  28.5 us
    all_to_all x2, blocking collectives, exchange_whole(): return lax.all_to_all(array, 'fft', 0, 0, tiled=True)  23.5 us
    unnamed x94, local copies, waits for them, and re-layouts  14.3 us
    all_to_all x3, starting transfers between devices, exchange_all(): lax.all_to_all(array, AXES, 0, 0, axis_index_groups=[everyone], tiled=True)  13.1 us
  transfers between devices with their start and end apart: 13, of which 11 were waited for; matrix products, arithmetic and copies ran while one was open for 1% of the time, Pallas kernels for 1%

profile of v6, /device:TPU:1, one launch (start us, length us, event | category | flops | bytes accessed | tf_op | source)
XLA Modules:
  0.0 500.0 jit_solution(14877257503921964313)
XLA Ops:
  6.5 1.5 shard_map.149.keep_ref
  8.4 2.4 shard_map.151
  10.8 7.1 %all-to-all-start = ((f32[32,3,32,128]{3,2,1,0:T(8,128)}), f32[32,3,32,128]{3,2,1,0:T(8,128)}, u32[]{:S(2)}, u32[]{:S(2)}) async-start(f32[32,3,32,128]{3,2,1,0:T(8,128)} %bitcast), calls=%async_computation | async-start | bytes 3145728 | tf_op jit(solution)/shard_map/all_to_all | solution.py:832
  22.1 3.7 shard_map.152
  32.3 22.8 %all-to-all-done.field_ref = f32[32,3,32,128]{3,2,1,0:T(8,128)} async-done(((f32[32,3,32,128]{3,2,1,0:T(8,128)}), f32[32,3,32,128]{3,2,1,0:T(8,128)}, u32[]{:S(2)}, u32[]{:S(2)}) %all-to-all-start) | async-done | bytes 1572896 | tf_op jit(solution)/shard_map/all_to_all | solution.py:832
  55.1 3.7 shard_map.153
  58.8 24.1 %all_to_all.100.field_ref = f32[16,3,8,8,128]{4,3,2,1,0:T(8,128)S(1)} all-to-all(f32[16,3,8,8,128]{4,3,2,1,0:T(8,128)S(1)} %bitcast.45), channel_id=1, replica_groups={{0,1,16,17,2,3,18,19,4,5,20,21,6,7,22,23},{8,9,24,25,10,11,26,27,12,13,..., dimensions={0} | all-to-all | bytes 3145728 | tf_op jit(solution)/shard_map/all_to_all | solution.py:826
  82.8 2.1 shard_map.154
  85.0 17.9 %all_to_all.101.field_ref = f32[16,2,8,8,128]{4,3,2,1,0:T(8,128)S(1)} all-to-all(f32[16,2,8,8,128]{4,3,2,1,0:T(8,128)S(1)} %bitcast.47), channel_id=1, replica_groups={{0,1,16,17,2,3,18,19,4,5,20,21,6,7,22,23},{8,9,24,25,10,11,26,27,12,13,..., dimensions={0} | all-to-all | bytes 2097152 | tf_op jit(solution)/shard_map/all_to_all | solution.py:826
  103.0 1.6 shard_map.155
  104.6 17.8 %all_to_all.102.field_ref = f32[16,2,8,8,128]{4,3,2,1,0:T(8,128)S(1)} all-to-all(f32[16,2,8,8,128]{4,3,2,1,0:T(8,128)S(1)} %bitcast.33), channel_id=1, replica_groups={{0,1,16,17,2,3,18,19,4,5,20,21,6,7,22,23},{8,9,24,25,10,11,26,27,12,13,..., dimensions={0} | all-to-all | bytes 2097152 | tf_op jit(solution)/shard_map/all_to_all | solution.py:826
  122.4 1.8 shard_map.156
  125.0 17.8 %all_to_all.103.field_ref = f32[16,2,8,8,128]{4,3,2,1,0:T(8,128)S(1)} all-to-all(f32[16,2,8,8,128]{4,3,2,1,0:T(8,128)S(1)} %bitcast.48), channel_id=1, replica_groups={{0,1,16,17,2,3,18,19,4,5,20,21,6,7,22,23},{8,9,24,25,10,11,26,27,12,13,..., dimensions={0} | all-to-all | bytes 2097152 | tf_op jit(solution)/shard_map/all_to_all | solution.py:826
  142.8 1.6 shard_map.157
  144.4 17.7 %all_to_all.104.field_ref = f32[16,2,8,8,128]{4,3,2,1,0:T(8,128)S(1)} all-to-all(f32[16,2,8,8,128]{4,3,2,1,0:T(8,128)S(1)} %bitcast.34), channel_id=1, replica_groups={{0,1,16,17,2,3,18,19,4,5,20,21,6,7,22,23},{8,9,24,25,10,11,26,27,12,13,..., dimensions={0} | all-to-all | bytes 2097152 | tf_op jit(solution)/shard_map/all_to_all | solution.py:826
  162.1 1.6 shard_map.158
  163.7 17.8 %all_to_all.105.field_ref = f32[16,2,8,8,128]{4,3,2,1,0:T(8,128)S(1)} all-to-all(f32[16,2,8,8,128]{4,3,2,1,0:T(8,128)S(1)} %bitcast.38), channel_id=1, replica_groups={{0,1,16,17,2,3,18,19,4,5,20,21,6,7,22,23},{8,9,24,25,10,11,26,27,12,13,..., dimensions={0} | all-to-all | bytes 2097152 | tf_op jit(solution)/shard_map/all_to_all | solution.py:826
  181.5 1.6 shard_map.159
  184.1 3.2 all-to-all-start.7
  187.3 26.3 %all-to-all-done.7 = f32[32,2,32,128]{3,2,1,0:T(8,128)} async-done(((f32[32,2,32,128]{3,2,1,0:T(8,128)}), f32[32,2,32,128]{3,2,1,0:T(8,128)}, u32[]{:S(2)}, u32[]{:S(2)}) %all-to-all-start.7) | async-done | bytes 1048608 | tf_op jit(solution)/shard_map/all_to_all | solution.py:832
  215.4 1.5 collective-permute-done.1.got_ref
  217.0 2.3 shard_map.160
  219.8 1.5 collective-permute-done.2.other_ref
  222.0 11.4 %all_to_all.106.field_ref = f32[16,4,8,128]{3,2,1,0:T(8,128)S(1)} all-to-all(f32[16,4,8,128]{3,2,1,0:T(8,128)S(1)} %bitcast.50), channel_id=1, replica_groups=mesh['ka'=2,'fft'=16] {'fft'}, dimensions={0} | all-to-all | bytes 524288 | tf_op jit(solution)/shard_map/all_to_all | solution.py:829
  233.9 12.1 %all_to_all.107 = f32[16,4,8,128]{3,2,1,0:T(8,128)S(1)} all-to-all(f32[16,4,8,128]{3,2,1,0:T(8,128)S(1)} %shard_map.162), channel_id=1, replica_groups=mesh['ka'=2,'fft'=16] {'fft'}, dimensions={0} | all-to-all | bytes 524288 | tf_op jit(solution)/shard_map/all_to_all | solution.py:829
  246.0 3.3 collective-permute-start.3
  254.0 28.5 %all_to_all.108.field_ref = f32[32,2,32,128]{3,2,1,0:T(8,128)S(1)} all-to-all(f32[32,2,32,128]{3,2,1,0:T(8,128)S(1)} %bitcast.40), channel_id=1, replica_groups={{0,4,2,6,1,5,3,7,8,12,10,14,9,13,11,15,16,20,18,22,17,21,19,23,24,28,26..., dimensions={0} | all-to-all | bytes 2097152 | tf_op jit(solution)/shard_map/all_to_all | solution.py:832
  282.6 1.7 shard_map.166
  285.2 4.7 all-to-all-start.11
  289.9 3.0 collective-permute-start.5
  293.0 15.6 %collective-permute-done.5.xc_ref = f32[8,128,128]{2,1,0:T(8,128)S(1)} collective-permute-done((f32[8,128,128]{2,1,0:T(8,128)}, f32[8,128,128]{2,1,0:T(8,128)S(1)}, u32[]{:S(2)}, u32[]{:S(2)}) %collective-permute-start.5) | collective-permute-done | bytes 524320 | tf_op jit(solution)/shard_map/ppermute | solution.py:851
  309.4 2.9 shard_map.167
  312.3 19.9 %all_to_all.109.field_ref = f32[16,2,8,8,128]{4,3,2,1,0:T(8,128)S(1)} all-to-all(f32[16,2,8,8,128]{4,3,2,1,0:T(8,128)S(1)} %bitcast.39), channel_id=1, replica_groups={{0,1,16,17,2,3,18,19,4,5,20,21,6,7,22,23},{8,9,24,25,10,11,26,27,12,13,..., dimensions={0} | all-to-all | bytes 2097152 | tf_op jit(solution)/shard_map/all_to_all | solution.py:826
  332.2 1.6 shard_map.168
  333.9 17.8 %all_to_all.110.field_ref = f32[16,2,8,8,128]{4,3,2,1,0:T(8,128)S(1)} all-to-all(f32[16,2,8,8,128]{4,3,2,1,0:T(8,128)S(1)} %bitcast.35), channel_id=1, replica_groups={{0,1,16,17,2,3,18,19,4,5,20,21,6,7,22,23},{8,9,24,25,10,11,26,27,12,13,..., dimensions={0} | all-to-all | bytes 2097152 | tf_op jit(solution)/shard_map/all_to_all | solution.py:826
  353.5 24.9 %collective-permute-done.6.other_ref = f32[8,128,128]{2,1,0:T(8,128)S(1)} collective-permute-done((f32[8,128,128]{2,1,0:T(8,128)S(1)}, f32[8,128,128]{2,1,0:T(8,128)S(1)}, u32[]{:S(2)}, u32[]{:S(2)}) %collective-permute-start.6) | collective-permute-done | bytes 524320 | tf_op jit(solution)/shard_map/ppermute | solution.py:851
  379.1 12.3 %all_to_all.111.field_ref = f32[16,8,8,128]{3,2,1,0:T(8,128)S(1)} all-to-all(f32[16,8,8,128]{3,2,1,0:T(8,128)S(1)} %bitcast.49), channel_id=1, replica_groups={{0,1,16,17,2,3,18,19,4,5,20,21,6,7,22,23},{8,9,24,25,10,11,26,27,12,13,..., dimensions={0} | all-to-all | bytes 1048576 | tf_op jit(solution)/shard_map/all_to_all | solution.py:826
  391.9 12.2 %all_to_all.112 = f32[16,8,8,128]{3,2,1,0:T(8,128)S(1)} all-to-all(f32[16,8,8,128]{3,2,1,0:T(8,128)S(1)} %shard_map.171), channel_id=1, replica_groups={{0,1,16,17,2,3,18,19,4,5,20,21,6,7,22,23},{8,9,24,25,10,11,26,27,12,13,..., dimensions={0} | all-to-all | bytes 1048576 | tf_op jit(solution)/shard_map/all_to_all | solution.py:826
  404.1 2.0 shard_map.172
  406.1 18.2 %all_to_all.113.field_ref = f32[16,2,8,8,128]{4,3,2,1,0:T(8,128)S(1)} all-to-all(f32[16,2,8,8,128]{4,3,2,1,0:T(8,128)S(1)} %bitcast.46), channel_id=1, replica_groups={{0,1,16,17,2,3,18,19,4,5,20,21,6,7,22,23},{8,9,24,25,10,11,26,27,12,13,..., dimensions={0} | all-to-all | bytes 2097152 | tf_op jit(solution)/shard_map/all_to_all | solution.py:826
  424.3 1.6 shard_map.173
  426.0 17.6 %all_to_all.114.field_ref = f32[16,2,8,8,128]{4,3,2,1,0:T(8,128)S(1)} all-to-all(f32[16,2,8,8,128]{4,3,2,1,0:T(8,128)S(1)} %bitcast.36), channel_id=1, replica_groups={{0,1,16,17,2,3,18,19,4,5,20,21,6,7,22,23},{8,9,24,25,10,11,26,27,12,13,..., dimensions={0} | all-to-all | bytes 2097152 | tf_op jit(solution)/shard_map/all_to_all | solution.py:826
  443.6 1.6 shard_map.174
  445.3 17.7 %all_to_all.115.field_ref = f32[16,2,8,8,128]{4,3,2,1,0:T(8,128)S(1)} all-to-all(f32[16,2,8,8,128]{4,3,2,1,0:T(8,128)S(1)} %bitcast.37), channel_id=1, replica_groups={{0,1,16,17,2,3,18,19,4,5,20,21,6,7,22,23},{8,9,24,25,10,11,26,27,12,13,..., dimensions={0} | all-to-all | bytes 2097152 | tf_op jit(solution)/shard_map/all_to_all | solution.py:826
  462.9 2.6 shard_map.175
  465.5 2.8 all-to-all-start.19
  468.7 25.8 %all-to-all-done.19 = f32[32,2,32,128]{3,2,1,0:T(8,128)S(1)} async-done(((f32[32,2,32,128]{3,2,1,0:T(8,128)}), f32[32,2,32,128]{3,2,1,0:T(8,128)S(1)}, u32[]{:S(2)}, u32[]{:S(2)}) %all-to-all-start.19) | async-done | bytes 1048608 | tf_op jit(solution)/shard_map/all_to_all | solution.py:832
  497.6 2.0 shard_map.176
  (127 shorter events, 32.3 us)
Async XLA Ops:
  0.6 1.0 copy-start.1
  1.6 1.0 copy-start.3
  2.6 0.9 copy-start.6
  3.5 1.2 copy-start.11
  4.8 1.7 copy-start.2
  4.8 1.7 copy-start.4
  4.8 1.7 copy-start.7
  4.8 1.7 copy-start.12
  6.3 1.7 copy-start.46
  6.3 2.1 collective-permute-start
  10.8 7.8 %copy-start.45 = (s32[2]{0:T(128)S(1)}, s32[2]{0:T(128)}, u32[]{:S(2)}) copy-start(s32[2]{0:T(128)} %param.19) | copy-start | bytes 28
  10.8 11.3 %copy-start.44 = (f32[128,256]{1,0:T(8,128)S(1)}, f32[128,256]{1,0:T(8,128)}, u32[]{:S(2)}) copy-start(f32[128,256]{1,0:T(8,128)} %constant.89.clone.lines_ref) | copy-start | bytes 393220
  10.8 44.3 %all-to-all-start = ((f32[32,3,32,128]{3,2,1,0:T(8,128)}), f32[32,3,32,128]{3,2,1,0:T(8,128)}, u32[]{:S(2)}, u32[]{:S(2)}) async-start(f32[32,3,32,128]{3,2,1,0:T(8,128)} %bitcast), calls=%async_computation | async-start | bytes 3145728 | tf_op jit(solution)/shard_map/all_to_all | solution.py:832
  85.0 18.0 %copy-start.41 = (bf16[128,512]{1,0:T(8,128)(2,1)S(1)}, bf16[128,512]{1,0:T(8,128)(2,1)}, u32[]{:S(2)}) copy-start(bf16[128,512]{1,0:T(8,128)(2,1)} %copy-done.40) | copy-start | bytes 393220
  85.0 18.0 %copy-start.43 = (bf16[128,512]{1,0:T(8,128)(2,1)S(1)}, bf16[128,512]{1,0:T(8,128)(2,1)}, u32[]{:S(2)}) copy-start(bf16[128,512]{1,0:T(8,128)(2,1)} %copy-done.42) | copy-start | bytes 393220
  125.0 19.4 %copy-start.17 = (f32[8,128,128]{2,1,0:T(8,128)}, f32[8,128,128]{2,1,0:T(8,128)S(1)}, u32[]{:S(2)}) copy-start(f32[8,128,128]{2,1,0:T(8,128)S(1)} %get-tuple-element.113.other_imag_ref.orbital_imag_ref) | copy-start | bytes 1572868
  125.0 17.8 %copy-start.37 = (bf16[128,512]{1,0:T(8,128)(2,1)S(1)}, bf16[128,512]{1,0:T(8,128)(2,1)}, u32[]{:S(2)}) copy-start(bf16[128,512]{1,0:T(8,128)(2,1)} %copy-done.36) | copy-start | bytes 393220
  125.0 17.8 %copy-start.39 = (bf16[128,512]{1,0:T(8,128)(2,1)S(1)}, bf16[128,512]{1,0:T(8,128)(2,1)}, u32[]{:S(2)}) copy-start(bf16[128,512]{1,0:T(8,128)(2,1)} %copy-done.38) | copy-start | bytes 393220
  163.7 17.8 %copy-start.35 = (bf16[128,512]{1,0:T(8,128)(2,1)S(1)}, bf16[128,512]{1,0:T(8,128)(2,1)}, u32[]{:S(2)}) copy-start(bf16[128,512]{1,0:T(8,128)(2,1)} %copy-done.34) | copy-start | bytes 393220
  183.1 1.0 copy-start.9
  184.1 29.4 %all-to-all-start.7 = ((f32[32,2,32,128]{3,2,1,0:T(8,128)}), f32[32,2,32,128]{3,2,1,0:T(8,128)}, u32[]{:S(2)}, u32[]{:S(2)}) async-start(f32[32,2,32,128]{3,2,1,0:T(8,128)} %copy-done.9), calls=%async_computation.7 | async-start | bytes 2097152 | tf_op jit(solution)/shard_map/all_to_all | solution.py:832
  213.6 3.4 copy-start.8
  214.7 6.6 %copy-start.13 = (bf16[128,256]{1,0:T(8,128)(2,1)S(1)}, bf16[128,256]{1,0:T(8,128)(2,1)}, u32[]{:S(2)}) copy-start(bf16[128,256]{1,0:T(8,128)(2,1)} %constant.90.clone.left_ref.cas_left_ref) | copy-start | bytes 196612
  214.8 6.6 %copy-start.19 = (bf16[256,128]{1,0:T(8,128)(2,1)S(1)}, bf16[256,128]{1,0:T(8,128)(2,1)}, u32[]{:S(2)}) copy-start(bf16[256,128]{1,0:T(8,128)(2,1)} %constant.91.clone.right_ref.cas_right_ref) | copy-start | bytes 196612
  214.8 2.2 collective-permute-start.1
  219.3 31.2 %copy-start = (bf16[512,256]{1,0:T(8,128)(2,1)S(1)}, bf16[512,256]{1,0:T(8,128)(2,1)}, u32[]{:S(2)}) copy-start(bf16[512,256]{1,0:T(8,128)(2,1)} %constant.95.clone.right_ref) | copy-start | bytes 786436
  219.3 31.1 %copy-start.5 = (bf16[128,512]{1,0:T(8,128)(2,1)S(1)}, bf16[128,512]{1,0:T(8,128)(2,1)}, u32[]{:S(2)}) copy-start(bf16[128,512]{1,0:T(8,128)(2,1)} %constant.93.clone.second_ref.first_ref) | copy-start | bytes 393220
  219.3 31.1 %copy-start.14 = (f32[8,128,128]{2,1,0:T(8,128)S(1)}, f32[8,128,128]{2,1,0:T(8,128)}, u32[]{:S(2)}) copy-start(f32[8,128,128]{2,1,0:T(8,128)} %xc_ref.3) | copy-start | bytes 1572868
  219.4 2.0 collective-permute-start.2
  246.0 4.5 collective-permute-start.3
  251.9 2.0 collective-permute-start.4
  254.0 28.6 %copy-start.31 = (bf16[128,512]{1,0:T(8,128)(2,1)S(1)}, bf16[128,512]{1,0:T(8,128)(2,1)}, u32[]{:S(2)}) copy-start(bf16[128,512]{1,0:T(8,128)(2,1)} %copy-done.30) | copy-start | bytes 393220
  254.0 28.6 %copy-start.33 = (bf16[128,512]{1,0:T(8,128)(2,1)S(1)}, bf16[128,512]{1,0:T(8,128)(2,1)}, u32[]{:S(2)}) copy-start(bf16[128,512]{1,0:T(8,128)(2,1)} %copy-done.32) | copy-start | bytes 393220
  284.3 1.0 copy-start.10
  285.2 24.1 %all-to-all-start.11 = ((f32[16,2,8,8,128]{4,3,2,1,0:T(8,128)}), f32[16,2,8,8,128]{4,3,2,1,0:T(8,128)}, u32[]{:S(2)}, u32[]{:S(2)}) async-start(f32[16,2,8,8,128]{4,3,2,1,0:T(8,128)} %bitcast.32), calls=%async_computation.11 | async-start | bytes 2097152 | tf_op jit(solution)/shard_map/all_to_all | solution.py:826
  289.9 18.7 %collective-permute-start.5 = (f32[8,128,128]{2,1,0:T(8,128)}, f32[8,128,128]{2,1,0:T(8,128)S(1)}, u32[]{:S(2)}, u32[]{:S(2)}) collective-permute-start(f32[8,128,128]{2,1,0:T(8,128)} %xc_ref.3), channel_id=1, source_target_pairs={{0,0},{1,1},{2,2},{3,3},{4,4},{5,5},{6,6},{7,7},{8,16},{9,17},{10,... | collective-permute-start | bytes 1572872 | tf_op jit(solution)/shard_map/ppermute | solution.py:851
  312.2 19.9 %copy-start.27 = (bf16[128,512]{1,0:T(8,128)(2,1)S(1)}, bf16[128,512]{1,0:T(8,128)(2,1)}, u32[]{:S(2)}) copy-start(bf16[128,512]{1,0:T(8,128)(2,1)} %copy-done.26) | copy-start | bytes 393220
  312.3 19.9 %copy-start.29 = (bf16[128,512]{1,0:T(8,128)(2,1)S(1)}, bf16[128,512]{1,0:T(8,128)(2,1)}, u32[]{:S(2)}) copy-start(bf16[128,512]{1,0:T(8,128)(2,1)} %copy-done.28) | copy-start | bytes 393220
  333.8 17.8 %copy-start.16 = (f32[8,128,128]{2,1,0:T(8,128)S(1)}, f32[8,128,128]{2,1,0:T(8,128)}, u32[]{:S(2)}) copy-start(f32[8,128,128]{2,1,0:T(8,128)} %copy-done.15) | copy-start | bytes 1572868
  333.8 17.8 %copy-start.18 = (f32[8,128,128]{2,1,0:T(8,128)S(1)}, f32[8,128,128]{2,1,0:T(8,128)}, u32[]{:S(2)}) copy-start(f32[8,128,128]{2,1,0:T(8,128)} %copy-done.17) | copy-start | bytes 1572868
  352.4 26.0 %collective-permute-start.6 = (f32[8,128,128]{2,1,0:T(8,128)S(1)}, f32[8,128,128]{2,1,0:T(8,128)S(1)}, u32[]{:S(2)}, u32[]{:S(2)}) collective-permute-start(f32[8,128,128]{2,1,0:T(8,128)S(1)} %get-tuple-element.115.own_ref), channel_id=1, source_target_pairs={{0,8},{1,9},{2,10},{3,11},{4,12},{5,13},{6,14},{7,15},{8,0},{9,1},... | collective-permute-start | bytes 1572872 | tf_op jit(solution)/shard_map/ppermute | solution.py:851
  379.0 25.1 %copy-start.21 = (f32[8,128,128]{2,1,0:T(8,128)S(1)}, f32[8,128,128]{2,1,0:T(8,128)}, u32[]{:S(2)}) copy-start(f32[8,128,128]{2,1,0:T(8,128)} %copy-done.20) | copy-start | bytes 1572868
  406.1 19.9 %copy-start.22 = (f32[8,128,128]{2,1,0:T(8,128)}, f32[8,128,128]{2,1,0:T(8,128)S(1)}, u32[]{:S(2)}) copy-start(f32[8,128,128]{2,1,0:T(8,128)S(1)} %get-tuple-element.127) | copy-start | bytes 1572868
  406.1 18.2 %copy-start.25 = (bf16[128,512]{1,0:T(8,128)(2,1)S(1)}, bf16[128,512]{1,0:T(8,128)(2,1)}, u32[]{:S(2)}) copy-start(bf16[128,512]{1,0:T(8,128)(2,1)} %copy-done.24) | copy-start | bytes 393220
  465.5 2.8 copy-start.23
  465.5 28.9 %all-to-all-start.19 = ((f32[32,2,32,128]{3,2,1,0:T(8,128)}), f32[32,2,32,128]{3,2,1,0:T(8,128)S(1)}, u32[]{:S(2)}, u32[]{:S(2)}) async-start(f32[32,2,32,128]{3,2,1,0:T(8,128)} %shard_map.175), calls=%async_computation.19 | async-start | bytes 2097152 | tf_op jit(solution)/shard_map/all_to_all | solution.py:832
  468.3 27.5 %collective-permute-start.8 = (f32[8,128,128]{2,1,0:T(8,128)S(1)}, f32[8,128,128]{2,1,0:T(8,128)S(1)}, u32[]{:S(2)}, u32[]{:S(2)}) collective-permute-start(f32[8,128,128]{2,1,0:T(8,128)S(1)} %copy-done.23), channel_id=1, source_target_pairs={{0,16},{16,0},{1,17},{17,1},{2,18},{18,2},{3,19},{19,3},{4,20},{20... | collective-permute-start | bytes 1572872 | tf_op jit(solution)/shard_map/ppermute | solution.py:837
  495.3 2.3 collective-permute-start.7
  (12 other events, 8.1 us)

commit v7 on v6

--- a/solution.py
+++ b/solution.py
@@ -193,6 +193,11 @@
     return jnp.concatenate(halves_of(matrix), axis=axis)
 
 
+def own_shift(count):
+    side = lax.axis_index("fft") // (count // 2)
+    return 0.5 * (jnp.full((ROWS, ROWS), side, jnp.int32).astype(jnp.float32) + 0.5) - 0.5
+
+
 def circulant(shift, numbers, cosine, sine):
     along = shift + numbers
     phase = 0.5 * sub_time * (along * along)
@@ -224,13 +229,17 @@
     )
 
 
-def table_kernel(shift_ref, lines_ref, *out_refs):
+def table_kernel(unit, push_ref, lines_ref, *out_refs):
     numbers = wave_numbers(lax.broadcasted_iota(jnp.int32, (ROWS, ROWS), 0), ROWS)
+    numbers = numbers + unit * own_shift(ROWS // PLANES)
     cosine, sine = lines_ref[:, :ROWS], lines_ref[:, ROWS:]
-    for line in range(len(out_refs) // 2):
-        matrix, turned = circulant(shift_ref[line], numbers, cosine, sine)
-        out_refs[2 * line][...] = side_by_side(matrix, 1)
-        out_refs[2 * line + 1][...] = side_by_side(turned, 1)
+    pairs = (len(out_refs) + 1) // 2
+    for line in range(2 * pairs):
+        pair, which = divmod(line, 2)
+        matrix, turned = circulant(push_ref[line], numbers, cosine, sine)
+        if pair > 0:
+            out_refs[pair - 1][which] = side_by_side(matrix, 1)
+        out_refs[2 * pairs - 2 - pair][1 - which] = side_by_side(turned, 1)
 
 
 def constant_circulant(shift, grid_size):
@@ -348,13 +357,13 @@
                 rows_to(out_ref, block, (part,), plane, rows_of)
 
 
-def between(sign, field, cosine, sine, first_ref, second_ref, right_ref, out_ref):
-    field = from_left(whole_left(first_ref[...]), field)
+def between(sign, field, cosine, sine, first, second, right, out_ref):
+    field = from_left(whole_left(first), field)
     real_part, imag_part = rotated(sign, field[:ROWS], field[ROWS:], *doubled(cosine, sine))
     field = from_left(
-        whole_left(second_ref[...]), jnp.concatenate([real_part, imag_part], axis=0)
-    )
-    scatter_planes(field[:ROWS], field[ROWS:], right_ref[...], out_ref)
+        whole_left(second), jnp.concatenate([real_part, imag_part], axis=0)
+    )
+    scatter_planes(field[:ROWS], field[ROWS:], right, out_ref)
 
 
 def mid_kernel(
@@ -362,7 +371,9 @@
 ):
     cosine, sine = natural(cosine_ref), natural(sine_ref)
     field = gather_planes(field_ref)
-    between(sign, field, cosine, sine, first_ref, second_ref, right_ref, out_ref)
+    between(
+        sign, field, cosine, sine, first_ref[...], second_ref[...], right_ref[...], out_ref
+    )
 
 
 def gather_all(field_ref, part):
@@ -382,8 +393,16 @@
 
 
 def first_mid_kernel(
-    sign, field_ref, first_ref, second_ref, right_ref, out_ref, cosine_ref, sine_ref
-):
+    sign, unit, field_ref, push_ref, lines_ref, right_ref, out_ref, cosine_ref, sine_ref
+):
+    numbers = wave_numbers(lax.broadcasted_iota(jnp.int32, (ROWS, ROWS), 0), ROWS)
+    numbers = numbers + unit * own_shift(ROWS // PLANES)
+    first, second = (
+        side_by_side(
+            circulant(push_ref[line], numbers, lines_ref[:, :ROWS], lines_ref[:, ROWS:])[0], 1
+        )
+        for line in range(2)
+    )
     pot = gather_all(field_ref, 2)
     for plane in range(PLANES):
         for block in range(ROWS // PLANES):
@@ -393,7 +412,7 @@
     store_natural(cosine_ref, cosine)
     store_natural(sine_ref, sine)
     field = jnp.concatenate([gather_all(field_ref, 0), gather_all(field_ref, 1)], axis=0)
-    between(sign, field, cosine, sine, first_ref, second_ref, right_ref, out_ref)
+    between(sign, field, cosine, sine, first, second, right_ref[...], out_ref)
 
 
 def all_mid_kernel(
@@ -401,7 +420,9 @@
 ):
     cosine, sine = natural(cosine_ref), natural(sine_ref)
     field = jnp.concatenate([gather_all(field_ref, 0), gather_all(field_ref, 1)], axis=0)
-    between(sign, field, cosine, sine, first_ref, second_ref, right_ref, out_ref)
+    between(
+        sign, field, cosine, sine, first_ref[...], second_ref[...], right_ref[...], out_ref
+    )
 
 
 def second_mid_kernel(
@@ -412,7 +433,9 @@
     store_natural(cosine_ref, cosine)
     store_natural(sine_ref, sine)
     field = gather_planes(field_ref)
-    between(sign, field, cosine, sine, first_ref, second_ref, right_ref, out_ref)
+    between(
+        sign, field, cosine, sine, first_ref[...], second_ref[...], right_ref[...], out_ref
+    )
 
 
 def last_mid_kernel(
@@ -420,12 +443,22 @@
 ):
     cosine, sine = natural(cosine_ref), natural(sine_ref)
     field = gather_planes(field_ref)
-    between(sign, field, cosine, sine, first_ref, second_ref, right_ref, (out_ref,))
+    between(
+        sign, field, cosine, sine, first_ref[...], second_ref[...], right_ref[...], (out_ref,)
+    )
 
 
 def store_natural(ref, value):
     for plane in range(PLANES):
         ref[plane] = lane(value, plane)
+
+
+def density_factor(weight_ref, occupation_ref, k_index):
+    def row(value):
+        return jnp.full((1, ROWS), value, jnp.int32).astype(jnp.float32)
+
+    total = row(weight_ref[0] + weight_ref[1])
+    return 2.0 * (row(weight_ref[k_index]) / total) * (row(occupation_ref[0]) / 100.0)
 
 
 def finish(sign, field_ref, cosine, sine, first_ref, real_ref, imag_ref):
@@ -487,28 +520,34 @@
 def start_kernel(
     given, field_ref, pot_ref, second_ref, right_ref, out_ref, field, pot, second, right, sems
 ):
+    start = plane_order(lax.axis_index("ka"))[given * QUARTER]
     copies = [
         pltpu.make_async_copy(source, target, sems.at[number])
         for number, (source, target) in enumerate(
-            ((pot_ref, pot), (field_ref, field), (second_ref, second), (right_ref, right))
+            (
+                (pot_ref.at[pl.ds(start, QUARTER)], pot),
+                (field_ref.at[0, 0, :, pl.ds(start, QUARTER)], field),
+                (second_ref, second),
+                (right_ref, right),
+            )
         )
     ]
     for copy in copies:
         copy.start()
-    order = plane_order(lax.axis_index("ka"))[given * QUARTER : (given + 1) * QUARTER]
     copies[0].wait()
     if out_ref.shape[2] > 2:
-        for number, plane in enumerate(order):
-            put_rows(out_ref, (2,), number, pot[plane])
+        for number in range(QUARTER):
+            put_rows(out_ref, (2,), number, pot[number])
+    planes = range(QUARTER)
     cosine, sine = cos_sin(
-        0.5 * sub_time * jnp.concatenate([pot[plane] for plane in order], axis=1)
+        0.5 * sub_time * jnp.concatenate([pot[plane] for plane in planes], axis=1)
     )
     for copy in copies[1:]:
         copy.wait()
     begin_some(
         1.0,
-        jnp.concatenate([field[0, 0, 0, plane] for plane in order], axis=1),
-        jnp.concatenate([field[0, 0, 1, plane] for plane in order], axis=1),
+        jnp.concatenate([field[0, plane] for plane in planes], axis=1),
+        jnp.concatenate([field[1, plane] for plane in planes], axis=1),
         cosine,
         sine,
         whole_left(second[...]),
@@ -535,7 +574,8 @@
     first_ref,
     other_real_ref,
     other_imag_ref,
-    factor_ref,
+    weight_ref,
+    occupation_ref,
     real_ref,
     imag_ref,
     density_ref,
@@ -544,7 +584,8 @@
     real_part, imag_part = finish(
         sign, field_ref, cosine, sine, first_ref, real_ref, imag_ref
     )
-    factor = factor_ref[0, 0]
+    side = lax.axis_index("fft") // (field_ref.shape[0] // 2)
+    factor = density_factor(weight_ref, occupation_ref, side)
     for plane in range(PLANES):
         density_ref[plane] = factor * (
             lane(real_part, plane) * other_real_ref[plane]
@@ -577,7 +618,21 @@
     return order, rotated(sign, field[:ROWS], field[ROWS:], cosine, sine)
 
 
-def final_kernel(sign, field_ref, got_ref, pot_ref, first_ref, out_ref):
+def final_kernel(
+    sign,
+    field_ref,
+    got_ref,
+    pot_ref,
+    first_ref,
+    cross_ref,
+    beside_ref,
+    out_ref,
+    cross_out_ref,
+):
+    blocks = ROWS // PLANES
+    here = lax.axis_index("ka") == lax.axis_index("fft") // (blocks // 2)
+    for plane in range(PLANES):
+        cross_out_ref[plane] = jnp.where(here, cross_ref[plane], beside_ref[plane])
     order, (real_part, imag_part) = finish_all(sign, field_ref, got_ref, pot_ref, first_ref)
     for number, plane in enumerate(order):
         out_ref[0, 0, 0, plane] = lane(real_part, number)
@@ -591,13 +646,14 @@
     pot_ref,
     first_ref,
     other_ref,
-    factor_ref,
+    weight_ref,
+    occupation_ref,
     real_ref,
     imag_ref,
     density_ref,
 ):
     order, (real_part, imag_part) = finish_all(sign, field_ref, got_ref, pot_ref, first_ref)
-    factor = factor_ref[0, 0]
+    factor = density_factor(weight_ref, occupation_ref, lax.axis_index("ka"))
     for number, plane in enumerate(order):
         real_ref[plane] = lane(real_part, number)
         imag_ref[plane] = lane(imag_part, number)
@@ -704,8 +760,13 @@
             rows_to(out_ref, block, (), plane, spectrum[start : start + PLANES])
 
 
-def coulomb_kernel(unit, placed, field_ref, square_ref, left_ref, out_ref):
+def coulomb_kernel(unit, placed, field_ref, left_ref, out_ref):
     blocks, lines = field_ref.shape[:2]
+    core, chip = lax.axis_index("ka"), lax.axis_index("fft")
+    if placed:
+        first = (core * (blocks // 2) + chip % (blocks // 2)) * PLANES
+    else:
+        first = chip * PLANES + core * QUARTER
     places = [place_of(block, blocks) if placed else block for block in range(blocks)]
     rows = jnp.concatenate(
         [
@@ -715,12 +776,17 @@
         axis=1,
     )
     rows = from_left(left_ref[...], rows)
-    index = lax.broadcasted_iota(jnp.int32, (ROWS, ROWS), 0)
-    number = unit * jnp.where(index < ROWS // 2, index, index - ROWS).astype(jnp.float32)
-    along = number * number
+
+    def squared(index):
+        number = unit * jnp.where(index < ROWS // 2, index, index - ROWS).astype(jnp.float32)
+        return number * number
+
+    along = squared(lax.broadcasted_iota(jnp.int32, (ROWS, ROWS), 0)) + squared(
+        lax.broadcasted_iota(jnp.int32, (ROWS, ROWS), 1)
+    )
     parts = []
     for line in range(lines):
-        square = along + square_ref[pl.ds(line, 1), :]
+        square = along + squared(jnp.full((1, ROWS), first + line, jnp.int32))
         nonzero = square > 0
         inverse = jnp.where(nonzero, 4.0 * math.pi / jnp.where(nonzero, square, 1.0), 0.0)
         parts.append(lane(rows, line) * inverse)
@@ -773,21 +839,35 @@
     )
 
 
-def run(kernel, outputs, *operands, space=pltpu.VMEM, scratch=()):
+def run(kernel, outputs, *operands, space=pltpu.VMEM, scratch=(), grant=24):
+    arrays, views = [], []
+    for operand in operands:
+        array, index = operand if isinstance(operand, tuple) else (operand, None)
+        known = [number for number, other in enumerate(arrays) if other is array]
+        if not known:
+            arrays.append(array)
+        views.append((known[0] if known else len(arrays) - 1, index))
+
+    def body(*refs):
+        seen = [
+            refs[number] if index is None else refs[number].at[index] for number, index in views
+        ]
+        kernel(*seen, *refs[len(arrays) :])
+
     made = pl.pallas_call(
-        kernel,
+        body,
         out_shape=[
             jax.ShapeDtypeStruct(out, jnp.float32) if isinstance(out, tuple) else out
             for out in outputs
         ],
         in_specs=[
-            pl.BlockSpec(memory_space=pltpu.SMEM if operand.size < ROWS else space)
-            for operand in operands
+            pl.BlockSpec(memory_space=pltpu.SMEM if array.size < ROWS else space)
+            for array in arrays
         ],
         out_specs=[pl.BlockSpec(memory_space=pltpu.VMEM) for _ in outputs],
         scratch_shapes=list(scratch),
-        compiler_params=pltpu.CompilerParams(vmem_limit_bytes=24 * 2**20),
-    )(*operands)
+        compiler_params=pltpu.CompilerParams(vmem_limit_bytes=grant * 2**20),
+    )(*arrays)
     return made[0] if len(outputs) == 1 else made
 
 
@@ -844,8 +924,11 @@
 
     def from_halves(sent):
         field = exchange_all(sent).reshape(2, 2, half, 2, PLANES * QUARTER, ROWS)
-        give = lax.dynamic_index_in_dim(field, 1 - core, 1, keepdims=False)
-        return field, other_core(give)
+        zero = np.uint32(0)
+        give = lax.dynamic_slice(
+            field, (zero, other, zero, zero, zero, zero), (2, 1) + field.shape[2:]
+        )
+        return field, other_core(give.reshape((2,) + field.shape[2:]))
 
     def move(array, pairs):
         return lax.ppermute(array, AXES, pairs)
@@ -870,23 +953,7 @@
     tables_y = {1.0: constant_table(line_y[0][:ROWS], 1), -1.0: constant_table(line_y[1][:ROWS], 1)}
     right_z = {1.0: constant_table(line_z[1], 0), -1.0: constant_table(line_z[0], 0)}
 
-    shift_x = lattice_unit * ((side.astype(jnp.float32) + 0.5) / 2 - 0.5) + vector_potential
     count_x = STEPS * SUB
-
-    numbers = wave_numbers(lax.iota(jnp.int32, grid_size), grid_size)
-    def squares_of(first, count):
-        own = wave_numbers(first + lax.iota(jnp.int32, count), grid_size)
-        return (own * own)[:, None] + (numbers * numbers)[None, :]
-
-    squares = squares_of(place * PLANES, PLANES)
-    squares_all = squares_of(fft_index * PLANES + core * QUARTER, QUARTER)
-
-    def factor_of(k_index):
-        own_weight = lax.dynamic_slice_in_dim(kpoint_weight, k_index, 1)[0].astype(jnp.float32)
-        weight = own_weight / jnp.sum(kpoint_weight).astype(jnp.float32)
-        return (2.0 * weight * occupation.astype(jnp.float32) / 100.0).reshape(1, 1)
-
-    factor, factor_all = factor_of(side), factor_of(core)
 
     def start(given, parts):
         return run(
@@ -897,9 +964,10 @@
             tables_y[1.0],
             right_z[1.0],
             space=pltpu.HBM,
+            grant=56,
             scratch=[
-                pltpu.VMEM(orbitals.shape, jnp.float32),
-                pltpu.VMEM(real_shape, jnp.float32),
+                pltpu.VMEM((2, QUARTER, ROWS, ROWS), jnp.float32),
+                pltpu.VMEM((QUARTER, ROWS, ROWS), jnp.float32),
                 pltpu.VMEM(tables_y[1.0].shape, jnp.bfloat16),
                 pltpu.VMEM(right_z[1.0].shape, jnp.bfloat16),
                 pltpu.SemaphoreType.DMA((4,)),
@@ -908,21 +976,8 @@
 
     give = start(1, 2)
     sent = joined(start(0, 3), give)
-    sent, shift_x = lax.optimization_barrier((sent, shift_x))
+    sent, other = lax.optimization_barrier((sent, (1 - core).astype(jnp.uint32)))
     field = to_halves(sent)
-    made = run(
-        table_kernel,
-        [jax.ShapeDtypeStruct((ROWS, 4 * ROWS), jnp.bfloat16)] * (2 * count_x),
-        shift_x,
-        line_pair,
-    )
-    early = (squares, squares_all, factor, factor_all)
-    made, early = lax.optimization_barrier((made, early))
-    squares, squares_all, factor, factor_all = early
-    tables_x = {1.0: made[::2], -1.0: made[1::2]}
-
-    def table_x(sign, count):
-        return tables_x[sign][count if sign > 0 else count_x - 1 - count]
 
     def table_y(sign):
         return tables_y[sign]
@@ -930,7 +985,8 @@
     def tables_of(sign, count):
         if count % 2 == 0:
             return table_y(sign), table_y(sign), right_z[sign]
-        return table_x(sign, count - 1), table_x(sign, count), right_z[sign]
+        pair = tables_x[sign][count // 2]
+        return (pair, 0), (pair, 1), right_z[sign]
 
     def middle(sign, field, count):
         waves = waves_rows if count % 2 == 0 else waves_cols
@@ -943,18 +999,33 @@
         )
 
     sent, *waves_cols = run(
-        functools.partial(first_mid_kernel, 1.0),
+        functools.partial(first_mid_kernel, 1.0, lattice_unit),
         [(blocks, 3) + sent_shape[2:], real_shape, real_shape],
         field,
-        *tables_of(1.0, 1),
+        vector_potential,
+        line_pair,
+        right_z[1.0],
     )
     sent, *waves_rows = run(
         functools.partial(second_mid_kernel, 1.0),
         [sent_shape, real_shape, real_shape],
         exchange(sent.reshape(blocks, 3, PLANES, PLANES, ROWS)),
-        *tables_of(1.0, 2),
-    )
-    sent = middle(1.0, swap_field(sent), 3)
+        table_y(1.0),
+        table_y(1.0),
+        right_z[1.0],
+    )
+    sent, push, xc_rows = lax.optimization_barrier((sent, vector_potential, xc_kernel))
+    xc_rows = move(xc_rows, regroup)
+    field = swap_field(sent)
+    made = run(
+        functools.partial(table_kernel, lattice_unit),
+        [jax.ShapeDtypeStruct((2, ROWS, 4 * ROWS), jnp.bfloat16)] * (count_x - 1),
+        push,
+        line_pair,
+    )
+    field, xc_rows, made = lax.optimization_barrier((field, xc_rows, made))
+    tables_x = {1.0: [None, *made[: count_x // 2 - 1]], -1.0: made[count_x // 2 - 1 :]}
+    sent = middle(1.0, field, 3)
     kept = []
     all_shape = (2 * blocks, 2, PLANES * QUARTER, ROWS)
     for count in range(4, count_x - 1):
@@ -984,7 +1055,8 @@
         potential,
         table_y(1.0),
         costate,
-        factor_all,
+        kpoint_weight,
+        occupation,
     )
 
     density, sent = run(
@@ -1001,7 +1073,6 @@
         functools.partial(coulomb_kernel, lattice_unit, False),
         [(blocks, QUARTER, PLANES, ROWS)],
         field,
-        squares_all,
         cas_left,
     )
     field = exchange_whole(sent)
@@ -1050,7 +1121,6 @@
                 functools.partial(coulomb_kernel, lattice_unit, True),
                 [(blocks, PLANES, PLANES, ROWS)],
                 field,
-                squares,
                 cas_left,
             )
             field = exchange(sent).reshape(blocks, PLANES * PLANES, ROWS)
@@ -1069,11 +1139,7 @@
                 right_z[-1.0],
             )
             sent = middle(-1.0, swap_field(sent), first + 1)
-            field = swap_field(sent)
-        else:
-            sent, xc_rows = lax.optimization_barrier((sent, xc_kernel))
-            field = swap_field(sent)
-            field, xc_rows = lax.optimization_barrier((field, move(xc_rows, regroup)))
+        field = swap_field(sent)
         sent = middle(-1.0, field, first + 2)
         field = swap_field(sent)
         if step_index > 0:
@@ -1085,7 +1151,8 @@
                 *waves_rows,
                 table_y(-1.0),
                 *kept[step_index - 1],
-                factor,
+                kpoint_weight,
+                occupation,
             )
     sent = run(
         functools.partial(last_mid_kernel, -1.0),
@@ -1094,14 +1161,18 @@
         *waves_cols,
         *tables_of(-1.0, count_x - 1),
     )
-    result = run(
+    field, got = from_halves(sent)
+    field, cross = lax.optimization_barrier((field, cross))
+    return run(
         functools.partial(final_kernel, -1.0),
-        [orbitals.shape],
-        *from_halves(sent),
+        [orbitals.shape, real_shape],
+        field,
+        got,
         potential,
         table_y(-1.0),
-    )
-    return (result, jnp.where(core == side, cross, other_core(cross)))
+        cross,
+        other_core(cross),
+    )
 
 
 def solution(mesh):

time: 510 us -> 498 us (0.976)
  blocking collectives: 281 us -> 382 us
  waiting for transfers between devices: 121 us -> 37.6 us
  starting transfers between devices: 27.9 us -> 12.8 us
  local copies, waits for them, and re-layouts: 16.9 us -> 9.85 us
    all_to_all x1 -> x4, blocking collectives: 28.5 us -> 130 us  [exchange_all(): lax.all_to_all(array, AXES, 0, 0, axis_index_groups=[everyone], tiled=True)]
    all_to_all x3 -> x0, waiting for transfers between devices: 74.8 us -> none  [exchange_all(): lax.all_to_all(array, AXES, 0, 0, axis_index_groups=[everyone], tiled=True)]
    all_to_all x3 -> x0, starting transfers between devices: 13.1 us -> none  [exchange_all(): lax.all_to_all(array, AXES, 0, 0, axis_index_groups=[everyone], tiled=True)]
    ppermute x2, waiting for transfers between devices: 40.5 us -> 31.7 us  [move(): return lax.ppermute(array, AXES, pairs)]
    unnamed x94 -> x62, local copies, waits for them, and re-layouts: 14.3 us -> 9.77 us
  transfers between devices with their start and end apart: 13 -> 10, of which waited for: 11 -> 8; matrix products, arithmetic and copies ran while one was open for 1% -> 0% of each run, Pallas kernels for 1% -> 2%
where the time goes in v7:
time: 498 us; the launch traced here: 491 us
  blocking collectives  382 us (77%)
  Pallas kernels  46.1 us (9%)
  waiting for transfers between devices  37.6 us (8%)
  starting transfers between devices  12.8 us (3%)
  local copies, waits for them, and re-layouts  9.85 us (2%)
    all_to_all x13, blocking collectives, exchange(): lax.all_to_all(array, AXES, 0, 0, axis_index_groups=groups, tiled=True)  229 us
    all_to_all x4, blocking collectives, exchange_all(): lax.all_to_all(array, AXES, 0, 0, axis_index_groups=[everyone], tiled=True)  130 us
    pallas_call x28, Pallas kernels, run(): pl.pallas_call(body, out_shape=[jax.ShapeDtypeStruct(out, jnp.float32) if...  46.1 us
    ppermute x2, waiting for transfers between devices, move(): return lax.ppermute(array, AXES, pairs)  31.7 us
    all_to_all x2, blocking collectives, exchange_whole(): return lax.all_to_all(array, 'fft', 0, 0, tiled=True)  23.4 us
  transfers between devices with their start and end apart: 10, of which 8 were waited for; matrix products, arithmetic and copies ran while one was open for 0% of the time, Pallas kernels for 2%

profile of v7, /device:TPU:1, one launch (start us, length us, event | category | flops | bytes accessed | tf_op | source)
XLA Modules:
  0.0 490.9 jit_solution(3269728797273869806)
XLA Ops:
  0.6 3.0 shard_map.150
  3.7 3.1 shard_map.149.refs_0_
  8.1 44.3 %all_to_all.100.refs_0_ = f32[32,3,32,128]{3,2,1,0:T(8,128)S(1)} all-to-all(f32[32,3,32,128]{3,2,1,0:T(8,128)S(1)} %bitcast.28), channel_id=1, replica_groups={{0,4,2,6,1,5,3,7,8,12,10,14,9,13,11,15,16,20,18,22,17,21,19,23,24,28,26..., dimensions={0} | all-to-all | bytes 3145728 | tf_op jit(solution)/shard_map/all_to_all | solution.py:912
  52.4 3.7 shard_map.152
  56.1 24.6 %all_to_all.101.refs_0_ = f32[16,3,8,8,128]{4,3,2,1,0:T(8,128)S(1)} all-to-all(f32[16,3,8,8,128]{4,3,2,1,0:T(8,128)S(1)} %bitcast.42), channel_id=1, replica_groups={{0,1,16,17,2,3,18,19,4,5,20,21,6,7,22,23},{8,9,24,25,10,11,26,27,12,13,..., dimensions={0} | all-to-all | bytes 3145728 | tf_op jit(solution)/shard_map/all_to_all | solution.py:906
  80.8 2.1 shard_map.153
  83.8 3.7 all-to-all-start.2
  87.5 2.7 collective-permute-start.1
  91.1 3.7 shard_map.154
  99.8 6.4 %collective-permute-done.1.refs_2_ = f32[8,128,128]{2,1,0:T(8,128)S(1)} collective-permute-done((f32[8,128,128]{2,1,0:T(8,128)}, f32[8,128,128]{2,1,0:T(8,128)S(1)}, u32[]{:S(2)}, u32[]{:S(2)}) %collective-permute-start.1) | collective-permute-done | bytes 524320 | tf_op jit(solution)/shard_map/ppermute | solution.py:934
  107.9 1.6 shard_map.155
  109.6 19.3 %all_to_all.102.refs_0_ = f32[16,2,8,8,128]{4,3,2,1,0:T(8,128)S(1)} all-to-all(f32[16,2,8,8,128]{4,3,2,1,0:T(8,128)S(1)} %bitcast.30), channel_id=1, replica_groups={{0,1,16,17,2,3,18,19,4,5,20,21,6,7,22,23},{8,9,24,25,10,11,26,27,12,13,..., dimensions={0} | all-to-all | bytes 2097152 | tf_op jit(solution)/shard_map/all_to_all | solution.py:906
  128.9 1.8 shard_map.156
  130.7 17.8 %all_to_all.103.refs_0_ = f32[16,2,8,8,128]{4,3,2,1,0:T(8,128)S(1)} all-to-all(f32[16,2,8,8,128]{4,3,2,1,0:T(8,128)S(1)} %bitcast.45), channel_id=1, replica_groups={{0,1,16,17,2,3,18,19,4,5,20,21,6,7,22,23},{8,9,24,25,10,11,26,27,12,13,..., dimensions={0} | all-to-all | bytes 2097152 | tf_op jit(solution)/shard_map/all_to_all | solution.py:906
  148.5 1.6 shard_map.157
  150.1 17.6 %all_to_all.104.refs_0_ = f32[16,2,8,8,128]{4,3,2,1,0:T(8,128)S(1)} all-to-all(f32[16,2,8,8,128]{4,3,2,1,0:T(8,128)S(1)} %bitcast.31), channel_id=1, replica_groups={{0,1,16,17,2,3,18,19,4,5,20,21,6,7,22,23},{8,9,24,25,10,11,26,27,12,13,..., dimensions={0} | all-to-all | bytes 2097152 | tf_op jit(solution)/shard_map/all_to_all | solution.py:906
  167.8 1.6 shard_map.158
  169.4 17.8 %all_to_all.105.refs_0_ = f32[16,2,8,8,128]{4,3,2,1,0:T(8,128)S(1)} all-to-all(f32[16,2,8,8,128]{4,3,2,1,0:T(8,128)S(1)} %bitcast.35), channel_id=1, replica_groups={{0,1,16,17,2,3,18,19,4,5,20,21,6,7,22,23},{8,9,24,25,10,11,26,27,12,13,..., dimensions={0} | all-to-all | bytes 2097152 | tf_op jit(solution)/shard_map/all_to_all | solution.py:906
  187.2 1.6 shard_map.159
  188.8 29.3 %all_to_all.106 = f32[32,2,32,128]{3,2,1,0:T(8,128)S(1)} all-to-all(f32[32,2,32,128]{3,2,1,0:T(8,128)S(1)} %shard_map.159), channel_id=1, replica_groups={{0,4,2,6,1,5,3,7,8,12,10,14,9,13,11,15,16,20,18,22,17,21,19,23,24,28,26..., dimensions={0} | all-to-all | bytes 2097152 | tf_op jit(solution)/shard_map/all_to_all | solution.py:912
  220.4 1.6 shard_map.160
  222.5 1.5 collective-permute-done.3.refs_1_
  224.8 11.5 %all_to_all.107.refs_0_ = f32[16,4,8,128]{3,2,1,0:T(8,128)S(1)} all-to-all(f32[16,4,8,128]{3,2,1,0:T(8,128)S(1)} %bitcast.47), channel_id=1, replica_groups=mesh['ka'=2,'fft'=16] {'fft'}, dimensions={0} | all-to-all | bytes 524288 | tf_op jit(solution)/shard_map/all_to_all | solution.py:909
  236.7 11.9 %all_to_all.108 = f32[16,4,8,128]{3,2,1,0:T(8,128)S(1)} all-to-all(f32[16,4,8,128]{3,2,1,0:T(8,128)S(1)} %shard_map.162), channel_id=1, replica_groups=mesh['ka'=2,'fft'=16] {'fft'}, dimensions={0} | all-to-all | bytes 524288 | tf_op jit(solution)/shard_map/all_to_all | solution.py:909
  248.6 3.3 collective-permute-start.4
  253.0 1.5 shard_map.164
  254.9 1.5 shard_map.163.refs_0_
  256.6 28.5 %all_to_all.109.refs_0_ = f32[32,2,32,128]{3,2,1,0:T(8,128)S(1)} all-to-all(f32[32,2,32,128]{3,2,1,0:T(8,128)S(1)} %bitcast.37), channel_id=1, replica_groups={{0,4,2,6,1,5,3,7,8,12,10,14,9,13,11,15,16,20,18,22,17,21,19,23,24,28,26..., dimensions={0} | all-to-all | bytes 2097152 | tf_op jit(solution)/shard_map/all_to_all | solution.py:912
  285.1 1.7 shard_map.166
  286.8 18.2 %all_to_all.110.refs_0_ = f32[16,2,8,8,128]{4,3,2,1,0:T(8,128)S(1)} all-to-all(f32[16,2,8,8,128]{4,3,2,1,0:T(8,128)S(1)} %bitcast.32), channel_id=1, replica_groups={{0,1,16,17,2,3,18,19,4,5,20,21,6,7,22,23},{8,9,24,25,10,11,26,27,12,13,..., dimensions={0} | all-to-all | bytes 2097152 | tf_op jit(solution)/shard_map/all_to_all | solution.py:906
  305.0 1.6 shard_map.167
  306.7 17.8 %all_to_all.111.refs_0_ = f32[16,2,8,8,128]{4,3,2,1,0:T(8,128)S(1)} all-to-all(f32[16,2,8,8,128]{4,3,2,1,0:T(8,128)S(1)} %bitcast.36), channel_id=1, replica_groups={{0,1,16,17,2,3,18,19,4,5,20,21,6,7,22,23},{8,9,24,25,10,11,26,27,12,13,..., dimensions={0} | all-to-all | bytes 2097152 | tf_op jit(solution)/shard_map/all_to_all | solution.py:906
  324.4 1.6 shard_map.168
  326.1 17.9 %all_to_all.112.refs_0_ = f32[16,2,8,8,128]{4,3,2,1,0:T(8,128)S(1)} all-to-all(f32[16,2,8,8,128]{4,3,2,1,0:T(8,128)S(1)} %bitcast.33), channel_id=1, replica_groups={{0,1,16,17,2,3,18,19,4,5,20,21,6,7,22,23},{8,9,24,25,10,11,26,27,12,13,..., dimensions={0} | all-to-all | bytes 2097152 | tf_op jit(solution)/shard_map/all_to_all | solution.py:906
  344.0 1.3 shard_map.169
  346.0 25.3 %collective-permute-done.6.refs_1_ = f32[8,128,128]{2,1,0:T(8,128)S(1)} collective-permute-done((f32[8,128,128]{2,1,0:T(8,128)S(1)}, f32[8,128,128]{2,1,0:T(8,128)S(1)}, u32[]{:S(2)}, u32[]{:S(2)}) %collective-permute-start.6) | collective-permute-done | bytes 524320 | tf_op jit(solution)/shard_map/ppermute | solution.py:934
  371.9 12.3 %all_to_all.113.refs_0_ = f32[16,8,8,128]{3,2,1,0:T(8,128)S(1)} all-to-all(f32[16,8,8,128]{3,2,1,0:T(8,128)S(1)} %bitcast.46), channel_id=1, replica_groups={{0,1,16,17,2,3,18,19,4,5,20,21,6,7,22,23},{8,9,24,25,10,11,26,27,12,13,..., dimensions={0} | all-to-all | bytes 1048576 | tf_op jit(solution)/shard_map/all_to_all | solution.py:906
  384.8 12.0 %all_to_all.114 = f32[16,8,8,128]{3,2,1,0:T(8,128)S(1)} all-to-all(f32[16,8,8,128]{3,2,1,0:T(8,128)S(1)} %shard_map.171), channel_id=1, replica_groups={{0,1,16,17,2,3,18,19,4,5,20,21,6,7,22,23},{8,9,24,25,10,11,26,27,12,13,..., dimensions={0} | all-to-all | bytes 1048576 | tf_op jit(solution)/shard_map/all_to_all | solution.py:906
  396.8 2.0 shard_map.172
  398.8 17.8 %all_to_all.115.refs_0_ = f32[16,2,8,8,128]{4,3,2,1,0:T(8,128)S(1)} all-to-all(f32[16,2,8,8,128]{4,3,2,1,0:T(8,128)S(1)} %bitcast.44), channel_id=1, replica_groups={{0,1,16,17,2,3,18,19,4,5,20,21,6,7,22,23},{8,9,24,25,10,11,26,27,12,13,..., dimensions={0} | all-to-all | bytes 2097152 | tf_op jit(solution)/shard_map/all_to_all | solution.py:906
  416.5 1.6 shard_map.173
  418.2 17.6 %all_to_all.116.refs_0_ = f32[16,2,8,8,128]{4,3,2,1,0:T(8,128)S(1)} all-to-all(f32[16,2,8,8,128]{4,3,2,1,0:T(8,128)S(1)} %bitcast.34), channel_id=1, replica_groups={{0,1,16,17,2,3,18,19,4,5,20,21,6,7,22,23},{8,9,24,25,10,11,26,27,12,13,..., dimensions={0} | all-to-all | bytes 2097152 | tf_op jit(solution)/shard_map/all_to_all | solution.py:906
  435.8 1.6 shard_map.174
  437.5 17.8 %all_to_all.117.refs_0_ = f32[16,2,8,8,128]{4,3,2,1,0:T(8,128)S(1)} all-to-all(f32[16,2,8,8,128]{4,3,2,1,0:T(8,128)S(1)} %bitcast.29), channel_id=1, replica_groups={{0,1,16,17,2,3,18,19,4,5,20,21,6,7,22,23},{8,9,24,25,10,11,26,27,12,13,..., dimensions={0} | all-to-all | bytes 2097152 | tf_op jit(solution)/shard_map/all_to_all | solution.py:906
  455.3 1.6 shard_map.175
  456.9 28.3 %all_to_all.118 = f32[32,2,32,128]{3,2,1,0:T(8,128)S(1)} all-to-all(f32[32,2,32,128]{3,2,1,0:T(8,128)S(1)} %shard_map.175), channel_id=1, replica_groups={{0,4,2,6,1,5,3,7,8,12,10,14,9,13,11,15,16,20,18,22,17,21,19,23,24,28,26..., dimensions={0} | all-to-all | bytes 2097152 | tf_op jit(solution)/shard_map/all_to_all | solution.py:912
  486.0 1.5 collective-permute-done.7.refs_1_
  488.2 2.2 shard_map.176
  (83 shorter events, 18.4 us)
Async XLA Ops:
  3.6 3.2 collective-permute-start
  6.8 1.1 copy-start.7
  8.1 44.3 %copy-start.1 = (bf16[512,256]{1,0:T(8,128)(2,1)S(1)}, bf16[512,256]{1,0:T(8,128)(2,1)}, u32[]{:S(2)}) copy-start(bf16[512,256]{1,0:T(8,128)(2,1)} %constant.29.clone.refs_3_.refs_2_.refs_4_) | copy-start | bytes 786436
  8.1 44.3 %copy-start.13 = (f32[128,256]{1,0:T(8,128)S(1)}, f32[128,256]{1,0:T(8,128)}, u32[]{:S(2)}) copy-start(f32[128,256]{1,0:T(8,128)} %constant.24.clone.refs_2_.refs_1_) | copy-start | bytes 393220
  8.1 44.3 %copy-start.29 = (f32[8]{0:T(128)S(1)}, f32[8]{0:T(128)}, u32[]{:S(2)}) copy-start(f32[8]{0:T(128)} %refs_0_.4) | copy-start | bytes 100
  56.1 24.7 %copy-start.5 = (bf16[128,512]{1,0:T(8,128)(2,1)S(1)}, bf16[128,512]{1,0:T(8,128)(2,1)}, u32[]{:S(2)}) copy-start(bf16[128,512]{1,0:T(8,128)(2,1)} %constant.27.clone.refs_2_.refs_1_.refs_3_) | copy-start | bytes 393220
  82.8 1.0 copy-start.10
  83.8 23.2 %all-to-all-start.2 = ((f32[16,2,8,8,128]{4,3,2,1,0:T(8,128)}), f32[16,2,8,8,128]{4,3,2,1,0:T(8,128)S(1)}, u32[]{:S(2)}, u32[]{:S(2)}) async-start(f32[16,2,8,8,128]{4,3,2,1,0:T(8,128)} %bitcast.43), calls=%async_computation.2 | async-start | bytes 2097152 | tf_op jit(solution)/shard_map/all_to_all | solution.py:906
  87.5 18.7 %collective-permute-start.1 = (f32[8,128,128]{2,1,0:T(8,128)}, f32[8,128,128]{2,1,0:T(8,128)S(1)}, u32[]{:S(2)}, u32[]{:S(2)}) collective-permute-start(f32[8,128,128]{2,1,0:T(8,128)} %refs_3_.15), channel_id=1, source_target_pairs={{0,0},{1,1},{2,2},{3,3},{4,4},{5,5},{6,6},{7,7},{8,16},{9,17},{10,... | collective-permute-start | bytes 1572872 | tf_op jit(solution)/shard_map/ppermute | solution.py:934
  90.2 0.9 copy-start.14
  94.8 0.7 copy-start.15
  95.5 0.7 copy-start.17
  96.2 0.7 copy-start.19
  96.9 0.7 copy-start.21
  97.6 0.7 copy-start.23
  98.3 0.7 copy-start.25
  99.0 0.7 copy-start.27
  106.2 0.8 copy-start.11
  107.0 1.0 copy-start.28
  130.7 17.8 %copy-start.26 = (bf16[2,128,512]{2,1,0:T(8,128)(2,1)S(1)}, bf16[2,128,512]{2,1,0:T(8,128)(2,1)}, u32[]{:S(2)}) copy-start(bf16[2,128,512]{2,1,0:T(8,128)(2,1)} %copy-done.25) | copy-start | bytes 786436
  169.4 17.8 %copy-start.24 = (bf16[2,128,512]{2,1,0:T(8,128)(2,1)S(1)}, bf16[2,128,512]{2,1,0:T(8,128)(2,1)}, u32[]{:S(2)}) copy-start(bf16[2,128,512]{2,1,0:T(8,128)(2,1)} %copy-done.23) | copy-start | bytes 786436
  188.8 31.6 %copy-start.2 = (f32[8,128,128]{2,1,0:T(8,128)S(1)}, f32[8,128,128]{2,1,0:T(8,128)}, u32[]{:S(2)}) copy-start(f32[8,128,128]{2,1,0:T(8,128)} %refs_2_.9) | copy-start | bytes 1572868
  188.8 31.6 %copy-start.3 = (f32[1,1,2,8,128,128]{5,4,3,2,1,0:T(8,128)S(1)}, f32[1,1,2,8,128,128]{5,4,3,2,1,0:T(8,128)}, u32[]{:S(2)}) copy-start(f32[1,1,2,8,128,128]{5,4,3,2,1,0:T(8,128)} %refs_6_.5) | copy-start | bytes 3145732
  188.8 31.5 %copy-start.30 = (s32[2]{0:T(128)S(1)}, s32[2]{0:T(128)}, u32[]{:S(2)}) copy-start(s32[2]{0:T(128)} %refs_6_.6) | copy-start | bytes 28
  218.2 2.2 collective-permute-start.2
  219.5 4.6 copy-start.6
  219.5 4.6 copy-start.9
  222.0 31.0 %copy-start = (bf16[512,256]{1,0:T(8,128)(2,1)S(1)}, bf16[512,256]{1,0:T(8,128)(2,1)}, u32[]{:S(2)}) copy-start(bf16[512,256]{1,0:T(8,128)(2,1)} %constant.30.clone.refs_11_.refs_4_.refs_12_) | copy-start | bytes 786436
  222.0 31.0 %copy-start.4 = (bf16[128,512]{1,0:T(8,128)(2,1)S(1)}, bf16[128,512]{1,0:T(8,128)(2,1)}, u32[]{:S(2)}) copy-start(bf16[128,512]{1,0:T(8,128)(2,1)} %constant.28.clone.refs_10_.refs_3_.refs_11_) | copy-start | bytes 393220
  222.1 31.0 %copy-start.8 = (f32[8,128,128]{2,1,0:T(8,128)S(1)}, f32[8,128,128]{2,1,0:T(8,128)}, u32[]{:S(2)}) copy-start(f32[8,128,128]{2,1,0:T(8,128)} %refs_3_.15) | copy-start | bytes 1572868
  222.1 2.0 collective-permute-start.3
  248.6 4.5 collective-permute-start.4
  254.5 2.0 collective-permute-start.5
  256.6 28.6 %copy-start.22 = (bf16[2,128,512]{2,1,0:T(8,128)(2,1)S(1)}, bf16[2,128,512]{2,1,0:T(8,128)(2,1)}, u32[]{:S(2)}) copy-start(bf16[2,128,512]{2,1,0:T(8,128)(2,1)} %copy-done.21) | copy-start | bytes 786436
  306.6 17.8 %copy-start.20 = (bf16[2,128,512]{2,1,0:T(8,128)(2,1)S(1)}, bf16[2,128,512]{2,1,0:T(8,128)(2,1)}, u32[]{:S(2)}) copy-start(bf16[2,128,512]{2,1,0:T(8,128)(2,1)} %copy-done.19) | copy-start | bytes 786436
  345.3 26.0 %collective-permute-start.6 = (f32[8,128,128]{2,1,0:T(8,128)S(1)}, f32[8,128,128]{2,1,0:T(8,128)S(1)}, u32[]{:S(2)}, u32[]{:S(2)}) collective-permute-start(f32[8,128,128]{2,1,0:T(8,128)S(1)} %get-tuple-element.78.refs_0_), channel_id=1, source_target_pairs={{0,8},{1,9},{2,10},{3,11},{4,12},{5,13},{6,14},{7,15},{8,0},{9,1},... | collective-permute-start | bytes 1572872 | tf_op jit(solution)/shard_map/ppermute | solution.py:934
  371.9 24.8 %copy-start.12 = (f32[8,128,128]{2,1,0:T(8,128)S(1)}, f32[8,128,128]{2,1,0:T(8,128)}, u32[]{:S(2)}) copy-start(f32[8,128,128]{2,1,0:T(8,128)} %copy-done.11) | copy-start | bytes 1572868
  398.7 17.8 %copy-start.18 = (bf16[2,128,512]{2,1,0:T(8,128)(2,1)S(1)}, bf16[2,128,512]{2,1,0:T(8,128)(2,1)}, u32[]{:S(2)}) copy-start(bf16[2,128,512]{2,1,0:T(8,128)(2,1)} %copy-done.17) | copy-start | bytes 786436
  437.5 17.8 %copy-start.16 = (bf16[2,128,512]{2,1,0:T(8,128)(2,1)S(1)}, bf16[2,128,512]{2,1,0:T(8,128)(2,1)}, u32[]{:S(2)}) copy-start(bf16[2,128,512]{2,1,0:T(8,128)(2,1)} %copy-done.15) | copy-start | bytes 786436
  485.3 2.2 collective-permute-start.7
  485.9 2.3 collective-permute-start.8

commit v8 on v7

--- a/solution.py
+++ b/solution.py
@@ -702,17 +702,21 @@
     order = plane_order(core)[given * QUARTER : (given + 1) * QUARTER]
     rows_ref[core] = field_ref[...]
     rows_ref[1 - core] = got_ref[...]
+
+    def rows_of(plane):
+        return jnp.concatenate(
+            [
+                rows_ref[number, block, pl.ds(plane, QUARTER, stride=PLANES), :]
+                for block in range(field_ref.shape[0])
+                for number in range(2)
+            ],
+            axis=0,
+        )
+
     spectrum = jnp.concatenate(
         [
-            jnp.concatenate(
-                [
-                    rows_ref[number, block, pl.ds(plane, QUARTER, stride=PLANES), :]
-                    for block in range(field_ref.shape[0])
-                    for number in range(2)
-                ],
-                axis=0,
-            )
-            for plane in order
+            jnp.where(core == given, rows_of(number), rows_of(QUARTER + number))
+            for number in range(QUARTER)
         ],
         axis=1,
     )

time: 498 us -> 498 us (level)
  no operation moved by 1% of the time
where the time goes in v8:
time: 498 us; the launch traced here: 491 us
  blocking collectives  382 us (77%)
  Pallas kernels  46.1 us (9%)
  waiting for transfers between devices  37.6 us (8%)
  starting transfers between devices  12.8 us (3%)
  local copies, waits for them, and re-layouts  9.85 us (2%)
    all_to_all x13, blocking collectives, exchange(): lax.all_to_all(array, AXES, 0, 0, axis_index_groups=groups, tiled=True)  229 us
    all_to_all x4, blocking collectives, exchange_all(): lax.all_to_all(array, AXES, 0, 0, axis_index_groups=[everyone], tiled=True)  130 us
    pallas_call x28, Pallas kernels, run(): pl.pallas_call(body, out_shape=[jax.ShapeDtypeStruct(out, jnp.float32) if...  46.1 us
    ppermute x2, waiting for transfers between devices, move(): return lax.ppermute(array, AXES, pairs)  31.7 us
    all_to_all x2, blocking collectives, exchange_whole(): return lax.all_to_all(array, 'fft', 0, 0, tiled=True)  23.4 us
  transfers between devices with their start and end apart: 10, of which 8 were waited for; matrix products, arithmetic and copies ran while one was open for 0% of the time, Pallas kernels for 2%

profile of v8, /device:TPU:1, one launch (start us, length us, event | category | flops | bytes accessed | tf_op | source)
XLA Modules:
  0.0 490.9 jit_solution(3173687461666194578)
XLA Ops:
  0.6 3.0 shard_map.150
  3.7 3.1 shard_map.149.refs_0_
  8.1 44.3 %all_to_all.100.refs_0_ = f32[32,3,32,128]{3,2,1,0:T(8,128)S(1)} all-to-all(f32[32,3,32,128]{3,2,1,0:T(8,128)S(1)} %bitcast.28), channel_id=1, replica_groups={{0,4,2,6,1,5,3,7,8,12,10,14,9,13,11,15,16,20,18,22,17,21,19,23,24,28,26..., dimensions={0} | all-to-all | bytes 3145728 | tf_op jit(solution)/shard_map/all_to_all | solution.py:916
  52.4 3.7 shard_map.152
  56.1 24.6 %all_to_all.101.refs_0_ = f32[16,3,8,8,128]{4,3,2,1,0:T(8,128)S(1)} all-to-all(f32[16,3,8,8,128]{4,3,2,1,0:T(8,128)S(1)} %bitcast.42), channel_id=1, replica_groups={{0,1,16,17,2,3,18,19,4,5,20,21,6,7,22,23},{8,9,24,25,10,11,26,27,12,13,..., dimensions={0} | all-to-all | bytes 3145728 | tf_op jit(solution)/shard_map/all_to_all | solution.py:910
  80.8 2.1 shard_map.153
  83.8 3.7 all-to-all-start.2
  87.5 2.7 collective-permute-start.1
  91.1 3.7 shard_map.154
  99.8 6.4 %collective-permute-done.1.refs_2_ = f32[8,128,128]{2,1,0:T(8,128)S(1)} collective-permute-done((f32[8,128,128]{2,1,0:T(8,128)}, f32[8,128,128]{2,1,0:T(8,128)S(1)}, u32[]{:S(2)}, u32[]{:S(2)}) %collective-permute-start.1) | collective-permute-done | bytes 524320 | tf_op jit(solution)/shard_map/ppermute | solution.py:938
  107.9 1.6 shard_map.155
  109.6 19.3 %all_to_all.102.refs_0_ = f32[16,2,8,8,128]{4,3,2,1,0:T(8,128)S(1)} all-to-all(f32[16,2,8,8,128]{4,3,2,1,0:T(8,128)S(1)} %bitcast.30), channel_id=1, replica_groups={{0,1,16,17,2,3,18,19,4,5,20,21,6,7,22,23},{8,9,24,25,10,11,26,27,12,13,..., dimensions={0} | all-to-all | bytes 2097152 | tf_op jit(solution)/shard_map/all_to_all | solution.py:910
  128.9 1.8 shard_map.156
  130.7 17.8 %all_to_all.103.refs_0_ = f32[16,2,8,8,128]{4,3,2,1,0:T(8,128)S(1)} all-to-all(f32[16,2,8,8,128]{4,3,2,1,0:T(8,128)S(1)} %bitcast.45), channel_id=1, replica_groups={{0,1,16,17,2,3,18,19,4,5,20,21,6,7,22,23},{8,9,24,25,10,11,26,27,12,13,..., dimensions={0} | all-to-all | bytes 2097152 | tf_op jit(solution)/shard_map/all_to_all | solution.py:910
  148.5 1.6 shard_map.157
  150.1 17.6 %all_to_all.104.refs_0_ = f32[16,2,8,8,128]{4,3,2,1,0:T(8,128)S(1)} all-to-all(f32[16,2,8,8,128]{4,3,2,1,0:T(8,128)S(1)} %bitcast.31), channel_id=1, replica_groups={{0,1,16,17,2,3,18,19,4,5,20,21,6,7,22,23},{8,9,24,25,10,11,26,27,12,13,..., dimensions={0} | all-to-all | bytes 2097152 | tf_op jit(solution)/shard_map/all_to_all | solution.py:910
  167.8 1.6 shard_map.158
  169.4 17.8 %all_to_all.105.refs_0_ = f32[16,2,8,8,128]{4,3,2,1,0:T(8,128)S(1)} all-to-all(f32[16,2,8,8,128]{4,3,2,1,0:T(8,128)S(1)} %bitcast.35), channel_id=1, replica_groups={{0,1,16,17,2,3,18,19,4,5,20,21,6,7,22,23},{8,9,24,25,10,11,26,27,12,13,..., dimensions={0} | all-to-all | bytes 2097152 | tf_op jit(solution)/shard_map/all_to_all | solution.py:910
  187.2 1.6 shard_map.159
  188.8 29.3 %all_to_all.106 = f32[32,2,32,128]{3,2,1,0:T(8,128)S(1)} all-to-all(f32[32,2,32,128]{3,2,1,0:T(8,128)S(1)} %shard_map.159), channel_id=1, replica_groups={{0,4,2,6,1,5,3,7,8,12,10,14,9,13,11,15,16,20,18,22,17,21,19,23,24,28,26..., dimensions={0} | all-to-all | bytes 2097152 | tf_op jit(solution)/shard_map/all_to_all | solution.py:916
  220.4 1.6 shard_map.160
  222.5 1.5 collective-permute-done.3.refs_1_
  224.8 11.5 %all_to_all.107.refs_0_ = f32[16,4,8,128]{3,2,1,0:T(8,128)S(1)} all-to-all(f32[16,4,8,128]{3,2,1,0:T(8,128)S(1)} %bitcast.47), channel_id=1, replica_groups=mesh['ka'=2,'fft'=16] {'fft'}, dimensions={0} | all-to-all | bytes 524288 | tf_op jit(solution)/shard_map/all_to_all | solution.py:913
  236.7 11.9 %all_to_all.108 = f32[16,4,8,128]{3,2,1,0:T(8,128)S(1)} all-to-all(f32[16,4,8,128]{3,2,1,0:T(8,128)S(1)} %shard_map.162), channel_id=1, replica_groups=mesh['ka'=2,'fft'=16] {'fft'}, dimensions={0} | all-to-all | bytes 524288 | tf_op jit(solution)/shard_map/all_to_all | solution.py:913
  248.6 3.3 collective-permute-start.4
  253.0 1.5 shard_map.164
  255.0 1.5 shard_map.163.refs_0_
  256.6 28.5 %all_to_all.109.refs_0_ = f32[32,2,32,128]{3,2,1,0:T(8,128)S(1)} all-to-all(f32[32,2,32,128]{3,2,1,0:T(8,128)S(1)} %bitcast.37), channel_id=1, replica_groups={{0,4,2,6,1,5,3,7,8,12,10,14,9,13,11,15,16,20,18,22,17,21,19,23,24,28,26..., dimensions={0} | all-to-all | bytes 2097152 | tf_op jit(solution)/shard_map/all_to_all | solution.py:916
  285.1 1.7 shard_map.166
  286.8 18.2 %all_to_all.110.refs_0_ = f32[16,2,8,8,128]{4,3,2,1,0:T(8,128)S(1)} all-to-all(f32[16,2,8,8,128]{4,3,2,1,0:T(8,128)S(1)} %bitcast.32), channel_id=1, replica_groups={{0,1,16,17,2,3,18,19,4,5,20,21,6,7,22,23},{8,9,24,25,10,11,26,27,12,13,..., dimensions={0} | all-to-all | bytes 2097152 | tf_op jit(solution)/shard_map/all_to_all | solution.py:910
  305.0 1.6 shard_map.167
  306.7 17.8 %all_to_all.111.refs_0_ = f32[16,2,8,8,128]{4,3,2,1,0:T(8,128)S(1)} all-to-all(f32[16,2,8,8,128]{4,3,2,1,0:T(8,128)S(1)} %bitcast.36), channel_id=1, replica_groups={{0,1,16,17,2,3,18,19,4,5,20,21,6,7,22,23},{8,9,24,25,10,11,26,27,12,13,..., dimensions={0} | all-to-all | bytes 2097152 | tf_op jit(solution)/shard_map/all_to_all | solution.py:910
  324.5 1.6 shard_map.168
  326.1 17.9 %all_to_all.112.refs_0_ = f32[16,2,8,8,128]{4,3,2,1,0:T(8,128)S(1)} all-to-all(f32[16,2,8,8,128]{4,3,2,1,0:T(8,128)S(1)} %bitcast.33), channel_id=1, replica_groups={{0,1,16,17,2,3,18,19,4,5,20,21,6,7,22,23},{8,9,24,25,10,11,26,27,12,13,..., dimensions={0} | all-to-all | bytes 2097152 | tf_op jit(solution)/shard_map/all_to_all | solution.py:910
  344.0 1.3 shard_map.169
  346.0 25.3 %collective-permute-done.6.refs_1_ = f32[8,128,128]{2,1,0:T(8,128)S(1)} collective-permute-done((f32[8,128,128]{2,1,0:T(8,128)S(1)}, f32[8,128,128]{2,1,0:T(8,128)S(1)}, u32[]{:S(2)}, u32[]{:S(2)}) %collective-permute-start.6) | collective-permute-done | bytes 524320 | tf_op jit(solution)/shard_map/ppermute | solution.py:938
  372.0 12.3 %all_to_all.113.refs_0_ = f32[16,8,8,128]{3,2,1,0:T(8,128)S(1)} all-to-all(f32[16,8,8,128]{3,2,1,0:T(8,128)S(1)} %bitcast.46), channel_id=1, replica_groups={{0,1,16,17,2,3,18,19,4,5,20,21,6,7,22,23},{8,9,24,25,10,11,26,27,12,13,..., dimensions={0} | all-to-all | bytes 1048576 | tf_op jit(solution)/shard_map/all_to_all | solution.py:910
  384.8 12.0 %all_to_all.114 = f32[16,8,8,128]{3,2,1,0:T(8,128)S(1)} all-to-all(f32[16,8,8,128]{3,2,1,0:T(8,128)S(1)} %shard_map.171), channel_id=1, replica_groups={{0,1,16,17,2,3,18,19,4,5,20,21,6,7,22,23},{8,9,24,25,10,11,26,27,12,13,..., dimensions={0} | all-to-all | bytes 1048576 | tf_op jit(solution)/shard_map/all_to_all | solution.py:910
  396.8 2.0 shard_map.172
  398.8 17.8 %all_to_all.115.refs_0_ = f32[16,2,8,8,128]{4,3,2,1,0:T(8,128)S(1)} all-to-all(f32[16,2,8,8,128]{4,3,2,1,0:T(8,128)S(1)} %bitcast.44), channel_id=1, replica_groups={{0,1,16,17,2,3,18,19,4,5,20,21,6,7,22,23},{8,9,24,25,10,11,26,27,12,13,..., dimensions={0} | all-to-all | bytes 2097152 | tf_op jit(solution)/shard_map/all_to_all | solution.py:910
  416.6 1.6 shard_map.173
  418.2 17.6 %all_to_all.116.refs_0_ = f32[16,2,8,8,128]{4,3,2,1,0:T(8,128)S(1)} all-to-all(f32[16,2,8,8,128]{4,3,2,1,0:T(8,128)S(1)} %bitcast.34), channel_id=1, replica_groups={{0,1,16,17,2,3,18,19,4,5,20,21,6,7,22,23},{8,9,24,25,10,11,26,27,12,13,..., dimensions={0} | all-to-all | bytes 2097152 | tf_op jit(solution)/shard_map/all_to_all | solution.py:910
  435.9 1.6 shard_map.174
  437.5 17.8 %all_to_all.117.refs_0_ = f32[16,2,8,8,128]{4,3,2,1,0:T(8,128)S(1)} all-to-all(f32[16,2,8,8,128]{4,3,2,1,0:T(8,128)S(1)} %bitcast.29), channel_id=1, replica_groups={{0,1,16,17,2,3,18,19,4,5,20,21,6,7,22,23},{8,9,24,25,10,11,26,27,12,13,..., dimensions={0} | all-to-all | bytes 2097152 | tf_op jit(solution)/shard_map/all_to_all | solution.py:910
  455.3 1.6 shard_map.175
  456.9 28.3 %all_to_all.118 = f32[32,2,32,128]{3,2,1,0:T(8,128)S(1)} all-to-all(f32[32,2,32,128]{3,2,1,0:T(8,128)S(1)} %shard_map.175), channel_id=1, replica_groups={{0,4,2,6,1,5,3,7,8,12,10,14,9,13,11,15,16,20,18,22,17,21,19,23,24,28,26..., dimensions={0} | all-to-all | bytes 2097152 | tf_op jit(solution)/shard_map/all_to_all | solution.py:916
  486.0 1.5 collective-permute-done.7.refs_1_
  488.2 2.2 shard_map.176
  (83 shorter events, 18.4 us)
Async XLA Ops:
  3.6 3.2 collective-permute-start
  6.8 1.1 copy-start.7
  8.1 44.3 %copy-start.1 = (bf16[512,256]{1,0:T(8,128)(2,1)S(1)}, bf16[512,256]{1,0:T(8,128)(2,1)}, u32[]{:S(2)}) copy-start(bf16[512,256]{1,0:T(8,128)(2,1)} %constant.29.clone.refs_3_.refs_2_.refs_4_) | copy-start | bytes 786436
  8.1 44.3 %copy-start.13 = (f32[128,256]{1,0:T(8,128)S(1)}, f32[128,256]{1,0:T(8,128)}, u32[]{:S(2)}) copy-start(f32[128,256]{1,0:T(8,128)} %constant.24.clone.refs_2_.refs_1_) | copy-start | bytes 393220
  8.1 44.3 %copy-start.29 = (f32[8]{0:T(128)S(1)}, f32[8]{0:T(128)}, u32[]{:S(2)}) copy-start(f32[8]{0:T(128)} %refs_0_.4) | copy-start | bytes 100
  56.1 24.7 %copy-start.5 = (bf16[128,512]{1,0:T(8,128)(2,1)S(1)}, bf16[128,512]{1,0:T(8,128)(2,1)}, u32[]{:S(2)}) copy-start(bf16[128,512]{1,0:T(8,128)(2,1)} %constant.27.clone.refs_2_.refs_1_.refs_3_) | copy-start | bytes 393220
  82.8 1.0 copy-start.10
  83.8 23.2 %all-to-all-start.2 = ((f32[16,2,8,8,128]{4,3,2,1,0:T(8,128)}), f32[16,2,8,8,128]{4,3,2,1,0:T(8,128)S(1)}, u32[]{:S(2)}, u32[]{:S(2)}) async-start(f32[16,2,8,8,128]{4,3,2,1,0:T(8,128)} %bitcast.43), calls=%async_computation.2 | async-start | bytes 2097152 | tf_op jit(solution)/shard_map/all_to_all | solution.py:910
  87.5 18.7 %collective-permute-start.1 = (f32[8,128,128]{2,1,0:T(8,128)}, f32[8,128,128]{2,1,0:T(8,128)S(1)}, u32[]{:S(2)}, u32[]{:S(2)}) collective-permute-start(f32[8,128,128]{2,1,0:T(8,128)} %refs_3_.15), channel_id=1, source_target_pairs={{0,0},{1,1},{2,2},{3,3},{4,4},{5,5},{6,6},{7,7},{8,16},{9,17},{10,... | collective-permute-start | bytes 1572872 | tf_op jit(solution)/shard_map/ppermute | solution.py:938
  90.2 0.9 copy-start.14
  94.8 0.7 copy-start.15
  95.5 0.7 copy-start.17
  96.2 0.7 copy-start.19
  96.9 0.7 copy-start.21
  97.6 0.7 copy-start.23
  98.3 0.7 copy-start.25
  99.0 0.7 copy-start.27
  106.2 0.8 copy-start.11
  107.0 1.0 copy-start.28
  130.7 17.8 %copy-start.26 = (bf16[2,128,512]{2,1,0:T(8,128)(2,1)S(1)}, bf16[2,128,512]{2,1,0:T(8,128)(2,1)}, u32[]{:S(2)}) copy-start(bf16[2,128,512]{2,1,0:T(8,128)(2,1)} %copy-done.25) | copy-start | bytes 786436
  169.4 17.8 %copy-start.24 = (bf16[2,128,512]{2,1,0:T(8,128)(2,1)S(1)}, bf16[2,128,512]{2,1,0:T(8,128)(2,1)}, u32[]{:S(2)}) copy-start(bf16[2,128,512]{2,1,0:T(8,128)(2,1)} %copy-done.23) | copy-start | bytes 786436
  188.8 31.6 %copy-start.2 = (f32[8,128,128]{2,1,0:T(8,128)S(1)}, f32[8,128,128]{2,1,0:T(8,128)}, u32[]{:S(2)}) copy-start(f32[8,128,128]{2,1,0:T(8,128)} %refs_2_.9) | copy-start | bytes 1572868
  188.8 31.6 %copy-start.3 = (f32[1,1,2,8,128,128]{5,4,3,2,1,0:T(8,128)S(1)}, f32[1,1,2,8,128,128]{5,4,3,2,1,0:T(8,128)}, u32[]{:S(2)}) copy-start(f32[1,1,2,8,128,128]{5,4,3,2,1,0:T(8,128)} %refs_6_.5) | copy-start | bytes 3145732
  188.8 31.5 %copy-start.30 = (s32[2]{0:T(128)S(1)}, s32[2]{0:T(128)}, u32[]{:S(2)}) copy-start(s32[2]{0:T(128)} %refs_6_.6) | copy-start | bytes 28
  218.2 2.2 collective-permute-start.2
  219.5 4.6 copy-start.6
  219.5 4.6 copy-start.9
  222.0 31.0 %copy-start = (bf16[512,256]{1,0:T(8,128)(2,1)S(1)}, bf16[512,256]{1,0:T(8,128)(2,1)}, u32[]{:S(2)}) copy-start(bf16[512,256]{1,0:T(8,128)(2,1)} %constant.30.clone.refs_11_.refs_4_.refs_12_) | copy-start | bytes 786436
  222.0 31.0 %copy-start.4 = (bf16[128,512]{1,0:T(8,128)(2,1)S(1)}, bf16[128,512]{1,0:T(8,128)(2,1)}, u32[]{:S(2)}) copy-start(bf16[128,512]{1,0:T(8,128)(2,1)} %constant.28.clone.refs_10_.refs_3_.refs_11_) | copy-start | bytes 393220
  222.1 31.0 %copy-start.8 = (f32[8,128,128]{2,1,0:T(8,128)S(1)}, f32[8,128,128]{2,1,0:T(8,128)}, u32[]{:S(2)}) copy-start(f32[8,128,128]{2,1,0:T(8,128)} %refs_3_.15) | copy-start | bytes 1572868
  222.1 2.0 collective-permute-start.3
  248.6 4.5 collective-permute-start.4
  254.5 2.0 collective-permute-start.5
  256.6 28.6 %copy-start.22 = (bf16[2,128,512]{2,1,0:T(8,128)(2,1)S(1)}, bf16[2,128,512]{2,1,0:T(8,128)(2,1)}, u32[]{:S(2)}) copy-start(bf16[2,128,512]{2,1,0:T(8,128)(2,1)} %copy-done.21) | copy-start | bytes 786436
  306.7 17.8 %copy-start.20 = (bf16[2,128,512]{2,1,0:T(8,128)(2,1)S(1)}, bf16[2,128,512]{2,1,0:T(8,128)(2,1)}, u32[]{:S(2)}) copy-start(bf16[2,128,512]{2,1,0:T(8,128)(2,1)} %copy-done.19) | copy-start | bytes 786436
  345.3 26.0 %collective-permute-start.6 = (f32[8,128,128]{2,1,0:T(8,128)S(1)}, f32[8,128,128]{2,1,0:T(8,128)S(1)}, u32[]{:S(2)}, u32[]{:S(2)}) collective-permute-start(f32[8,128,128]{2,1,0:T(8,128)S(1)} %get-tuple-element.78.refs_0_), channel_id=1, source_target_pairs={{0,8},{1,9},{2,10},{3,11},{4,12},{5,13},{6,14},{7,15},{8,0},{9,1},... | collective-permute-start | bytes 1572872 | tf_op jit(solution)/shard_map/ppermute | solution.py:938
  372.0 24.8 %copy-start.12 = (f32[8,128,128]{2,1,0:T(8,128)S(1)}, f32[8,128,128]{2,1,0:T(8,128)}, u32[]{:S(2)}) copy-start(f32[8,128,128]{2,1,0:T(8,128)} %copy-done.11) | copy-start | bytes 1572868
  398.8 17.8 %copy-start.18 = (bf16[2,128,512]{2,1,0:T(8,128)(2,1)S(1)}, bf16[2,128,512]{2,1,0:T(8,128)(2,1)}, u32[]{:S(2)}) copy-start(bf16[2,128,512]{2,1,0:T(8,128)(2,1)} %copy-done.17) | copy-start | bytes 786436
  437.5 17.8 %copy-start.16 = (bf16[2,128,512]{2,1,0:T(8,128)(2,1)S(1)}, bf16[2,128,512]{2,1,0:T(8,128)(2,1)}, u32[]{:S(2)}) copy-start(bf16[2,128,512]{2,1,0:T(8,128)(2,1)} %copy-done.15) | copy-start | bytes 786436
  485.3 2.2 collective-permute-start.7
  486.0 2.3 collective-permute-start.8
